TPU v7x, 32 devices: a whole 2x2x4 slice. The times are simulated.
32 devices in a mesh: batch: 4 (over x, core), seq: 8 (over z, y).
Axes of the slice: x: 2, y: 2, z: 4, core: 2. Of those that a mesh axis runs over, the one named last changes fastest.
Arguments:
- token_ids: int32 [4, 2048], P('batch', 'seq'), may hold values from 0 to 151935, as said below
- row_lengths: int32 [4], replicated, may hold values from 1280 to 2048, as said below
- prompt_lengths: int32 [4], replicated, may hold values from 128 to 511
- picks: int32 [4, 256], P('batch', 'seq'), may hold values from 0 to 254, as said below
- old_logp: float32 [4, 256], P('batch', 'seq'), may hold values from -18 to -10
- ref_logp: float32 [4, 256], P('batch', 'seq'), may hold values from -18 to -10
- rewards: float32 [4], replicated, may hold values from -4 to 4
- embed: float32 [151936, 896], P(('batch', 'seq'))
- embed_m: float32 [151936, 896], P(('batch', 'seq')), may hold values from -3.33786e-06 to 3.33786e-06
- embed_v: float32 [151936, 896], P(('batch', 'seq')), may hold values from 1.09236845e-13 to 1.7213079e-12
- w_qkv: float32 [896, 1152], P('seq'), may hold values from -0.1875 to 0.1875
- w_qkv_m: float32 [896, 1152], P('seq'), may hold values from -6.67572e-06 to 6.67572e-06
- w_qkv_v: float32 [896, 1152], P('seq'), may hold values from 4.3694738e-13 to 6.9514355e-12
- w_out: float32 [896, 896], P('seq'), may hold values from -0.75 to 0.75
- w_out_m: float32 [896, 896], P('seq'), may hold values from -6.67572e-06 to 6.67572e-06
- w_out_v: float32 [896, 896], P('seq'), may hold values from 4.3694738e-13 to 6.9514355e-12
- w_gateup: float32 [896, 9728], P('seq'), may hold values from -0.1875 to 0.1875
- w_gateup_m: float32 [896, 9728], P('seq'), may hold values from -6.67572e-06 to 6.67572e-06
- w_gateup_v: float32 [896, 9728], P('seq'), may hold values from 4.3694738e-13 to 6.9514355e-12
- w_down: float32 [4864, 896], P('seq'), may hold values from -0.078125 to 0.078125
- w_down_m: float32 [4864, 896], P('seq'), may hold values from -6.67572e-06 to 6.67572e-06
- w_down_v: float32 [4864, 896], P('seq'), may hold values from 4.3694738e-13 to 6.9514355e-12
- gains: float32 [3, 896], replicated, may hold values from 0.48 to 2.25
- gains_m: float32 [3, 896], replicated, may hold values from -6.1035156e-05 to 6.1035156e-05
- gains_v: float32 [3, 896], replicated, may hold values from 4.369474e-11 to 6.9514355e-10
- bias: float32 [1152], replicated, may hold values from -3 to 3
- bias_m: float32 [1152], replicated, may hold values from -3.0517578e-05 to 3.0517578e-05
- bias_v: float32 [1152], replicated, may hold values from 1.0923685e-11 to 1.7213078e-10
Outputs:
- loss_sum: float32 [], replicated
- token_count: float32 [], replicated
- grad_norm: float32 [], replicated
- embed_new: float32 [151936, 896], P(('batch', 'seq'))
- embed_m_new: float32 [151936, 896], P(('batch', 'seq'))
- embed_v_new: float32 [151936, 896], P(('batch', 'seq'))
- w_qkv_new: float32 [896, 1152], P('seq')
- w_qkv_m_new: float32 [896, 1152], P('seq')
- w_qkv_v_new: float32 [896, 1152], P('seq')
- w_out_new: float32 [896, 896], P('seq')
- w_out_m_new: float32 [896, 896], P('seq')
- w_out_v_new: float32 [896, 896], P('seq')
- w_gateup_new: float32 [896, 9728], P('seq')
- w_gateup_m_new: float32 [896, 9728], P('seq')
- w_gateup_v_new: float32 [896, 9728], P('seq')
- w_down_new: float32 [4864, 896], P('seq')
- w_down_m_new: float32 [4864, 896], P('seq')
- w_down_v_new: float32 [4864, 896], P('seq')
- gains_new: float32 [3, 896], replicated
- gains_m_new: float32 [3, 896], replicated
- gains_v_new: float32 [3, 896], replicated
- bias_new: float32 [1152], replicated
- bias_m_new: float32 [1152], replicated
- bias_v_new: float32 [1152], replicated
Inputs may be any that keep to these rules, and one draw needn't show every extreme that they name: `token_ids`: among the 256 tokens of one device, at most 16 have ids in any one owner's table rows (aligned ranges of 4748 ids), for every owner; on every device some owner receives exactly 16. `row_lengths`: one row has length 2048 in every draw. `picks`: the 32 offsets of one device are distinct.
All inputs are finite; a program needn't handle non-finite values.
Results may differ from a plain program's by a relative error of at most 0.03.
Values may be sent and summed in bfloat16 or wider, within the bound.
No kernel may reach another device: no remote copies, remote signals or barrier semaphores. Data moves between devices by JAX's collectives and lax.ppermute only.
A program may use at most 224 MiB of HBM per device.

v0:
```python
import jax
import jax.numpy as jnp
from jax import lax
from jax.sharding import PartitionSpec as P

H = 14
KV = 2
HD = 64
FF = 4864
STEP = 5


NORM_EPS = 1e-06
ROPE_BASE = 1000000.0
NEG_BIG = -1e30
EPS_LOW = 0.8
EPS_HIGH = 0.28
BETA_KL = 0.1
CLIP_NORM = 0.05
BETA_ONE = 0.9
BETA_TWO = 0.95
ADAM_EPS = 1e-08
DECAY = 0.1
LR_MATRIX = 0.02
LR_OUT = 0.12
LR_GAIN = 1.0
LR_BIAS = 0.5


def merged(value, axis, join):
    pieces = jax.tree.map(lambda part: lax.all_gather(part, axis), value)
    head = jax.tree.map(lambda part: part[0], pieces)
    tail = jax.tree.map(lambda part: part[1:], pieces)
    running, _ = lax.scan(lambda running, share: (join(running, share), None), head, tail)
    return running


def norm_rows(values, gain):
    return values * lax.rsqrt(jnp.mean(values * values, axis=-1, keepdims=True) + NORM_EPS) * gain


def rotate(values, places, sign):
    half_width = values.shape[-1] // 2
    frequency = ROPE_BASE ** (-2.0 * jnp.arange(half_width, dtype=jnp.float32) / values.shape[-1])
    angles = places.astype(jnp.float32)[:, None] * frequency[None, :]
    cosine = jnp.cos(angles)[:, None, :]
    sine_part = sign * jnp.sin(angles)[:, None, :]
    front = values[..., :half_width]
    back_half = values[..., half_width:]
    return jnp.concatenate(
        [front * cosine - back_half * sine_part, back_half * cosine + front * sine_part], axis=-1
    )


def block_scores(grouped, keys3, offset, span, places):
    key_piece = lax.dynamic_slice_in_dim(keys3, offset, span, 0)
    raw = jnp.einsum(
        "cgrd,kgd->cgrk", grouped, key_piece, preferred_element_type=jnp.float32
    ) * HD ** (-0.5)
    allowed = (offset + jnp.arange(span, dtype=jnp.int32))[None, :] <= places[:, None]
    return (jnp.where(allowed[:, None, None, :], raw, NEG_BIG), key_piece)


def attend(grouped, keys3, values3, places):
    span = min(1024, keys3.shape[0])
    reach = places[-1] // span + 1
    stat_shape = grouped.shape[:3]

    def statistics(block_index, carry):
        highest, summed = carry
        scores, key_piece = block_scores(grouped, keys3, block_index * span, span, places)
        new_high = jnp.maximum(highest, jnp.max(scores, axis=-1))
        summed = summed * jnp.exp(highest - new_high) + jnp.sum(
            jnp.exp(scores - new_high[..., None]), axis=-1
        )
        return (new_high, summed)

    highest, summed = lax.fori_loop(
        0,
        reach,
        statistics,
        (jnp.full(stat_shape, NEG_BIG, jnp.float32), jnp.zeros(stat_shape, jnp.float32)),
    )
    log_total = highest + jnp.log(summed)

    def outputs(block_index, carry):
        scores, key_piece = block_scores(grouped, keys3, block_index * span, span, places)
        chance = jnp.exp(scores - log_total[..., None]).astype(jnp.bfloat16)
        value_piece = lax.dynamic_slice_in_dim(values3, block_index * span, span, 0)
        return carry + jnp.einsum(
            "cgrk,kgd->cgrd", chance, value_piece, preferred_element_type=jnp.float32
        )

    attended = lax.fori_loop(0, reach, outputs, jnp.zeros(grouped.shape, jnp.float32))
    return (attended, log_total)


def attend_back(grouped, keys3, values3, places, log_total, attended, grad_attended):
    span = min(1024, keys3.shape[0])
    reach = places[-1] // span + 1
    inner = jnp.sum(grad_attended.astype(jnp.float32) * attended, axis=-1)

    def accumulate(block_index, carry):
        grad_query, grad_keys, grad_values = carry
        offset = block_index * span
        scores, key_piece = block_scores(grouped, keys3, offset, span, places)
        chance = jnp.exp(scores - log_total[..., None])
        value_piece = lax.dynamic_slice_in_dim(values3, offset, span, 0)
        grad_chance = jnp.einsum(
            "cgrd,kgd->cgrk", grad_attended, value_piece, preferred_element_type=jnp.float32
        )
        grad_scores = (chance * (grad_chance - inner[..., None])).astype(jnp.bfloat16)
        grad_query = grad_query + jnp.einsum(
            "cgrk,kgd->cgrd", grad_scores, key_piece, preferred_element_type=jnp.float32
        ) * HD ** (-0.5)
        key_part = jnp.einsum(
            "cgrk,cgrd->kgd", grad_scores, grouped, preferred_element_type=jnp.float32
        ) * HD ** (-0.5)
        value_part = jnp.einsum(
            "cgrk,cgrd->kgd",
            chance.astype(jnp.bfloat16),
            grad_attended,
            preferred_element_type=jnp.float32,
        )
        grad_keys = lax.dynamic_update_slice_in_dim(
            grad_keys, lax.dynamic_slice_in_dim(grad_keys, offset, span, 0) + key_part, offset, 0
        )
        grad_values = lax.dynamic_update_slice_in_dim(
            grad_values,
            lax.dynamic_slice_in_dim(grad_values, offset, span, 0) + value_part,
            offset,
            0,
        )
        return (grad_query, grad_keys, grad_values)

    zeros_start = (
        jnp.zeros(grouped.shape, jnp.float32),
        jnp.zeros(keys3.shape, jnp.float32),
        jnp.zeros(values3.shape, jnp.float32),
    )
    return lax.fori_loop(0, reach, accumulate, zeros_start)


def layer_forward(stream_zero, gathered, gains, bias, places):
    w_qkv_full, w_out_full, w_gateup_full, w_down_full = gathered
    local_len = stream_zero.shape[0]
    normed_one = norm_rows(stream_zero, gains[0]).astype(jnp.bfloat16)
    mixed_qkv = jnp.dot(normed_one, w_qkv_full, preferred_element_type=jnp.float32) + bias
    queries = rotate(mixed_qkv[:, : H * HD].reshape(local_len, H, HD), places, 1.0).astype(
        jnp.bfloat16
    )
    keys = rotate(
        mixed_qkv[:, H * HD : (H + KV) * HD].reshape(local_len, KV, HD), places, 1.0
    ).astype(jnp.bfloat16)
    values = mixed_qkv[:, (H + KV) * HD :].astype(jnp.bfloat16)
    keys_all, values_all = (
        lax.all_gather(keys.reshape(local_len, KV * HD), "seq", axis=0, tiled=True),
        lax.all_gather(values, "seq", axis=0, tiled=True),
    )
    length = keys_all.shape[0]
    grouped = queries.reshape(local_len, KV, H // KV, HD)
    keys3 = keys_all.reshape(length, KV, HD)
    values3 = values_all.reshape(length, KV, HD)
    attended, log_total = attend(grouped, keys3, values3, places)
    mixed = attended.reshape(local_len, H * HD).astype(jnp.bfloat16)
    stream_one = stream_zero + jnp.dot(mixed, w_out_full, preferred_element_type=jnp.float32)
    normed_two = norm_rows(stream_one, gains[1]).astype(jnp.bfloat16)
    gate_up = jnp.dot(normed_two, w_gateup_full, preferred_element_type=jnp.float32)
    hidden = (jax.nn.silu(gate_up[:, :FF]) * gate_up[:, FF:]).astype(jnp.bfloat16)
    stream_two = stream_one + jnp.dot(hidden, w_down_full, preferred_element_type=jnp.float32)
    saved = (
        stream_zero,
        normed_one,
        grouped,
        keys3,
        values3,
        attended,
        log_total,
        mixed,
        stream_one,
        normed_two,
        gate_up,
        hidden,
    )
    return (stream_two, saved)


def layer_backward(grad_two, saved, gathered, gains, places):
    (
        stream_zero,
        normed_one,
        grouped,
        keys3,
        values3,
        attended,
        log_total,
        mixed,
        stream_one,
        normed_two,
        gate_up,
        hidden,
    ) = saved
    w_qkv_full, w_out_full, w_gateup_full, w_down_full = gathered
    local_len = stream_zero.shape[0]
    length = keys3.shape[0]
    branch_grad = grad_two.astype(jnp.bfloat16)
    grad_hidden = jnp.einsum(
        "cd,fd->cf", branch_grad, w_down_full, preferred_element_type=jnp.float32
    )
    grad_down = jnp.einsum("cf,cd->fd", hidden, branch_grad, preferred_element_type=jnp.float32)
    gate_part = gate_up[:, :FF]
    up_part = gate_up[:, FF:]
    sigmoid_gate = jax.nn.sigmoid(gate_part)
    grad_gate = grad_hidden * up_part * sigmoid_gate * (1.0 + gate_part * (1.0 - sigmoid_gate))
    grad_up = grad_hidden * gate_part * sigmoid_gate
    grad_gateup = jnp.concatenate([grad_gate, grad_up], axis=1).astype(jnp.bfloat16)
    grad_normed_two = jnp.einsum(
        "cf,df->cd", grad_gateup, w_gateup_full, preferred_element_type=jnp.float32
    )
    grad_gateup_w = jnp.einsum(
        "cd,cf->df", normed_two, grad_gateup, preferred_element_type=jnp.float32
    )
    unused, pull_two = jax.vjp(norm_rows, stream_one, gains[1])
    part_one, grad_gain_one = pull_two(grad_normed_two)
    grad_one = grad_two + part_one
    mixed_grad = grad_one.astype(jnp.bfloat16)
    grad_attended = jnp.einsum(
        "cd,ed->ce", mixed_grad, w_out_full, preferred_element_type=jnp.float32
    ).astype(jnp.bfloat16)
    grad_out_w = jnp.einsum("ce,cd->ed", mixed, mixed_grad, preferred_element_type=jnp.float32)
    grad_query, grad_keys, grad_values = attend_back(
        grouped, keys3, values3, places, log_total, attended, grad_attended.reshape(grouped.shape)
    )
    own_keys, own_values = (
        lax.psum_scatter(
            grad_keys.reshape(length, KV * HD).astype(jnp.bfloat16),
            "seq",
            scatter_dimension=0,
            tiled=True,
        ).astype(jnp.float32),
        lax.psum_scatter(
            grad_values.reshape(length, KV * HD).astype(jnp.bfloat16),
            "seq",
            scatter_dimension=0,
            tiled=True,
        ).astype(jnp.float32),
    )
    query_pre = rotate(grad_query.reshape(local_len, H, HD), places, -1.0).reshape(
        local_len, H * HD
    )
    key_pre = rotate(own_keys.reshape(local_len, KV, HD), places, -1.0).reshape(local_len, KV * HD)
    grad_qkv = jnp.concatenate([query_pre, key_pre, own_values], axis=1).astype(jnp.bfloat16)
    grad_normed_one = jnp.einsum(
        "cq,dq->cd", grad_qkv, w_qkv_full, preferred_element_type=jnp.float32
    )
    grad_qkv_w = jnp.einsum("cd,cq->dq", normed_one, grad_qkv, preferred_element_type=jnp.float32)
    grad_bias = jnp.sum(grad_qkv.astype(jnp.float32), axis=0)
    unused_zero, pull_one = jax.vjp(norm_rows, stream_zero, gains[0])
    part_zero, grad_gain_zero = pull_one(grad_normed_one)
    return (
        grad_one + part_zero,
        (grad_qkv_w, grad_out_w, grad_gateup_w, grad_down),
        grad_gain_zero,
        grad_gain_one,
        grad_bias,
    )


def combine(earlier, later):
    highest = jnp.maximum(earlier[0], later[0])
    summed = earlier[1] * jnp.exp(earlier[0] - highest) + later[1] * jnp.exp(later[0] - highest)
    return (highest, summed, earlier[2] + later[2])


def adam(weight, moment, second, gradient, learn_rate, decay_rate):
    moment = BETA_ONE * moment + (1.0 - BETA_ONE) * gradient
    second = BETA_TWO * second + (1.0 - BETA_TWO) * gradient * gradient
    corrected = moment / (1.0 - BETA_ONE**STEP)
    scaled = second / (1.0 - BETA_TWO**STEP)
    return (
        weight - learn_rate * (corrected / (jnp.sqrt(scaled) + ADAM_EPS) + decay_rate * weight),
        moment,
        second,
    )


def per_device(
    token_ids,
    row_lengths,
    prompt_lengths,
    picks,
    old_logp,
    ref_logp,
    rewards,
    embed,
    embed_m,
    embed_v,
    w_qkv,
    w_qkv_m,
    w_qkv_v,
    w_out,
    w_out_m,
    w_out_v,
    w_gateup,
    w_gateup_m,
    w_gateup_v,
    w_down,
    w_down_m,
    w_down_v,
    gains,
    gains_m,
    gains_v,
    bias,
    bias_m,
    bias_v,
):
    owners = lax.axis_size(("batch", "seq"))
    owner_index = lax.axis_index(("batch", "seq"))
    seq_index = lax.axis_index("seq")
    row_index = lax.axis_index("batch")
    batch_count = lax.axis_size("batch")
    token_list = token_ids[0]
    local_len = token_list.shape[0]
    vrows, width = embed.shape
    capacity = max(2, 2 * local_len // owners)
    table = embed.astype(jnp.bfloat16)
    places = seq_index * local_len + jnp.arange(local_len, dtype=jnp.int32)
    owner_of = token_list // vrows
    matches = (owner_of[:, None] == jnp.arange(owners, dtype=jnp.int32)[None, :]).astype(jnp.int32)
    slot_of = jnp.sum(matches * (jnp.cumsum(matches, axis=0) - 1), axis=1)
    place_of = owner_of * capacity + slot_of
    requests = (
        jnp.zeros((owners * capacity,), jnp.int32).at[place_of].set(token_list - owner_of * vrows)
    )
    wanted = lax.all_to_all(
        requests.reshape(owners, capacity),
        ("batch", "seq"),
        split_axis=0,
        concat_axis=0,
        tiled=True,
    )
    found = jnp.take(table, wanted.reshape(-1), axis=0).reshape(owners, capacity, width)
    returned = lax.all_to_all(found, ("batch", "seq"), split_axis=0, concat_axis=0, tiled=True)
    stream_zero = jnp.take(returned.reshape(owners * capacity, width), place_of, axis=0).astype(
        jnp.float32
    )
    matrices = (
        w_qkv.astype(jnp.bfloat16),
        w_out.astype(jnp.bfloat16),
        w_gateup.astype(jnp.bfloat16),
        w_down.astype(jnp.bfloat16),
    )
    gathered = (
        lax.all_gather(matrices[0], "seq", axis=0, tiled=True),
        lax.all_gather(matrices[1], "seq", axis=0, tiled=True),
        lax.all_gather(matrices[2], "seq", axis=0, tiled=True),
        lax.all_gather(matrices[3], "seq", axis=0, tiled=True),
    )
    stream_two, saved = layer_forward(stream_zero, gathered, gains, bias, places)
    local_picks = picks[0]
    picked = jnp.take(stream_two, local_picks, axis=0)
    targets = jnp.take(token_list, local_picks + 1)
    pick_places = seq_index * local_len + local_picks
    live_mask = (
        (pick_places >= prompt_lengths[row_index]) & (pick_places + 1 < row_lengths[row_index])
    ).astype(jnp.float32)
    final = norm_rows(picked, gains[2]).astype(jnp.bfloat16)
    all_final = lax.all_gather(final, ("batch", "seq"), axis=0, tiled=True)
    all_targets, all_live, all_old, all_ref = (
        lax.all_gather(targets.astype(jnp.float32), ("batch", "seq"), axis=0, tiled=True),
        lax.all_gather(live_mask, ("batch", "seq"), axis=0, tiled=True),
        lax.all_gather(old_logp[0], ("batch", "seq"), axis=0, tiled=True),
        lax.all_gather(ref_logp[0], ("batch", "seq"), axis=0, tiled=True),
    )
    all_targets = all_targets.astype(jnp.int32)
    logits = jnp.einsum("pd,vd->pv", all_final, table, preferred_element_type=jnp.float32)
    local_target = all_targets - owner_index * vrows
    inside = (local_target >= 0) & (local_target < vrows)
    target_logit = jnp.take_along_axis(
        logits, jnp.clip(local_target, 0, vrows - 1)[:, None], axis=1
    )[:, 0]
    local_high = jnp.max(logits, axis=1)
    local_sum = jnp.sum(jnp.exp(logits - local_high[:, None]), axis=1)
    highest, summed, target_total = merged(
        (local_high, local_sum, jnp.where(inside, target_logit, 0.0)), ("batch", "seq"), combine
    )
    log_total = highest + jnp.log(summed)
    logp = target_total - log_total
    advantage = jnp.repeat(rewards - jnp.mean(rewards), all_live.shape[0] // batch_count)
    clip_weight = jnp.clip(jnp.exp(logp - all_old), 1.0 - EPS_LOW, 1.0 + EPS_HIGH)
    token_count = jnp.maximum(jnp.sum(all_live), 1.0)
    loss_sum = jnp.sum(
        all_live * (-clip_weight * advantage * logp + 0.5 * BETA_KL * (logp - all_ref) ** 2)
    )
    coefficient = all_live * (-clip_weight * advantage + BETA_KL * (logp - all_ref)) / token_count
    is_target = jnp.arange(vrows, dtype=jnp.int32)[None, :] == local_target[:, None]
    softened = jnp.exp(logits - log_total[:, None])
    grad_logits = (coefficient[:, None] * (jnp.where(is_target, 1.0, 0.0) - softened)).astype(
        jnp.bfloat16
    )
    grad_head = jnp.einsum("pv,pd->vd", grad_logits, all_final, preferred_element_type=jnp.float32)
    grad_final = lax.psum_scatter(
        jnp.dot(grad_logits, table, preferred_element_type=jnp.float32),
        ("batch", "seq"),
        scatter_dimension=0,
        tiled=True,
    )
    unused, pull_final = jax.vjp(norm_rows, picked, gains[2])
    grad_picked, grad_gain_two = pull_final(grad_final)
    grad_two = jnp.zeros(stream_two.shape, jnp.float32).at[local_picks].add(grad_picked)
    gathered_back = (
        lax.all_gather(matrices[0], "seq", axis=0, tiled=True),
        lax.all_gather(matrices[1], "seq", axis=0, tiled=True),
        lax.all_gather(matrices[2], "seq", axis=0, tiled=True),
        lax.all_gather(matrices[3], "seq", axis=0, tiled=True),
    )
    grad_zero, layer_grads, grad_gain_zero, grad_gain_one, grad_bias = layer_backward(
        grad_two, saved, gathered_back, gains, places
    )
    sendback = jnp.zeros((owners * capacity, width), jnp.float32).at[place_of].set(grad_zero)
    arrived = lax.all_to_all(
        sendback.reshape(owners, capacity, width).astype(jnp.bfloat16),
        ("batch", "seq"),
        split_axis=0,
        concat_axis=0,
        tiled=True,
    ).astype(jnp.float32)
    grad_embed = grad_head + jax.ops.segment_sum(
        arrived.reshape(owners * capacity, width), wanted.reshape(-1), num_segments=vrows
    )
    shards = (
        lax.psum_scatter(
            layer_grads[0].astype(jnp.bfloat16), "seq", scatter_dimension=0, tiled=True
        ).astype(jnp.float32),
        lax.psum_scatter(
            layer_grads[1].astype(jnp.bfloat16), "seq", scatter_dimension=0, tiled=True
        ).astype(jnp.float32),
        lax.psum_scatter(
            layer_grads[2].astype(jnp.bfloat16), "seq", scatter_dimension=0, tiled=True
        ).astype(jnp.float32),
        lax.psum_scatter(
            layer_grads[3].astype(jnp.bfloat16), "seq", scatter_dimension=0, tiled=True
        ).astype(jnp.float32),
    )
    shards = (
        lax.psum(shards[0].astype(jnp.bfloat16), "batch").astype(jnp.float32),
        lax.psum(shards[1].astype(jnp.bfloat16), "batch").astype(jnp.float32),
        lax.psum(shards[2].astype(jnp.bfloat16), "batch").astype(jnp.float32),
        lax.psum(shards[3].astype(jnp.bfloat16), "batch").astype(jnp.float32),
    )
    shard_squares = (
        jnp.sum(shards[0] * shards[0])
        + jnp.sum(shards[1] * shards[1])
        + jnp.sum(shards[2] * shards[2])
        + jnp.sum(shards[3] * shards[3])
    )
    local_squares = jnp.sum(grad_embed * grad_embed) + shard_squares / batch_count
    squares, grad_gains, grad_bias_all = lax.psum(
        (local_squares, jnp.stack([grad_gain_zero, grad_gain_one, grad_gain_two]), grad_bias),
        ("batch", "seq"),
    )
    grad_norm = jnp.sqrt(
        squares + jnp.sum(grad_gains * grad_gains) + jnp.sum(grad_bias_all * grad_bias_all)
    )
    factor = jnp.minimum(1.0, CLIP_NORM / (grad_norm + 1e-06))
    embed_new = adam(embed, embed_m, embed_v, grad_embed * factor, LR_MATRIX, DECAY)
    qkv_new = adam(w_qkv, w_qkv_m, w_qkv_v, shards[0] * factor, LR_MATRIX, DECAY)
    out_new = adam(w_out, w_out_m, w_out_v, shards[1] * factor, LR_OUT, DECAY)
    gateup_new = adam(w_gateup, w_gateup_m, w_gateup_v, shards[2] * factor, LR_MATRIX, DECAY)
    down_new = adam(w_down, w_down_m, w_down_v, shards[3] * factor, LR_MATRIX, DECAY)
    gains_new = adam(gains, gains_m, gains_v, grad_gains * factor, LR_GAIN, 0.0)
    bias_new = adam(bias, bias_m, bias_v, grad_bias_all * factor, LR_BIAS, 0.0)
    return (
        loss_sum,
        token_count,
        grad_norm,
        embed_new[0],
        embed_new[1],
        embed_new[2],
        qkv_new[0],
        qkv_new[1],
        qkv_new[2],
        out_new[0],
        out_new[1],
        out_new[2],
        gateup_new[0],
        gateup_new[1],
        gateup_new[2],
        down_new[0],
        down_new[1],
        down_new[2],
        gains_new[0],
        gains_new[1],
        gains_new[2],
        bias_new[0],
        bias_new[1],
        bias_new[2],
    )


def solution(mesh):
    in_specs = (
        P("batch", "seq"),
        P(),
        P(),
        P("batch", "seq"),
        P("batch", "seq"),
        P("batch", "seq"),
        P(),
        P(("batch", "seq"), None),
        P(("batch", "seq"), None),
        P(("batch", "seq"), None),
        P("seq", None),
        P("seq", None),
        P("seq", None),
        P("seq", None),
        P("seq", None),
        P("seq", None),
        P("seq", None),
        P("seq", None),
        P("seq", None),
        P("seq", None),
        P("seq", None),
        P("seq", None),
        P(),
        P(),
        P(),
        P(),
        P(),
        P(),
    )
    out_specs = (
        P(),
        P(),
        P(),
        P(("batch", "seq"), None),
        P(("batch", "seq"), None),
        P(("batch", "seq"), None),
        P("seq", None),
        P("seq", None),
        P("seq", None),
        P("seq", None),
        P("seq", None),
        P("seq", None),
        P("seq", None),
        P("seq", None),
        P("seq", None),
        P("seq", None),
        P("seq", None),
        P("seq", None),
        P(),
        P(),
        P(),
        P(),
        P(),
        P(),
    )
    return jax.shard_map(
        per_device, mesh=mesh, in_specs=in_specs, out_specs=out_specs, check_vma=False
    )
```

profile of v0, /device:TPU:0, one launch (start us, length us, event | category | flops | bytes accessed | tf_op | source)
XLA Modules:
  0.0 2097.2 jit_solution(13303589064550006124)
XLA Ops:
  10.9 3.8 convert_element_type.162
  17.8 7.3 all-to-all-start
  25.1 9.1 convert_element_type.152
  35.5 7.1 gather_fusion
  43.7 5.8 all-to-all-start.1
  49.6 2.7 convert_element_type.164
  56.6 25.1 %all-to-all-done.1 = bf16[32,16,896]{2,1,0:T(8,128)(2,1)S(1)} async-done(((bf16[32,16,896]{2,1,0:T(8,128)(2,1)}), bf16[32,16,896]{2,1,0:T(8,128)(2,1)S(1)}, u32[]{:S(2)}, u32[]{:S(2)}) %all-to-all-start.1) | async-done | bytes 917536 | tf_op jit(solution)/shard_map/all_to_all | solution.py:343
  83.3 2.5 convolution_add_fusion
  86.6 32.2 %all_gather.58 = bf16[2048,128]{0,1:T(8,128)(2,1)S(1)} all-gather(bf16[256,128]{0,1:T(8,128)(2,1)S(1)} %bitcast.317), channel_id=1, replica_groups=mesh['batch'=4,'seq'=8] {'seq'}, dimensions={0}, use_global_device_ids=true | all-gather | bytes 589824 | tf_op jit(solution)/shard_map/all_gather | solution.py:157
  118.8 53.5 %all_gather.57 = bf16[2048,128]{1,0:T(8,128)(2,1)S(1)} all-gather(bf16[256,128]{1,0:T(8,128)(2,1)S(1)} %slice.181), channel_id=1, replica_groups=mesh['batch'=4,'seq'=8] {'seq'}, dimensions={0}, use_global_device_ids=true | all-gather | bytes 589824 | tf_op jit(solution)/shard_map/all_gather | solution.py:158
  173.4 16.4 while.54
  173.9 7.7 fusion.210
  181.5 8.3 exponential_reduce_fusion.3
  190.0 5.1 while.55
  190.2 4.6 fusion.215
  196.0 2.2 multiply_reduce_fusion.4
  198.3 268.6 %all-gather.15.cloned.1.call-done = bf16[896,9728]{1,0:T(8,128)(2,1)} async-done(((bf16[112,9728]{1,0:T(8,128)(2,1)}), bf16[896,9728]{1,0:T(8,128)(2,1)}) %all-gather.15.cloned.1.call-update) | async-done | bytes 17432592 | tf_op jit(solution)/shard_map/all_gather | solution.py:356
  466.9 9.1 fusion.146
  476.0 4.2 copy-done.2
  480.2 2.5 multiply_convert_fusion.3
  482.7 115.8 %all-gather.17.cloned.1.call-done = bf16[4864,896]{1,0:T(8,128)(2,1)} async-done(((bf16[608,896]{1,0:T(8,128)(2,1)}), bf16[4864,896]{1,0:T(8,128)(2,1)}) %all-gather.17.cloned.1.call-update) | async-done | bytes 8716304 | tf_op jit(solution)/shard_map/all_gather | solution.py:357
  598.5 7.9 convolution_add_fusion.1
  614.2 39.2 %all-reduce.5 = (f32[1024]{0:T(1024)S(1)}, f32[1024]{0:T(1024)S(1)}, f32[1024]{0:T(1024)S(1)}, f32[1024]{0:T(1024)S(1)}) all-reduce(f32[1024]{0:T(1024)S(1)} %fusion.138, f32[1024]{0:T(1024)S(1)} %bitcast_dynamic-update-slice_fusion, f32[1024]{0:T(1024)S(1)} %bitcast_dynamic-update-slice_fusion.1, ...), channel_id=1, replica_groups=mesh['batch'=4,'seq'=8] {'batch','seq'}, use_global_device_ids=true, to_apply=%add | all-reduce | flops 4096 | bytes 32768
  653.4 10.0 all-gather.19.cloned.1.call-done
  663.5 17.1 fusion.162
  680.5 66.9 %all-gather = f32[32768]{0:T(1024)S(1)} all-gather(f32[1024]{0:T(1024)S(1)} %get-tuple-element.452), channel_id=2, replica_groups=mesh['batch'=4,'seq'=8] {'batch','seq'}, dimensions={0}, use_global_device_ids=true | all-gather | bytes 135168 | tf_op jit(solution)/shard_map/all_gather | solution.py:31
  747.5 9.2 exponential_reduce_fusion.1
  756.6 43.9 %gather_fusion.4 = f32[1024]{0:T(1024)S(1)} fusion(f32[1024,4748]{0,1:T(8,128)} %get-tuple-element.453, s32[1024]{0:T(1024)S(1)} %bitcast.288), kind=kCustom, calls=%fused_computation.4 | custom fusion | bytes 16384 | tf_op jit(solution)/shard_map/jit(take_along_axis)/gather | solution.py:379
  800.6 64.1 %all-gather.2 = f32[32768]{0:T(1024)S(1)} all-gather(f32[1024]{0:T(1024)S(1)} %select_select_fusion), channel_id=4, replica_groups=mesh['batch'=4,'seq'=8] {'batch','seq'}, dimensions={0}, use_global_device_ids=true | all-gather | bytes 135168 | tf_op jit(solution)/shard_map/all_gather | solution.py:31
  864.7 66.4 %all-gather.1 = f32[32768]{0:T(1024)S(1)} all-gather(f32[1024]{0:T(1024)S(1)} %exponential_reduce_fusion.1), channel_id=3, replica_groups=mesh['batch'=4,'seq'=8] {'batch','seq'}, dimensions={0}, use_global_device_ids=true | all-gather | bytes 135168 | tf_op jit(solution)/shard_map/all_gather | solution.py:31
  931.2 2.7 while.53
  935.3 18.3 fusion.148
  953.6 138.6 %reduce-scatter.8.cloned.1.call-done = f32[32,896]{1,0:T(8,128)} async-done(((f32[1024,896]{1,0:T(8,128)}), f32[32,896]{1,0:T(8,128)}) %reduce-scatter.8.cloned.1.call-update) | async-done | bytes 114704 | tf_op jit(solution)/shard_map/reduce_scatter | solution.py:402
  1095.4 11.8 multiply_convert_fusion.2
  1107.2 12.4 multiply_reduce_fusion.1
  1121.3 2.5 convolution_convert_fusion.4
  1127.4 22.1 %while.56 = (s32[]{:T(128)}, f32[256,2,7,64]{0,3,2,1:T(8,128)S(1)}, f32[2048,2,64]{0,2,1:T(8,128)S(1)}, f32[2048,2,64]{0,2,1:T(8,128)}, s32[]{:T(128)}, /*index=...) while((s32[]{:T(128)}, f32[256,2,7,64]{0,3,2,1:T(8,128)S(1)}, ...), condition=%wide.region_26.27_spmd.clone, body=%wide.region_25.26_spmd.clone.sunk | while | flops 2386625792 | bytes 132174072 | solution.py:141
  1130.0 6.0 fusion.227
  1136.0 2.3 fusion.229
  1139.8 9.7 fusion.230
  1152.7 3.1 convolution_convert_fusion.3
  1156.0 75.7 %reduce-scatter.10.cloned.1.call-done = bf16[256,128]{0,1:T(8,128)(2,1)} async-done(((bf16[2048,128]{0,1:T(8,128)(2,1)}), bf16[256,128]{0,1:T(8,128)(2,1)}) %reduce-scatter.10.cloned.1.call-update) | async-done | bytes 65552 | tf_op jit(solution)/shard_map/reduce_scatter | solution.py:235
  1232.6 64.5 %reduce-scatter.12.cloned.1.call-done = bf16[256,128]{0,1:T(8,128)(2,1)} async-done(((bf16[2048,128]{0,1:T(8,128)(2,1)}), bf16[256,128]{0,1:T(8,128)(2,1)}) %reduce-scatter.12.cloned.1.call-update) | async-done | bytes 65552 | tf_op jit(solution)/shard_map/reduce_scatter | solution.py:241
  1297.1 3.1 convolution_convert_fusion.2
  1300.7 8.0 convolution_convert_fusion.1
  1309.9 10.3 convolution_convert_fusion
  1321.1 2.7 fusion.85
  1323.9 3.2 scatter_custom_fusion.2
  1327.1 2.6 convert_element_type.177
  1329.6 3.7 all-to-all-start.2
  1333.6 34.0 %reduce-scatter.16.cloned.1.call-done = bf16[112,896]{1,0:T(8,128)(2,1)} async-done(((bf16[896,896]{1,0:T(8,128)(2,1)}), bf16[112,896]{1,0:T(8,128)(2,1)}) %reduce-scatter.16.cloned.1.call-update) | async-done | bytes 200720 | tf_op jit(solution)/shard_map/reduce_scatter | solution.py:435
  1367.6 70.6 %reduce-scatter.14.cloned.1.call-done = bf16[112,1152]{1,0:T(8,128)(2,1)} async-done(((bf16[896,1152]{1,0:T(8,128)(2,1)}), bf16[112,1152]{1,0:T(8,128)(2,1)}) %reduce-scatter.14.cloned.1.call-update) | async-done | bytes 258064 | tf_op jit(solution)/shard_map/reduce_scatter | solution.py:432
  1438.2 157.0 %reduce-scatter.20.cloned.1.call-done = bf16[608,896]{1,0:T(8,128)(2,1)} async-done(((bf16[4864,896]{1,0:T(8,128)(2,1)}), bf16[608,896]{1,0:T(8,128)(2,1)}) %reduce-scatter.20.cloned.1.call-update) | async-done | bytes 1089552 | tf_op jit(solution)/shard_map/reduce_scatter | solution.py:441
  1595.3 296.4 %reduce-scatter.18.cloned.1.call-done = bf16[112,9728]{1,0:T(8,128)(2,1)} async-done(((bf16[896,9728]{1,0:T(8,128)(2,1)}), bf16[112,9728]{1,0:T(8,128)(2,1)}) %reduce-scatter.18.cloned.1.call-update) | async-done | bytes 2179088 | tf_op jit(solution)/shard_map/reduce_scatter | solution.py:438
  1891.8 19.2 fusion.149
  1911.3 17.2 scatter_custom_fusion.3
  1928.5 11.0 multiply_reduce_fusion
  1939.6 32.5 %all-reduce.9.cloned.1.call-done = (bf16[112,1152]{1,0:T(8,128)(2,1)}, bf16[112,896]{1,0:T(8,128)(2,1)}, bf16[112,9728]{1,0:T(8,128)(2,1)}, bf16[608,896]{1,0:T(8,128)(2,1)}) async-done(((bf16[112,1152]{1,0:T(8,128)(2,1)}, bf16[112,896]{1,0:T(8,128)(2,1)}, bf16[112,9728]{1,0:T(8,128)(2,1)}, bf16[608,896]{1,0:T(8,128)(2,1)}), (bf16[112,1152]{1,0:T(8,128)(2,1)}, bf16[112,896]{1,0:T(8,128)(2,1)}, ...) | async-done | bytes 3727376 | tf_op jit(solution)/shard_map/psum | solution.py:446
  1975.3 3.4 fusion.73
  1978.7 2.4 fusion.78
  1984.4 40.0 %all-reduce.4 = (f32[]{:T(128)}, f32[3,896]{1,0:T(4,128)S(1)}, f32[1152]{0:T(1024)S(1)}) all-reduce(f32[]{:T(128)S(6)} %add.548, f32[3,896]{1,0:T(4,128)S(1)} %pad_maximum_fusion.8, f32[1152]{0:T(1024)S(1)} %convert_reduce_fusion), channel_id=1, replica_groups=mesh['batch'=4,'seq'=8] {'batch','seq'}, use_global_device_ids=true, to_apply=%region_45.46 | all-reduce | flops 3841 | bytes 30728 | tf_op jit(solution)/shard_map/psum | solution.py:458
  2028.9 6.6 multiply_subtract_fusion.2
  2035.7 8.4 multiply_subtract_fusion.1
  2046.7 41.5 %multiply_subtract_fusion = (f32[4748,896]{1,0:T(8,128)}, f32[4748,896]{1,0:T(8,128)}, f32[4748,896]{1,0:T(8,128)}) fusion(f32[4748,896]{1,0:T(8,128)} %param.43, f32[4748,896]{1,0:T(8,128)} %scatter_custom_fusion.3, f32[]{:T(128)S(6)} %min.23, f32[4748,896]{1,0:T(8,128)} %param.44, f32[4748,896]{1,0:T(8,128)} %param.45), kind=kLoop, calls=%fused_computation.87 | loop fusion | flops 68067328 | bytes 119117824 | tf_op jit(solution)/shard_map/sub | solution.py:281
  (417 shorter events, 52.8 us)
Async XLA Ops:
  7.2 76.1 %all-gather.11.cloned.1.call-start = ((), (), s32[]{:S(2)}) async-start(), calls=%async_computation.10 | async-start | bytes 2322432 | tf_op jit(solution)/shard_map/all_gather | solution.py:354
  9.0 186.1 %all-gather.13.cloned.1.call-start = ((), (), s32[]{:S(2)}) async-start(), calls=%async_computation.11 | async-start | bytes 1806336 | tf_op jit(solution)/shard_map/all_gather | solution.py:355
  10.8 456.1 %all-gather.15.cloned.1.call-start = ((), (), s32[]{:S(2)}) async-start(), calls=%async_computation.12 | async-start | bytes 19611648 | tf_op jit(solution)/shard_map/all_gather | solution.py:356
  15.7 39.9 %copy-start.54 = (s32[256,1]{0,1:T(1,128)}, s32[256,1]{0,1:T(1,128)S(1)}, u32[]{:S(2)}) copy-start(s32[256,1]{0,1:T(1,128)S(1)} %compare_select_fusion.3) | copy-start | bytes 3076
  17.8 16.4 all-to-all-start
  34.2 9.5 copy-start.28
  42.6 13.1 copy-start.56
  42.6 13.1 copy-start.31
  43.7 38.0 %all-to-all-start.1 = ((bf16[32,16,896]{2,1,0:T(8,128)(2,1)}), bf16[32,16,896]{2,1,0:T(8,128)(2,1)S(1)}, u32[]{:S(2)}, u32[]{:S(2)}) async-start(bf16[32,16,896]{2,1,0:T(8,128)(2,1)} %broadcast_select_fusion), calls=%async_computation.1 | async-start | bytes 1835008 | tf_op jit(solution)/shard_map/all_to_all | solution.py:343
  49.6 33.7 %copy-start.46 = (f32[1152]{0:T(1024)S(1)}, f32[1152]{0:T(1024)}, u32[]{:S(2)}) copy-start(f32[1152]{0:T(1024)} %param.61) | copy-start | bytes 13828
  49.6 548.9 %all-gather.17.cloned.1.call-start = ((), (), s32[]{:S(2)}) async-start(), calls=%async_computation.13 | async-start | bytes 9805824 | tf_op jit(solution)/shard_map/all_gather | solution.py:357
  52.4 611.1 %all-gather.19.cloned.1.call-start = ((), (), s32[]{:S(2)}) async-start(), calls=%async_computation.14 | async-start | bytes 1892352 | tf_op jit(solution)/shard_map/all_gather | solution.py:368
  55.7 30.2 %copy-start.57 = (s32[32]{0:T(128)}, s32[32]{0:T(128)S(1)}, u32[]{:S(2)}) copy-start(s32[32]{0:T(128)S(1)} %get-tuple-element.448) | copy-start | bytes 388
  55.8 30.2 %copy-start.35 = (f32[896]{0:T(1024)}, f32[896]{0:T(1024)S(1)}, u32[]{:S(2)}) copy-start(f32[896]{0:T(1024)S(1)} %get-tuple-element.321) | copy-start | bytes 10756
  55.8 140.2 %copy-start.33 = (pred[256]{0:T(512)(128)(4,1)}, pred[256]{0:T(512)(128)(4,1)S(1)}, u32[]{:S(2)}) copy-start(pred[256]{0:T(512)(128)(4,1)S(1)} %compare_and_fusion.2) | copy-start | bytes 772
  56.6 29.9 %copy-start.19 = (f32[256,32]{0,1:T(8,128)}, f32[256,32]{0,1:T(8,128)S(1)}, u32[]{:S(2)}) copy-start(f32[256,32]{0,1:T(8,128)S(1)} %get-tuple-element.447) | copy-start | bytes 98308
  83.0 113.0 %copy-start.12 = (bf16[256,896]{1,0:T(8,128)(2,1)}, bf16[256,896]{1,0:T(8,128)(2,1)S(1)}, u32[]{:S(2)}) copy-start(bf16[256,896]{1,0:T(8,128)(2,1)S(1)} %gather_fusion.1) | copy-start | bytes 1376260
  173.4 16.5 copy-start.22
  195.1 280.9 %copy-start.14 = (bf16[256,2,7,64]{0,3,2,1:T(8,128)(2,1)}, bf16[256,2,7,64]{0,3,2,1:T(8,128)(2,1)S(1)}, u32[]{:S(2)}) copy-start(bf16[256,2,7,64]{0,3,2,1:T(8,128)(2,1)S(1)} %convert_element_type.158) | copy-start | bytes 1376260
  198.3 921.3 %copy-start.3 = (f32[256,896]{1,0:T(8,128)}, f32[256,896]{1,0:T(8,128)S(1)}, u32[]{:S(2)}) copy-start(f32[256,896]{1,0:T(8,128)S(1)} %get-tuple-element.451) | copy-start | bytes 2752516
  482.7 126.5 %copy-start.58 = (s32[4]{0:T(128)S(1)}, s32[4]{0:T(128)}, u32[]{:S(2)}) copy-start(s32[4]{0:T(128)} %param.38) | copy-start | bytes 52
  482.7 127.1 %copy-start.59 = (s32[4]{0:T(128)S(1)}, s32[4]{0:T(128)}, u32[]{:S(2)}) copy-start(s32[4]{0:T(128)} %param.37) | copy-start | bytes 52
  482.7 128.4 %copy-start.60 = (f32[4]{0:T(128)S(1)}, f32[4]{0:T(128)}, u32[]{:S(2)}) copy-start(f32[4]{0:T(128)} %param.42) | copy-start | bytes 52
  482.7 129.8 %copy-start.61 = (f32[1,32]{1,0:T(1,128)S(1)}, f32[1,32]{1,0:T(1,128)}, u32[]{:S(2)}) copy-start(f32[1,32]{1,0:T(1,128)} %param.41) | copy-start | bytes 388
  482.7 129.9 %copy-start.62 = (f32[1,32]{1,0:T(1,128)S(1)}, f32[1,32]{1,0:T(1,128)}, u32[]{:S(2)}) copy-start(f32[1,32]{1,0:T(1,128)} %param.40) | copy-start | bytes 388
  609.2 483.1 %reduce-scatter.8.cloned.1.call-start = ((), (), s32[]{:S(2)}) async-start(), calls=%async_computation.15 | async-start | bytes 3784704 | tf_op jit(solution)/shard_map/reduce_scatter | solution.py:402
  653.4 281.9 %copy-start.37 = (s32[1024]{0:T(1024)}, s32[1024]{0:T(1024)S(1)}, u32[]{:S(2)}) copy-start(s32[1024]{0:T(1024)S(1)} %get-tuple-element.428) | copy-start | bytes 12292
  934.6 19.0 copy-start.39
  935.3 18.3 copy-start.52
  953.6 278.1 %reduce-scatter.10.cloned.1.call-start = ((), (), s32[]{:S(2)}) async-start(), calls=%async_computation.16 | async-start | bytes 589824 | tf_op jit(solution)/shard_map/reduce_scatter | solution.py:235
  1095.4 11.8 copy-start.10
  1150.4 146.8 %copy-start.13 = (bf16[256,896]{1,0:T(8,128)(2,1)S(1)}, bf16[256,896]{1,0:T(8,128)(2,1)}, u32[]{:S(2)}) copy-start(bf16[256,896]{1,0:T(8,128)(2,1)} %copy-done.12) | copy-start | bytes 1376260
  1150.4 146.8 %copy-start.34 = (pred[256]{0:T(512)(128)(4,1)S(1)}, pred[256]{0:T(512)(128)(4,1)}, u32[]{:S(2)}) copy-start(pred[256]{0:T(512)(128)(4,1)} %copy-done.33) | copy-start | bytes 772
  1150.4 146.8 %copy-start.36 = (f32[896]{0:T(1024)S(1)}, f32[896]{0:T(1024)}, u32[]{:S(2)}) copy-start(f32[896]{0:T(1024)} %copy-done.35) | copy-start | bytes 10756
  1150.4 146.8 %copy-start.51 = (f32[256]{0:T(256)S(1)}, f32[256]{0:T(256)}, u32[]{:S(2)}) copy-start(f32[256]{0:T(256)} %copy-done.50) | copy-start | bytes 3076
  1150.4 146.7 %reduce-scatter.12.cloned.1.call-start = ((), (), s32[]{:S(2)}) async-start(), calls=%async_computation.17 | async-start | bytes 589824 | tf_op jit(solution)/shard_map/reduce_scatter | solution.py:241
  1152.6 215.0 %reduce-scatter.16.cloned.1.call-start = ((), (), s32[]{:S(2)}) async-start(), calls=%async_computation.19 | async-start | bytes 1806336 | tf_op jit(solution)/shard_map/reduce_scatter | solution.py:435
  1155.8 145.0 %copy-start.11 = (f32[256,896]{1,0:T(8,128)S(1)}, f32[256,896]{1,0:T(8,128)}, u32[]{:S(2)}) copy-start(f32[256,896]{1,0:T(8,128)} %copy-done.10) | copy-start | bytes 2752516
  1155.8 282.4 %reduce-scatter.14.cloned.1.call-start = ((), (), s32[]{:S(2)}) async-start(), calls=%async_computation.18 | async-start | bytes 2322432 | tf_op jit(solution)/shard_map/reduce_scatter | solution.py:432
  1300.3 295.0 %reduce-scatter.20.cloned.1.call-start = ((), (), s32[]{:S(2)}) async-start(), calls=%async_computation.21 | async-start | bytes 9805824 | tf_op jit(solution)/shard_map/reduce_scatter | solution.py:441
  1308.8 582.9 %reduce-scatter.18.cloned.1.call-start = ((), (), s32[]{:S(2)}) async-start(), calls=%async_computation.20 | async-start | bytes 19611648 | tf_op jit(solution)/shard_map/reduce_scatter | solution.py:438
  1327.1 564.6 %copy-start.38 = (s32[1024]{0:T(1024)S(1)}, s32[1024]{0:T(1024)}, u32[]{:S(2)}) copy-start(s32[1024]{0:T(1024)} %copy-done.37) | copy-start | bytes 12292
  1327.1 564.7 %copy-start.40 = (f32[1024]{0:T(1024)S(1)}, f32[1024]{0:T(1024)}, u32[]{:S(2)}) copy-start(f32[1024]{0:T(1024)} %copy-done.39) | copy-start | bytes 12292
  1327.1 564.7 %copy-start.53 = (f32[1024]{0:T(1024)S(1)}, f32[1024]{0:T(1024)}, u32[]{:S(2)}) copy-start(f32[1024]{0:T(1024)} %copy-done.52) | copy-start | bytes 12292
  1329.6 581.6 %all-to-all-start.2 = ((bf16[32,16,896]{2,1,0:T(8,128)(2,1)}), bf16[32,16,896]{2,1,0:T(8,128)(2,1)S(1)}, u32[]{:S(2)}, u32[]{:S(2)}) async-start(bf16[32,16,896]{2,1,0:T(8,128)(2,1)} %bitcast.43), calls=%async_computation.5 | async-start | bytes 1835008 | tf_op jit(solution)/shard_map/all_to_all | solution.py:421
  1333.3 638.7 %all-reduce.9.cloned.1.call-start = ((), (), s32[]{:S(2)}) async-start(), calls=%async_computation.22 | async-start | bytes 7454720 | tf_op jit(solution)/shard_map/psum | solution.py:446
  1891.7 19.2 copy-start.55
  1891.8 19.2 copy-start.41
  1928.5 99.1 %copy-start.47 = (f32[1152]{0:T(1024)S(1)}, f32[1152]{0:T(1024)}, u32[]{:S(2)}) copy-start(f32[1152]{0:T(1024)} %param.61) | copy-start | bytes 13828
  1928.5 99.1 %copy-start.48 = (f32[1152]{0:T(1024)S(1)}, f32[1152]{0:T(1024)}, u32[]{:S(2)}) copy-start(f32[1152]{0:T(1024)} %param.62) | copy-start | bytes 13828
  1928.5 99.1 %copy-start.49 = (f32[1152]{0:T(1024)S(1)}, f32[1152]{0:T(1024)}, u32[]{:S(2)}) copy-start(f32[1152]{0:T(1024)} %param.63) | copy-start | bytes 13828
  1928.5 99.8 %copy-start.32 = (f32[3,896]{1,0:T(4,128)S(1)}, f32[3,896]{1,0:T(4,128)}, u32[]{:S(2)}) copy-start(f32[3,896]{1,0:T(4,128)} %param.58) | copy-start | bytes 32260
  1928.5 99.7 %copy-start.42 = (f32[3,896]{1,0:T(4,128)S(1)}, f32[3,896]{1,0:T(4,128)}, u32[]{:S(2)}) copy-start(f32[3,896]{1,0:T(4,128)} %param.59) | copy-start | bytes 32260
  1928.5 99.7 %copy-start.43 = (f32[3,896]{1,0:T(4,128)S(1)}, f32[3,896]{1,0:T(4,128)}, u32[]{:S(2)}) copy-start(f32[3,896]{1,0:T(4,128)} %param.60) | copy-start | bytes 32260
  1939.6 89.4 %copy-start.8 = (f32[608,896]{1,0:T(8,128)S(1)}, f32[608,896]{1,0:T(8,128)}, u32[]{:S(2)}) copy-start(f32[608,896]{1,0:T(8,128)} %param.55) | copy-start | bytes 6537220
  1975.3 60.2 %slice-start = ((s8[4358144]{0:T(1024)(128)(4,1)}), s8[163840]{0:T(1024)(128)(4,1)S(1)}, s32[]{:S(2)}) async-start(s8[4358144]{0:T(1024)(128)(4,1)} %bitcast.292), calls=%async_computation.23 | async-start | bytes 327680
  2035.6 8.5 copy-start.17
  2035.6 8.5 copy-start.21
  2035.6 8.5 copy-start.25
  2035.6 8.4 copy-start.26
  2035.6 9.7 copy-start.15
  2035.6 9.7 copy-start.18
  2035.6 9.7 copy-start.23
  2035.6 9.7 copy-start.24
  (17 other events, 63.9 us)
Sparse Core Ops, SparseCore 0:
  10.8 66.0 all-gather.10
  79.6 48.3 all-gather.12
  130.2 336.7 all-gather.14
  469.5 128.8 all-gather.16
  609.3 54.1 all-gather.18
  953.7 138.4 reduce-scatter.7
  1150.5 81.1 reduce-scatter.9
  1235.6 61.4 reduce-scatter.11
  1301.6 65.9 reduce-scatter.15
  1371.5 66.6 reduce-scatter.13
  1442.4 152.7 reduce-scatter.19
  1599.0 292.6 reduce-scatter.17
  1894.3 77.6 all-reduce.8
where the time goes:
time: 2110 us; the launch traced here: 2100 us
  waiting for transfers between devices  1290 us (61%)
  blocking collectives  362 us (17%)
  matrix products  164 us (8%)
  other arithmetic  163 us (8%)
  local copies, waits for them, and re-layouts  71.7 us (3%)
  between operations  26.8 us (1%)
    reduce_scatter x1, waiting for transfers between devices, per_device(): lax.psum_scatter(layer_grads[2].astype(jnp.bfloat16), 'seq', scatter_dime...  296 us
    all_gather x1, waiting for transfers between devices, per_device(): lax.all_gather(matrices[2], 'seq', axis=0, tiled=True)  269 us
    all_gather x3, blocking collectives, merged(): pieces = jax.tree.map(lambda part: lax.all_gather(part, axis), value)  197 us
    reduce_scatter x1, waiting for transfers between devices, per_device(): lax.psum_scatter(layer_grads[3].astype(jnp.bfloat16), 'seq', scatter_dime...  157 us
    reduce_scatter x1, waiting for transfers between devices, per_device(): lax.psum_scatter(jnp.dot(grad_logits, table, preferred_element_type=jnp.f...  139 us
    all_gather x1, waiting for transfers between devices, per_device(): lax.all_gather(matrices[3], 'seq', axis=0, tiled=True)  116 us
    reduce_scatter x1, waiting for transfers between devices, layer_backward(): lax.psum_scatter(grad_keys.reshape(length, KV * HD).astype(jnp.bfloat16),...  75.7 us
    reduce_scatter x1, waiting for transfers between devices, per_device(): lax.psum_scatter(layer_grads[0].astype(jnp.bfloat16), 'seq', scatter_dime...  70.6 us
  transfers between devices with their start and end apart: 16, of which 12 were waited for; matrix products, arithmetic and copies ran while one was open for 8% of the time, Pallas kernels for 0%

commit v1 on v0

v1 whole, which is shorter than its diff:
```python
import jax
import jax.numpy as jnp
from jax import lax
from jax.sharding import PartitionSpec as P

H = 14
KV = 2
HD = 64
FF = 4864
STEP = 5


NORM_EPS = 1e-06
ROPE_BASE = 1000000.0
NEG_BIG = -1e30
EPS_LOW = 0.8
EPS_HIGH = 0.28
BETA_KL = 0.1
CLIP_NORM = 0.05
BETA_ONE = 0.9
BETA_TWO = 0.95
ADAM_EPS = 1e-08
DECAY = 0.1
LR_MATRIX = 0.02
LR_OUT = 0.12
LR_GAIN = 1.0
LR_BIAS = 0.5


def norm_rows(values, gain):
    return values * lax.rsqrt(jnp.mean(values * values, axis=-1, keepdims=True) + NORM_EPS) * gain


def rotate(values, places, sign):
    half_width = values.shape[-1] // 2
    frequency = ROPE_BASE ** (-2.0 * jnp.arange(half_width, dtype=jnp.float32) / values.shape[-1])
    angles = places.astype(jnp.float32)[:, None] * frequency[None, :]
    cosine = jnp.cos(angles)[:, None, :]
    sine_part = sign * jnp.sin(angles)[:, None, :]
    front = values[..., :half_width]
    back_half = values[..., half_width:]
    return jnp.concatenate(
        [front * cosine - back_half * sine_part, back_half * cosine + front * sine_part], axis=-1
    )


def bit_groups(size, spans):
    stages, low = [], 0
    bits = size.bit_length() - 1
    for span in spans:
        span = min(span, bits - low)
        if span > 0:
            stages.append([mask << low for mask in range(1, 1 << span)])
            low += span
    while low < bits:
        span = min(2, bits - low)
        stages.append([mask << low for mask in range(1, 1 << span)])
        low += span
    return stages


def partner(value, axis, mask):
    size = lax.axis_size(axis)
    return lax.ppermute(value, axis, [(place, place ^ mask) for place in range(size)])


def spread(value, stages):
    held = value[None]
    for axis, masks in stages:
        held = jnp.concatenate([held] + [partner(held, axis, mask) for mask in masks])
    return held


def collect(blocks, stages):
    held = blocks
    for axis, masks in reversed(stages):
        count = len(masks) + 1
        held = held.reshape((count, held.shape[0] // count) + held.shape[1:])
        total = held[0].astype(jnp.float32)
        for place, mask in enumerate(masks):
            total = total + partner(held[place + 1], axis, mask).astype(jnp.float32)
        held = total.astype(jnp.bfloat16)
    return held[0]


def offsets_of(stages):
    offsets = [0]
    for _, masks in stages:
        offsets = offsets + [offset ^ mask for mask in masks for offset in offsets]
    return offsets


def exchange(value, axes):
    return lax.all_to_all(value, axes, split_axis=0, concat_axis=0, tiled=True)


def exchange_copies(value, axes):
    size = lax.axis_size(axes)
    return exchange(jnp.broadcast_to(value[None], (size,) + value.shape), axes)


def halve(value, axis, mask):
    own = (lax.axis_index(axis) & mask) != 0
    keep = jnp.where(own, value[1], value[0])
    send = jnp.where(own, value[0], value[1])
    return (
        keep.astype(jnp.float32) + partner(send, axis, mask).astype(jnp.float32)
    ).astype(jnp.bfloat16)


def double(value, axis, mask):
    own = (lax.axis_index(axis) & mask) != 0
    other = partner(value, axis, mask)
    return jnp.stack([jnp.where(own, other, value), jnp.where(own, value, other)])


def batch_scatter(value):
    size = lax.axis_size("batch")
    masks = []
    mask = 1
    while mask < size:
        masks.append(mask)
        mask *= 2
    held = value.reshape((2,) * len(masks) + (value.shape[0] // size,) + value.shape[1:])
    for depth, mask in enumerate(masks):
        held = halve(jnp.moveaxis(held, len(masks) - 1 - depth, 0), "batch", mask)
    return held


def batch_gather(value):
    size = lax.axis_size("batch")
    held = value
    mask = size // 2
    depth = 0
    while mask:
        held = double(held, "batch", mask)
        held = jnp.moveaxis(held, 0, depth)
        depth += 1
        mask //= 2
    return held.reshape((value.shape[0] * size,) + value.shape[1:])


def one_hot(places, size, dtype):
    return (places[:, None] == jnp.arange(size, dtype=jnp.int32)[None, :]).astype(dtype)


def place_rows(picker, values):
    return lax.dot_general(
        picker,
        values,
        (((0,), (0,)), ((), ())),
        precision=lax.Precision.HIGHEST,
        preferred_element_type=jnp.float32,
    )


def take_rows(picker, values):
    return jnp.dot(picker, values, preferred_element_type=jnp.float32)


def dot_tn(left, right):
    return lax.dot_general(
        left, right, (((0,), (0,)), ((), ())), preferred_element_type=jnp.float32
    )


def dot_nt(left, right):
    return lax.dot_general(
        left, right, (((1,), (1,)), ((), ())), preferred_element_type=jnp.float32
    )


def adam(weight, moment, second, gradient, learn_rate, decay_rate):
    moment = BETA_ONE * moment + (1.0 - BETA_ONE) * gradient
    second = BETA_TWO * second + (1.0 - BETA_TWO) * gradient * gradient
    corrected = moment / (1.0 - BETA_ONE**STEP)
    scaled = second / (1.0 - BETA_TWO**STEP)
    return (
        weight - learn_rate * (corrected / (jnp.sqrt(scaled) + ADAM_EPS) + decay_rate * weight),
        moment,
        second,
    )


def per_device(
    token_ids,
    row_lengths,
    prompt_lengths,
    picks,
    old_logp,
    ref_logp,
    rewards,
    embed,
    embed_m,
    embed_v,
    w_qkv,
    w_qkv_m,
    w_qkv_v,
    w_out,
    w_out_m,
    w_out_v,
    w_gateup,
    w_gateup_m,
    w_gateup_v,
    w_down,
    w_down_m,
    w_down_v,
    gains,
    gains_m,
    gains_v,
    bias,
    bias_m,
    bias_v,
):
    both = ("batch", "seq")
    owners = lax.axis_size(both)
    owner_index = lax.axis_index(both)
    seq_index = lax.axis_index("seq")
    row_index = lax.axis_index("batch")
    batch_count = lax.axis_size("batch")
    seq_count = lax.axis_size("seq")
    core_mask = 1
    low = jnp.bfloat16
    f32 = jnp.float32
    token_list = token_ids[0]
    local_len = token_list.shape[0]
    vrows, width = embed.shape
    shard = w_qkv.shape[0]
    ff_part = FF // seq_count
    capacity = max(2, 2 * local_len // owners)
    seq_stages = [("seq", masks) for masks in reversed(bit_groups(seq_count, (1, 2)))]
    batch_stages = [("batch", masks) for masks in reversed(bit_groups(batch_count, (1, 1)))]
    all_stages = seq_stages + batch_stages

    local_picks = picks[0]
    n_picks = local_picks.shape[0]
    pick_places = seq_index * local_len + local_picks
    live_mask = (
        (pick_places >= prompt_lengths[row_index]) & (pick_places + 1 < row_lengths[row_index])
    ).astype(f32)
    live_here = jnp.sum(live_mask).astype(jnp.int32)

    owner_of = token_list // vrows
    order = jnp.arange(local_len, dtype=jnp.int32)
    slot_of = jnp.sum(
        ((owner_of[:, None] == owner_of[None, :]) & (order[None, :] < order[:, None])).astype(
            jnp.int32
        ),
        axis=1,
    )
    place_of = owner_of * capacity + slot_of
    request_grid = jnp.arange(owners * capacity, dtype=jnp.int32)
    requests = jnp.sum(
        jnp.where(
            request_grid[:, None] == place_of[None, :],
            (token_list - owner_of * vrows)[None, :],
            0,
        ),
        axis=1,
    )
    message = jnp.concatenate(
        [
            requests.reshape(owners, capacity),
            jnp.broadcast_to(live_here[None, None], (owners, 1)),
        ],
        axis=1,
    )
    received = exchange(message, both)
    wanted = received[:, :capacity].reshape(-1)
    token_count = jnp.maximum(jnp.sum(received[:, capacity]).astype(f32), 1.0)
    found = jnp.take(embed, wanted, axis=0).astype(low).reshape(owners, capacity, width)
    returned = exchange(found, both).reshape(owners * capacity, width)
    placer = one_hot(place_of, owners * capacity, low)
    x_zero = take_rows(placer, returned).astype(low)
    stream_zero = x_zero.astype(f32)

    w_kv_low = w_qkv[:, H * HD :].astype(low)
    w_q_low = w_qkv[:, : H * HD].astype(low)
    w_out_low = w_out.astype(low)
    w_kv_full = lax.all_gather(w_kv_low, "seq", axis=0, tiled=True)
    w_q_full = lax.all_gather(w_q_low, "seq", axis=0, tiled=True)
    w_out_full = lax.all_gather(w_out_low, "seq", axis=0, tiled=True)
    half = shard // 2
    core = lax.axis_index("batch") & core_mask
    my_half = lax.dynamic_slice_in_dim(w_gateup, core * half, half, 0).astype(low)
    pieces = jnp.transpose(my_half.reshape(half, 2, seq_count, ff_part), (2, 0, 1, 3)).reshape(
        seq_count, half, 2 * ff_part
    )
    half_cols = exchange(pieces, "seq")
    w_gu = jnp.moveaxis(double(half_cols, "batch", core_mask), 0, 1).reshape(width, 2 * ff_part)
    w_down_low = w_down.astype(low)

    places = seq_index * local_len + order
    normed_one = norm_rows(stream_zero, gains[0]).astype(low)
    kv = jnp.dot(normed_one, w_kv_full, preferred_element_type=f32) + bias[H * HD :]
    keys = rotate(kv[:, : KV * HD].reshape(local_len, KV, HD), places, 1.0).reshape(
        local_len, KV * HD
    )
    kv_low = jnp.concatenate([keys, kv[:, KV * HD :]], axis=1).astype(low)
    kv_all = spread(kv_low, seq_stages).reshape(seq_count * local_len, 2 * KV * HD)
    key_places = (
        (seq_index ^ jnp.array(offsets_of(seq_stages), jnp.int32))[:, None] * local_len
        + order[None, :]
    ).reshape(-1)
    picker = one_hot(local_picks, local_len, low)
    targeter = one_hot(local_picks + 1, local_len, low)
    picked_zero = take_rows(picker, x_zero)
    target_rows = take_rows(targeter, x_zero)
    normed_picked = take_rows(picker, normed_one).astype(low)
    queries = jnp.dot(normed_picked, w_q_full, preferred_element_type=f32) + bias[: H * HD]
    queries = rotate(queries.reshape(n_picks, H, HD), pick_places, 1.0).astype(low)
    group = H // KV
    grouped = jnp.transpose(queries.reshape(n_picks, KV, group, HD), (1, 0, 2, 3)).reshape(
        KV, n_picks * group, HD
    )
    length = kv_all.shape[0]
    keys3 = jnp.transpose(kv_all[:, : KV * HD].reshape(length, KV, HD), (1, 0, 2))
    values3 = jnp.transpose(kv_all[:, KV * HD :].reshape(length, KV, HD), (1, 0, 2))
    scores = jnp.einsum("gqd,gkd->gqk", grouped, keys3, preferred_element_type=f32) * HD ** (-0.5)
    allowed = key_places[None, :] <= jnp.repeat(pick_places, group)[:, None]
    scores = jnp.where(allowed[None], scores, NEG_BIG)
    top = jnp.max(scores, axis=-1, keepdims=True)
    raised = jnp.exp(scores - top)
    chance = raised / jnp.sum(raised, axis=-1, keepdims=True)
    chance_low = chance.astype(low)
    attended = jnp.einsum("gqk,gkd->gqd", chance_low, values3, preferred_element_type=f32)
    mixed = (
        jnp.transpose(attended.reshape(KV, n_picks, group, HD), (1, 0, 2, 3))
        .reshape(n_picks, H * HD)
        .astype(low)
    )
    stream_one = picked_zero + jnp.dot(mixed, w_out_full, preferred_element_type=f32)

    normed_two = norm_rows(stream_one, gains[1]).astype(low)
    normed_two_all = spread(normed_two, seq_stages).reshape(seq_count * n_picks, width)
    gate_up = jnp.dot(normed_two_all, w_gu, preferred_element_type=f32)
    gate_part = gate_up[:, :ff_part]
    up_part = gate_up[:, ff_part:]
    hidden = (jax.nn.silu(gate_part) * up_part).astype(low)
    down_part = jnp.dot(hidden, w_down_low, preferred_element_type=f32).astype(low)
    stream_two = stream_one + collect(
        down_part.reshape(seq_count, n_picks, width), seq_stages
    ).astype(f32)

    final = norm_rows(stream_two, gains[2]).astype(low)
    all_final = spread(final, all_stages).reshape(owners * n_picks, width)
    table = embed.astype(low)
    logits = dot_nt(all_final, table)
    local_high = jnp.max(logits, axis=1, keepdims=True)
    raised_head = jnp.exp(logits - local_high)
    local_sum = jnp.sum(raised_head, axis=1, keepdims=True)
    raised_low = raised_head.astype(low)
    mean_row = jnp.dot(raised_low, table, preferred_element_type=f32) / local_sum
    held_row = mean_row.astype(low).reshape(owners, n_picks, width)
    held_log = (local_high + jnp.log(local_sum)).reshape(owners, n_picks, 1)
    for axis, masks in reversed(all_stages):
        count = len(masks) + 1
        rows = held_row.reshape((count, held_row.shape[0] // count) + held_row.shape[1:])
        logs = held_log.reshape((count, held_log.shape[0] // count) + held_log.shape[1:])
        others_rows = [rows[0]] + [
            partner(rows[at + 1], axis, mask) for at, mask in enumerate(masks)
        ]
        others_logs = [logs[0]] + [
            partner(logs[at + 1], axis, mask) for at, mask in enumerate(masks)
        ]
        highest = others_logs[0]
        for other in others_logs[1:]:
            highest = jnp.maximum(highest, other)
        shares = [jnp.exp(other - highest) for other in others_logs]
        summed = sum(shares[1:], shares[0])
        mixed_rows = sum(
            (
                share * other.astype(f32)
                for share, other in zip(shares[1:], others_rows[1:])
            ),
            shares[0] * others_rows[0].astype(f32),
        )
        held_row = (mixed_rows / summed).astype(low)
        held_log = highest + jnp.log(summed)
    mean_rows = held_row[0].astype(f32)
    log_total = held_log[0][:, 0]
    target_logit = jnp.sum(final.astype(f32) * target_rows, axis=1)
    logp = target_logit - log_total
    advantage = rewards[row_index] - jnp.mean(rewards)
    clip_weight = jnp.clip(jnp.exp(logp - old_logp[0]), 1.0 - EPS_LOW, 1.0 + EPS_HIGH)
    loss_here = jnp.sum(
        live_mask
        * (-clip_weight * advantage * logp + 0.5 * BETA_KL * (logp - ref_logp[0]) ** 2)
    )
    coefficient = (
        live_mask * (-clip_weight * advantage + BETA_KL * (logp - ref_logp[0])) / token_count
    )
    grad_final = coefficient[:, None] * (target_rows - mean_rows)
    pair = spread(jnp.stack([coefficient, log_total], axis=1), all_stages).reshape(
        owners * n_picks, 2
    )
    scaled_final = (
        all_final.astype(f32) * (-pair[:, :1] * jnp.exp(local_high - pair[:, 1:]))
    ).astype(low)
    grad_head = dot_tn(raised_low, scaled_final)

    unused, pull_final = jax.vjp(norm_rows, stream_two, gains[2])
    grad_two, grad_gain_two = pull_final(grad_final)
    branch_all = spread(grad_two.astype(low), seq_stages).reshape(seq_count * n_picks, width)
    grad_hidden = dot_nt(branch_all, w_down_low)
    grad_down = dot_tn(hidden, branch_all).astype(low)
    sigmoid_gate = jax.nn.sigmoid(gate_part)
    grad_gate = grad_hidden * up_part * sigmoid_gate * (1.0 + gate_part * (1.0 - sigmoid_gate))
    grad_up = grad_hidden * gate_part * sigmoid_gate
    grad_gu = jnp.concatenate([grad_gate, grad_up], axis=1).astype(low)
    grad_normed_two = collect(
        dot_nt(grad_gu, w_gu).astype(low).reshape(seq_count, n_picks, width), seq_stages
    ).astype(f32)
    grad_gu_w = dot_tn(normed_two_all, grad_gu).astype(low)
    unused, pull_two = jax.vjp(norm_rows, stream_one, gains[1])
    part_one, grad_gain_one = pull_two(grad_normed_two)
    grad_one = grad_two + part_one
    mixed_grad = grad_one.astype(low)
    grad_mixed = dot_nt(mixed_grad, w_out_full).astype(low)
    grad_grouped = jnp.transpose(
        grad_mixed.reshape(n_picks, KV, group, HD), (1, 0, 2, 3)
    ).reshape(KV, n_picks * group, HD)
    inner = jnp.sum(grad_grouped.astype(f32) * attended, axis=-1, keepdims=True)
    grad_chance = jnp.einsum("gqd,gkd->gqk", grad_grouped, values3, preferred_element_type=f32)
    grad_scores = (chance * (grad_chance - inner)).astype(low)
    grad_query = jnp.einsum(
        "gqk,gkd->gqd", grad_scores, keys3, preferred_element_type=f32
    ) * HD ** (-0.5)
    grad_keys = jnp.einsum(
        "gqk,gqd->kgd", grad_scores, grouped, preferred_element_type=f32
    ) * HD ** (-0.5)
    grad_values = jnp.einsum("gqk,gqd->kgd", chance_low, grad_grouped, preferred_element_type=f32)
    grad_kv = jnp.concatenate(
        [grad_keys.reshape(length, KV * HD), grad_values.reshape(length, KV * HD)], axis=1
    ).astype(low)
    own_kv = collect(grad_kv.reshape(seq_count, local_len, 2 * KV * HD), seq_stages).astype(f32)
    query_pre = jnp.transpose(grad_query.reshape(KV, n_picks, group, HD), (1, 0, 2, 3))
    query_pre = (
        rotate(query_pre.reshape(n_picks, H, HD), pick_places, -1.0)
        .reshape(n_picks, H * HD)
        .astype(low)
    )
    key_pre = rotate(own_kv[:, : KV * HD].reshape(local_len, KV, HD), places, -1.0)
    kv_pre = jnp.concatenate(
        [key_pre.reshape(local_len, KV * HD), own_kv[:, KV * HD :]], axis=1
    ).astype(low)
    grad_bias = jnp.concatenate(
        [jnp.sum(query_pre.astype(f32), axis=0), jnp.sum(kv_pre.astype(f32), axis=0)]
    )
    picker_f32 = picker.astype(f32)
    grad_normed_one = dot_nt(kv_pre, w_kv_full) + place_rows(
        picker_f32, dot_nt(query_pre, w_q_full)
    )
    unused, pull_one = jax.vjp(norm_rows, stream_zero, gains[0])
    part_zero, grad_gain_zero = pull_one(grad_normed_one)
    grad_zero = part_zero + place_rows(
        jnp.concatenate([picker_f32, targeter.astype(f32)], axis=0),
        jnp.concatenate([grad_one, coefficient[:, None] * final.astype(f32)], axis=0),
    )
    sendback = dot_tn(placer, grad_zero.astype(low)).astype(low)
    arrived = exchange(sendback.reshape(owners, capacity, width), both).reshape(-1, width)
    grad_embed = grad_head.at[wanted].add(arrived.astype(f32))

    def columns_out(value):
        rows = value.shape[0]
        cut = jnp.transpose(value.reshape(rows, seq_count, shard), (1, 0, 2))
        return exchange(cut, "seq").reshape(seq_count * rows, shard)

    def rows_out(value):
        return exchange_copies(value, "seq").reshape(seq_count * value.shape[0], -1)

    grad_q_w = dot_tn(columns_out(normed_picked), rows_out(query_pre))
    grad_out_w = dot_tn(columns_out(mixed), rows_out(mixed_grad))
    grad_kv_w = jnp.sum(
        exchange(
            dot_tn(normed_one, kv_pre).astype(low).reshape(seq_count, shard, 2 * KV * HD), "seq"
        ).astype(f32),
        axis=0,
    )
    small = jnp.concatenate([grad_q_w, grad_kv_w, grad_out_w], axis=1).astype(low)
    small = batch_gather(batch_scatter(small)).astype(f32)
    gu_quarter = batch_scatter(grad_gu_w)
    gu_rows = width // batch_count
    gu_cut = gu_quarter
    grad_gu_all = batch_gather(gu_cut).reshape(seq_count, shard, 2 * ff_part)
    gu_shard = exchange(grad_gu_all, "seq")
    gu_shard = jnp.transpose(
        gu_shard.reshape(seq_count, shard, 2, ff_part), (1, 2, 0, 3)
    ).reshape(shard, 2 * FF)
    shards = (
        small[:, : (H + 2 * KV) * HD],
        small[:, (H + 2 * KV) * HD :],
        gu_shard.astype(f32),
        batch_gather(batch_scatter(grad_down)).astype(f32),
    )
    shard_squares = (
        jnp.sum(shards[0] * shards[0])
        + jnp.sum(shards[1] * shards[1])
        + jnp.sum(shards[2] * shards[2])
        + jnp.sum(shards[3] * shards[3])
    )
    local_squares = jnp.sum(grad_embed * grad_embed) + shard_squares / batch_count
    summary = jnp.concatenate(
        [
            jnp.stack([local_squares, loss_here]),
            grad_gain_zero,
            grad_gain_one,
            grad_gain_two,
            grad_bias,
        ]
    )
    summary = jnp.sum(exchange_copies(summary, both), axis=0)
    squares, loss_sum = summary[0], summary[1]
    grad_gains = summary[2 : 2 + 3 * width].reshape(3, width)
    grad_bias_all = summary[2 + 3 * width :]
    grad_norm = jnp.sqrt(
        squares + jnp.sum(grad_gains * grad_gains) + jnp.sum(grad_bias_all * grad_bias_all)
    )
    factor = jnp.minimum(1.0, CLIP_NORM / (grad_norm + 1e-06))
    embed_new = adam(embed, embed_m, embed_v, grad_embed * factor, LR_MATRIX, DECAY)
    qkv_new = adam(w_qkv, w_qkv_m, w_qkv_v, shards[0] * factor, LR_MATRIX, DECAY)
    out_new = adam(w_out, w_out_m, w_out_v, shards[1] * factor, LR_OUT, DECAY)
    gateup_new = adam(w_gateup, w_gateup_m, w_gateup_v, shards[2] * factor, LR_MATRIX, DECAY)
    down_new = adam(w_down, w_down_m, w_down_v, shards[3] * factor, LR_MATRIX, DECAY)
    gains_new = adam(gains, gains_m, gains_v, grad_gains * factor, LR_GAIN, 0.0)
    bias_new = adam(bias, bias_m, bias_v, grad_bias_all * factor, LR_BIAS, 0.0)
    return (
        loss_sum,
        token_count,
        grad_norm,
        *embed_new,
        *qkv_new,
        *out_new,
        *gateup_new,
        *down_new,
        *gains_new,
        *bias_new,
    )


def solution(mesh):
    in_specs = (
        P("batch", "seq"),
        P(),
        P(),
        P("batch", "seq"),
        P("batch", "seq"),
        P("batch", "seq"),
        P(),
        P(("batch", "seq"), None),
        P(("batch", "seq"), None),
        P(("batch", "seq"), None),
        P("seq", None),
        P("seq", None),
        P("seq", None),
        P("seq", None),
        P("seq", None),
        P("seq", None),
        P("seq", None),
        P("seq", None),
        P("seq", None),
        P("seq", None),
        P("seq", None),
        P("seq", None),
        P(),
        P(),
        P(),
        P(),
        P(),
        P(),
    )
    out_specs = (
        P(),
        P(),
        P(),
        P(("batch", "seq"), None),
        P(("batch", "seq"), None),
        P(("batch", "seq"), None),
        P("seq", None),
        P("seq", None),
        P("seq", None),
        P("seq", None),
        P("seq", None),
        P("seq", None),
        P("seq", None),
        P("seq", None),
        P("seq", None),
        P("seq", None),
        P("seq", None),
        P("seq", None),
        P(),
        P(),
        P(),
        P(),
        P(),
        P(),
    )
    return jax.shard_map(
        per_device, mesh=mesh, in_specs=in_specs, out_specs=out_specs, check_vma=False
    )
```

time: 2110 us -> 737 us (0.35)
  waiting for transfers between devices: 1290 us -> 181 us
  blocking collectives: 362 us -> 66.9 us
  starting transfers between devices: 17.9 us -> 114 us
  matrix products: 164 us -> 98.2 us
    reduce_scatter x7 -> x0, waiting for transfers between devices: 837 us -> none  [the longest x1 296 us: per_device(): lax.psum_scatter(layer_grads[2].astype(jnp.bfloat16), 'seq', scatter_dime...]
    all_gather x5 -> x2, waiting for transfers between devices: 394 us -> 0.04 us  [the longest x1 0.02 us: per_device(): w_q_full = lax.all_gather(w_q_low, 'seq', axis=0, tiled=True)]
    all_gather x5 -> x1, blocking collectives: 283 us -> 47.4 us  [per_device(): w_kv_full = lax.all_gather(w_kv_low, 'seq', axis=0, tiled=True)]
    ppermute x0 -> x61, waiting for transfers between devices: none -> 124 us  [partner(): lax.ppermute(value, axis, [(place, place ^ mask) for place in range(size)])]
    ppermute x0 -> x61, starting transfers between devices: none -> 73.3 us  [partner(): lax.ppermute(value, axis, [(place, place ^ mask) for place in range(size)])]
    dot_general x22 -> x30, matrix products: 164 us -> 93.9 us  [the longest x7 26.3 us: dot_tn(): lax.dot_general(left, right, (((0,), (0,)), ((), ())), preferred_element_...]
    gather x5 -> x1, local copies, waits for them, and re-layouts: 54.8 us -> 8.37 us  [per_device(): jnp.take(embed, wanted, axis=0).astype(low).reshape(owners, capacity, width)]
    psum x1 -> x0, blocking collectives: 40 us -> none  [per_device(): lax.psum((local_squares, jnp.stack([grad_gain_zero, grad_gain_one, grad_g...]
  transfers between devices with their start and end apart: 16 -> 73, of which waited for: 12 -> 38; matrix products, arithmetic and copies ran while one was open for 8% -> 28% of each run, Pallas kernels for 0% -> 0%
where the time goes in v1:
time: 737 us; the launch traced here: 729 us
  waiting for transfers between devices  181 us (25%)
  other arithmetic  156 us (21%)
  starting transfers between devices  114 us (15%)
  matrix products  98.2 us (13%)
  local copies, waits for them, and re-layouts  86.4 us (12%)
  blocking collectives  66.9 us (9%)
  between operations  26.8 us (4%)
    ppermute x61, waiting for transfers between devices, partner(): lax.ppermute(value, axis, [(place, place ^ mask) for place in range(size)])  124 us
    ppermute x61, starting transfers between devices, partner(): lax.ppermute(value, axis, [(place, place ^ mask) for place in range(size)])  73.3 us
    sub x7, other arithmetic, adam(): weight - learn_rate * (corrected / (jnp.sqrt(scaled) + ADAM_EPS) + decay_...  60.7 us
    all_to_all x10, waiting for transfers between devices, exchange(): return lax.all_to_all(value, axes, split_axis=0, concat_axis=0, tiled=True)  56.3 us
    all_gather x1, blocking collectives, per_device(): w_kv_full = lax.all_gather(w_kv_low, 'seq', axis=0, tiled=True)  47.4 us
    all_to_all x10, starting transfers between devices, exchange(): return lax.all_to_all(value, axes, split_axis=0, concat_axis=0, tiled=True)  40.3 us
    dot_general x7, matrix products, dot_tn(): lax.dot_general(left, right, (((0,), (0,)), ((), ())), preferred_element_...  26.3 us
    dot_general x6, matrix products, dot_nt(): lax.dot_general(left, right, (((1,), (1,)), ((), ())), preferred_element_...  25.2 us
  transfers between devices with their start and end apart: 73, of which 38 were waited for; matrix products, arithmetic and copies ran while one was open for 28% of the time, Pallas kernels for 0%

profile of v1, /device:TPU:0, one launch (start us, length us, event | category | flops | bytes accessed | tf_op | source)
XLA Modules:
  0.0 729.3 jit_solution(5906011547828867677)
XLA Ops:
  18.2 7.3 %all-to-all-start = ((s32[32,1,17]{2,1,0:T(1,128)}), s32[32,1,17]{2,1,0:T(1,128)S(1)}, u32[]{:S(2)}, u32[]{:S(2)}) async-start(s32[32,1,17]{2,1,0:T(1,128)} %bitcast.9), calls=%async_computation | async-start | bytes 32768 | tf_op jit(solution)/shard_map/all_to_all | solution.py:94
  29.0 3.5 all-to-all-done
  32.6 8.4 %gather_fusion = bf16[512,896]{1,0:T(8,128)(2,1)S(1)} fusion(f32[4748,896]{1,0:T(8,128)} %param.36, s32[1024]{0:T(1024)S(1)} %pad_clamp_fusion), kind=kCustom, calls=%fused_computation | custom fusion | bytes 1837056 | tf_op jit(solution)/shard_map/jit(_take)/gather | solution.py:271
  42.2 2.6 all-to-all-start.1
  50.0 47.4 %all_gather.10 = bf16[896,256]{1,0:T(8,128)(2,1)S(1)} all-gather(bf16[112,256]{1,0:T(8,128)(2,1)S(1)} %slice-done.2), channel_id=1, replica_groups=mesh['batch'=4,'seq'=8] {'seq'}, dimensions={0}, use_global_device_ids=true | all-gather | bytes 516096 | tf_op jit(solution)/shard_map/all_gather | solution.py:280
  100.1 3.7 all-to-all-start.2
  108.9 2.4 collective-permute-start.1
  112.2 23.3 %collective-permute-done = bf16[1,256,256]{1,2,0:T(8,128)(2,1)S(1)} collective-permute-done((bf16[1,256,256]{1,2,0:T(8,128)(2,1)S(1)}, bf16[1,256,256]{1,2,0:T(8,128)(2,1)S(1)}, u32[]{:S(2)}, u32[]{:S(2)}) %collective-permute-start) | collective-permute-done | bytes 131104 | tf_op jit(solution)/shard_map/ppermute | solution.py:64
  135.5 14.2 %collective-permute-done.1 = bf16[1,256,256]{1,2,0:T(8,128)(2,1)S(1)} collective-permute-done((bf16[1,256,256]{1,2,0:T(8,128)(2,1)S(1)}, bf16[1,256,256]{1,2,0:T(8,128)(2,1)S(1)}, u32[]{:S(2)}, u32[]{:S(2)}) %collective-permute-start.1) | collective-permute-done | bytes 131104 | tf_op jit(solution)/shard_map/ppermute | solution.py:64
  153.3 7.9 %collective-permute-done.3 = bf16[4,256,256]{1,2,0:T(8,128)(2,1)S(1)} collective-permute-done((bf16[4,256,256]{1,2,0:T(8,128)(2,1)S(1)}, bf16[4,256,256]{1,2,0:T(8,128)(2,1)S(1)}, u32[]{:S(2)}, u32[]{:S(2)}) %collective-permute-start.3) | collective-permute-done | bytes 524320 | tf_op jit(solution)/shard_map/ppermute | solution.py:64
  168.8 4.3 fusion.142
  173.1 2.5 fusion.29
  180.6 3.4 collective-permute-start.4
  186.4 3.1 collective-permute-done.5
  194.2 2.4 collective-permute-done.7
  201.5 4.3 collective-permute-done.9
  216.3 2.4 collective-permute-start.14
  221.4 3.3 collective-permute-done.15
  228.5 2.4 collective-permute-done.16
  232.2 7.8 %collective-permute-done.17 = bf16[8,32,896]{2,1,0:T(8,128)(2,1)S(1)} collective-permute-done((bf16[8,32,896]{2,1,0:T(8,128)(2,1)S(1)}, bf16[8,32,896]{2,1,0:T(8,128)(2,1)S(1)}, u32[]{:S(2)}, u32[]{:S(2)}) %collective-permute-start.17) | collective-permute-done | bytes 458784 | tf_op jit(solution)/shard_map/ppermute | solution.py:64
  248.2 18.3 %fusion.144 = (f32[1024]{0:T(1024)S(1)}, f32[1024,4748]{0,1:T(8,128)}) fusion(bf16[1024,896]{1,0:T(8,128)(2,1)} %bitcast.477, f32[4748,896]{1,0:T(8,128)} %param.36), kind=kOutput, calls=%fused_computation.421 | convolution fusion | flops 8721732608 | bytes 38303744 | tf_op jit(solution)/shard_map/dot_general | solution.py:168
  266.5 9.2 %fusion.1 = f32[1024]{0:T(1024)S(1)} fusion(f32[1024,4748]{0,1:T(8,128)} %get-tuple-element.206, f32[1024]{0:T(1024)S(1)} %get-tuple-element.205), kind=kLoop, calls=%fused_computation.5 | loop fusion | flops 9722880 | bytes 19456000 | tf_op jit(solution)/shard_map/reduce_sum | solution.py:351
  278.4 4.6 all-to-all-start.4
  284.9 20.2 %divide_convert_fusion = bf16[1024,896]{1,0:T(8,128)(2,1)} fusion(f32[1024]{0:T(1024)S(1)} %fusion.1, f32[4748,896]{1,0:T(8,128)} %param.36, f32[1024,4748]{0,1:T(8,128)} %get-tuple-element.206, f32[1024]{0:T(1024)S(1)} %get-tuple-element.205), kind=kOutput, calls=%fused_computation.23 | convolution fusion | flops 8728430592 | bytes 38307840 | tf_op jit(solution)/shard_map/dot_general | solution.py:353
  309.6 3.7 collective-permute-start.24
  315.0 2.8 collective-permute-done.23
  324.7 2.9 collective-permute-done.27
  333.0 5.4 collective-permute-done.29
  340.8 6.1 collective-permute-done.33
  348.1 2.4 collective-permute-start.36
  363.3 18.7 %fusion.12 = f32[4748,896]{1,0:T(8,128)} fusion(f32[1024,4748]{0,1:T(8,128)} %get-tuple-element.206, f32[1024]{0:T(1024)S(1)} %copy-done.65, bf16[1024,896]{1,0:T(8,128)(2,1)S(1)} %bitcast.478, f32[1024]{0:T(1024)S(1)} %bitcast.474), kind=kOutput, calls=%fused_computation.32 | convolution fusion | flops 8725094400 | bytes 38307840 | tf_op jit(solution)/shard_map/dot_general | solution.py:162
  383.4 5.3 collective-permute-done.40
  394.6 3.3 copy.282
  417.7 2.8 multiply_convert_fusion
  429.5 2.8 fusion.146
  433.5 4.8 collective-permute-done.45
  448.0 4.8 collective-permute-done.47
  454.3 3.4 all-to-all-start.7
  457.7 2.9 fusion.39
  460.6 3.9 all-to-all-done.7
  465.3 4.1 all-to-all-start.8
  472.4 8.8 %all-to-all-done.8 = bf16[8,32,896]{2,1,0:T(8,128)(2,1)} async-done(((bf16[8,32,896]{2,1,0:T(8,128)(2,1)}), bf16[8,32,896]{2,1,0:T(8,128)(2,1)}, u32[]{:S(2)}, u32[]{:S(2)}) %all-to-all-start.8) | async-done | bytes 458784 | tf_op jit(solution)/shard_map/all_to_all | solution.py:94
  482.8 3.8 all-to-all-start.5
  491.8 7.3 all-to-all-done.5
  499.8 3.6 all-to-all-start.6
  508.4 7.5 %all-to-all-done.6 = bf16[8,112,256]{2,1,0:T(8,128)(2,1)S(1)} async-done(((bf16[8,112,256]{2,1,0:T(8,128)(2,1)}), bf16[8,112,256]{2,1,0:T(8,128)(2,1)S(1)}, u32[]{:S(2)}, u32[]{:S(2)}) %all-to-all-start.6) | async-done | bytes 458784 | tf_op jit(solution)/shard_map/all_to_all | solution.py:94
  515.9 3.5 all-to-all-start.3
  525.8 18.4 %all-to-all-done.3 = bf16[32,16,896]{2,1,0:T(8,128)(2,1)S(1)} async-done(((bf16[32,16,896]{2,1,0:T(8,128)(2,1)}), bf16[32,16,896]{2,1,0:T(8,128)(2,1)S(1)}, u32[]{:S(2)}, u32[]{:S(2)}) %all-to-all-start.3) | async-done | bytes 917536 | tf_op jit(solution)/shard_map/all_to_all | solution.py:94
  545.0 3.6 all-to-all-start.9
  549.4 4.4 collective-permute-done.50
  555.3 3.6 collective-permute-done.51
  565.9 17.4 %scatter_custom_fusion = f32[4748,896]{1,0:T(8,128)} fusion(f32[4748,896]{1,0:T(8,128)} %fusion.12, s32[512]{0:T(512)} %bitcast.470, bf16[512,896]{1,0:T(8,128)(2,1)} %bitcast.404), kind=kCustom, calls=%fused_computation.47 | custom fusion | flops 917504 | bytes 17934336 | tf_op jit(solution)/shard_map/scatter-add | solution.py:462
  583.3 10.8 %multiply_reduce_fusion = f32[]{:T(128)} fusion(f32[4748,896]{1,0:T(8,128)} %scatter_custom_fusion), kind=kLoop, calls=%fused_computation.10 | loop fusion | flops 8508415 | bytes 17016836 | tf_op jit(solution)/shard_map/reduce_sum | solution.py:502
  594.1 7.0 all-to-all-done.9
  605.9 19.5 %all_to_all.63 = f32[32,1,3842]{2,1,0:T(1,128)} all-to-all(f32[32,1,3842]{2,1,0:T(1,128)S(1)} %broadcast_in_dim.75), channel_id=1, replica_groups=mesh['batch'=4,'seq'=8] {'batch','seq'}, dimensions={0} | all-to-all | bytes 983552 | tf_op jit(solution)/shard_map/all_to_all | solution.py:94
  630.7 2.7 fusion.17
  633.5 2.5 convert_multiply_fusion
  636.0 6.8 mul.1171
  642.8 7.1 copy.289
  649.9 6.1 mul.1173
  657.8 41.4 %multiply_subtract_fusion = (f32[4748,896]{1,0:T(8,128)}, f32[4748,896]{1,0:T(8,128)}, f32[4748,896]{1,0:T(8,128)}) fusion(f32[4748,896]{1,0:T(8,128)} %param.36, f32[4748,896]{1,0:T(8,128)} %scatter_custom_fusion, f32[]{:T(128)S(6)} %min.19, f32[4748,896]{1,0:T(8,128)} %param.37, f32[4748,896]{1,0:T(8,128)} %param.38), kind=kLoop, calls=%fused_computation.8 | loop fusion | flops 68067328 | bytes 119117824 | tf_op jit(solution)/shard_map/sub | solution.py:179
  699.3 2.7 multiply_subtract_fusion.3
  704.0 10.2 %multiply_subtract_fusion.1 = (f32[112,9728]{1,0:T(8,128)}, f32[112,9728]{1,0:T(8,128)}, f32[112,9728]{1,0:T(8,128)}) fusion(f32[112,9728]{1,0:T(8,128)} %param.45, f32[112,9728]{1,0:T(8,128)S(1)} %bitcast.393, f32[112,9728]{1,0:T(8,128)} %param.46, f32[112,9728]{1,0:T(8,128)} %param.47), kind=kLoop, calls=%fused_computation.16 | loop fusion | flops 16343040 | bytes 30507008 | tf_op jit(solution)/shard_map/sub | solution.py:179
  715.3 3.8 multiply_subtract_fusion.2
  (569 shorter events, 210.9 us)
Async XLA Ops:
  7.2 158.9 %all-gather.3.cloned.1.call-start = ((), (), s32[]{:S(2)}) async-start(), calls=%async_computation.11 | async-start | bytes 1806336 | tf_op jit(solution)/shard_map/all_gather | solution.py:281
  18.2 14.4 %all-to-all-start = ((s32[32,1,17]{2,1,0:T(1,128)}), s32[32,1,17]{2,1,0:T(1,128)S(1)}, u32[]{:S(2)}, u32[]{:S(2)}) async-start(s32[32,1,17]{2,1,0:T(1,128)} %bitcast.9), calls=%async_computation | async-start | bytes 32768 | tf_op jit(solution)/shard_map/all_to_all | solution.py:94
  25.5 153.1 %all-gather.5.cloned.1.call-start = ((), (), s32[]{:S(2)}) async-start(), calls=%async_computation.12 | async-start | bytes 1806336 | tf_op jit(solution)/shard_map/all_gather | solution.py:282
  42.2 57.9 %all-to-all-start.1 = ((bf16[32,16,896]{2,1,0:T(8,128)(2,1)}), bf16[32,16,896]{2,1,0:T(8,128)(2,1)S(1)}, u32[]{:S(2)}, u32[]{:S(2)}) async-start(bf16[32,16,896]{2,1,0:T(8,128)(2,1)} %select_convert_fusion), calls=%async_computation.1 | async-start | bytes 1835008 | tf_op jit(solution)/shard_map/all_to_all | solution.py:94
  100.1 51.1 %all-to-all-start.2 = ((bf16[8,56,1216]{2,1,0:T(8,128)(2,1)}), bf16[8,56,1216]{2,1,0:T(8,128)(2,1)S(1)}, u32[]{:S(2)}, u32[]{:S(2)}) async-start(bf16[8,56,1216]{2,1,0:T(8,128)(2,1)} %reshape.876), calls=%async_computation.2 | async-start | bytes 2293760 | tf_op jit(solution)/shard_map/all_to_all | solution.py:94
  106.9 28.5 %collective-permute-start = (bf16[1,256,256]{1,2,0:T(8,128)(2,1)S(1)}, bf16[1,256,256]{1,2,0:T(8,128)(2,1)S(1)}, u32[]{:S(2)}, u32[]{:S(2)}) collective-permute-start(bf16[1,256,256]{1,2,0:T(8,128)(2,1)S(1)} %get-tuple-element.148), channel_id=1, source_target_pairs={{0,2},{1,3},{2,0},{3,1},{4,6},{5,7},{6,4},{7,5},{8,10},{9,11},{10,... | collective-permute-start | bytes 393224 | tf_op jit(solution)/shard_map/ppermute | solution.py:64
  108.9 40.8 %collective-permute-start.1 = (bf16[1,256,256]{1,2,0:T(8,128)(2,1)S(1)}, bf16[1,256,256]{1,2,0:T(8,128)(2,1)S(1)}, u32[]{:S(2)}, u32[]{:S(2)}) collective-permute-start(bf16[1,256,256]{1,2,0:T(8,128)(2,1)S(1)} %get-tuple-element.148), channel_id=1, source_target_pairs={{0,4},{1,5},{2,6},{3,7},{4,0},{5,1},{6,2},{7,3},{8,12},{9,13},{10,... | collective-permute-start | bytes 393224 | tf_op jit(solution)/shard_map/ppermute | solution.py:64
  111.3 38.4 %collective-permute-start.2 = (bf16[1,256,256]{1,2,0:T(8,128)(2,1)S(1)}, bf16[1,256,256]{1,2,0:T(8,128)(2,1)S(1)}, u32[]{:S(2)}, u32[]{:S(2)}) collective-permute-start(bf16[1,256,256]{1,2,0:T(8,128)(2,1)S(1)} %get-tuple-element.148), channel_id=1, source_target_pairs={{0,6},{1,7},{2,4},{3,5},{4,2},{5,3},{6,0},{7,1},{8,14},{9,15},{10,... | collective-permute-start | bytes 393224 | tf_op jit(solution)/shard_map/ppermute | solution.py:64
  149.7 11.5 %collective-permute-start.3 = (bf16[4,256,256]{1,2,0:T(8,128)(2,1)S(1)}, bf16[4,256,256]{1,2,0:T(8,128)(2,1)S(1)}, u32[]{:S(2)}, u32[]{:S(2)}) collective-permute-start(bf16[4,256,256]{1,2,0:T(8,128)(2,1)S(1)} %pad_maximum_fusion.5), channel_id=1, source_target_pairs={{0,1},{1,0},{2,3},{3,2},{4,5},{5,4},{6,7},{7,6},{8,9},{9,8},{10,11... | collective-permute-start | bytes 1572872 | tf_op jit(solution)/shard_map/ppermute | solution.py:64
  151.3 41.1 %collective-permute-start.8 = (bf16[8,56,1216]{2,1,0:T(8,128)(2,1)S(1)}, bf16[8,56,1216]{2,1,0:T(8,128)(2,1)}, u32[]{:S(2)}, u32[]{:S(2)}) collective-permute-start(bf16[8,56,1216]{2,1,0:T(8,128)(2,1)S(1)} %all-to-all-done.2), channel_id=1, source_target_pairs={{0,8},{8,0},{16,24},{24,16},{1,9},{9,1},{17,25},{25,17},{2,10},{10... | collective-permute-start | bytes 3268616 | tf_op jit(solution)/shard_map/ppermute | solution.py:64
  180.6 5.9 collective-permute-start.4
  184.0 5.5 collective-permute-start.5
  184.4 6.1 collective-permute-start.6
  190.5 6.1 collective-permute-start.7
  199.7 6.1 collective-permute-start.9
  205.9 6.4 collective-permute-start.12
  208.0 6.5 collective-permute-start.11
  208.2 6.3 collective-permute-start.10
  216.2 5.0 collective-permute-start.13
  216.3 5.1 collective-permute-start.14
  218.7 6.0 collective-permute-start.15
  224.8 6.1 collective-permute-start.16
  231.6 8.5 %collective-permute-start.17 = (bf16[8,32,896]{2,1,0:T(8,128)(2,1)S(1)}, bf16[8,32,896]{2,1,0:T(8,128)(2,1)S(1)}, u32[]{:S(2)}, u32[]{:S(2)}) collective-permute-start(bf16[8,32,896]{2,1,0:T(8,128)(2,1)S(1)} %get-tuple-element.138), channel_id=1, source_target_pairs={{0,16},{8,24},{16,0},{24,8},{1,17},{9,25},{17,1},{25,9},{2,18},{10... | collective-permute-start | bytes 1376264 | tf_op jit(solution)/shard_map/ppermute | solution.py:64
  275.8 8.1 %collective-permute-start.19 = (f32[16,32,1]{1,2,0:T(1,128)S(1)}, f32[16,32,1]{1,2,0:T(1,128)S(1)}, u32[]{:S(2)}, u32[]{:S(2)}) collective-permute-start(f32[16,32,1]{1,2,0:T(1,128)S(1)} %bitcast.468), channel_id=1, source_target_pairs={{0,8},{8,0},{16,24},{24,16},{1,9},{9,1},{17,25},{25,17},{2,10},{10... | collective-permute-start | bytes 6152 | tf_op jit(solution)/shard_map/ppermute | solution.py:64
  278.4 175.9 %all-to-all-start.4 = ((bf16[8,32,112]{2,1,0:T(8,128)(2,1)}), bf16[8,32,112]{2,1,0:T(8,128)(2,1)}, u32[]{:S(2)}, u32[]{:S(2)}) async-start(bf16[8,32,112]{2,1,0:T(8,128)(2,1)} %bitcast.381), calls=%async_computation.4 | async-start | bytes 131072 | tf_op jit(solution)/shard_map/all_to_all | solution.py:94
  284.0 21.2 %collective-permute-start.20 = (f32[8,32,1]{1,2,0:T(1,128)S(1)}, f32[8,32,1]{1,2,0:T(1,128)S(1)}, u32[]{:S(2)}, u32[]{:S(2)}) collective-permute-start(f32[8,32,1]{1,2,0:T(1,128)S(1)} %slice.414), channel_id=1, source_target_pairs={{0,16},{8,24},{16,0},{24,8},{1,17},{9,25},{17,1},{25,9},{2,18},{10... | collective-permute-start | bytes 3080 | tf_op jit(solution)/shard_map/ppermute | solution.py:64
  308.9 20.2 %collective-permute-start.31 = (bf16[16,32,896]{2,1,0:T(8,128)(2,1)S(1)}, bf16[16,32,896]{2,1,0:T(8,128)(2,1)S(1)}, u32[]{:S(2)}, u32[]{:S(2)}) collective-permute-start(bf16[16,32,896]{2,1,0:T(8,128)(2,1)S(1)} %bitcast.419), channel_id=1, source_target_pairs={{0,8},{8,0},{16,24},{24,16},{1,9},{9,1},{17,25},{25,17},{2,10},{10... | collective-permute-start | bytes 2752520 | tf_op jit(solution)/shard_map/ppermute | solution.py:64
  309.6 5.3 collective-permute-start.24
  313.3 4.4 collective-permute-start.22
  320.1 4.5 collective-permute-start.25
  320.2 4.5 collective-permute-start.26
  322.3 5.4 collective-permute-start.27
  329.7 8.7 %collective-permute-start.32 = (bf16[8,32,896]{2,1,0:T(8,128)(2,1)S(1)}, bf16[8,32,896]{2,1,0:T(8,128)(2,1)S(1)}, u32[]{:S(2)}, u32[]{:S(2)}) collective-permute-start(bf16[8,32,896]{2,1,0:T(8,128)(2,1)S(1)} %slice.427), channel_id=1, source_target_pairs={{0,16},{8,24},{16,0},{24,8},{1,17},{9,25},{17,1},{25,9},{2,18},{10... | collective-permute-start | bytes 1376264 | tf_op jit(solution)/shard_map/ppermute | solution.py:64
  331.3 7.1 collective-permute-start.29
  338.8 8.2 %collective-permute-start.33 = (bf16[4,32,896]{2,1,0:T(8,128)(2,1)S(1)}, bf16[4,32,896]{2,1,0:T(8,128)(2,1)}, u32[]{:S(2)}, u32[]{:S(2)}) collective-permute-start(bf16[4,32,896]{2,1,0:T(8,128)(2,1)S(1)} %slice.429), channel_id=1, source_target_pairs={{0,1},{1,0},{2,3},{3,2},{4,5},{5,4},{6,7},{7,6},{8,9},{9,8},{10,11... | collective-permute-start | bytes 688136 | tf_op jit(solution)/shard_map/ppermute | solution.py:64
  348.1 6.1 collective-permute-start.36
  350.4 5.5 collective-permute-start.35
  350.4 5.5 collective-permute-start.34
  358.8 23.1 %collective-permute-start.37 = (bf16[1,32,896]{2,1,0:T(8,128)(2,1)S(1)}, bf16[1,32,896]{2,1,0:T(8,128)(2,1)S(1)}, u32[]{:S(2)}, u32[]{:S(2)}) collective-permute-start(bf16[1,32,896]{2,1,0:T(8,128)(2,1)S(1)} %get-tuple-element.66), channel_id=1, source_target_pairs={{0,2},{1,3},{2,0},{3,1},{4,6},{5,7},{6,4},{7,5},{8,10},{9,11},{10,... | collective-permute-start | bytes 172040 | tf_op jit(solution)/shard_map/ppermute | solution.py:64
  359.6 22.3 %collective-permute-start.38 = (bf16[1,32,896]{2,1,0:T(8,128)(2,1)S(1)}, bf16[1,32,896]{2,1,0:T(8,128)(2,1)S(1)}, u32[]{:S(2)}, u32[]{:S(2)}) collective-permute-start(bf16[1,32,896]{2,1,0:T(8,128)(2,1)S(1)} %get-tuple-element.66), channel_id=1, source_target_pairs={{0,4},{1,5},{2,6},{3,7},{4,0},{5,1},{6,2},{7,3},{8,12},{9,13},{10,... | collective-permute-start | bytes 172040 | tf_op jit(solution)/shard_map/ppermute | solution.py:64
  361.7 20.2 %collective-permute-start.39 = (bf16[1,32,896]{2,1,0:T(8,128)(2,1)S(1)}, bf16[1,32,896]{2,1,0:T(8,128)(2,1)S(1)}, u32[]{:S(2)}, u32[]{:S(2)}) collective-permute-start(bf16[1,32,896]{2,1,0:T(8,128)(2,1)S(1)} %get-tuple-element.66), channel_id=1, source_target_pairs={{0,6},{1,7},{2,4},{3,5},{4,2},{5,3},{6,0},{7,1},{8,14},{9,15},{10,... | collective-permute-start | bytes 172040 | tf_op jit(solution)/shard_map/ppermute | solution.py:64
  382.0 6.6 collective-permute-start.40
  393.4 6.3 collective-permute-start.41
  399.1 71.5 %collective-permute-start.53 = (bf16[2,224,1216]{2,1,0:T(8,128)(2,1)}, bf16[2,224,1216]{2,1,0:T(8,128)(2,1)}, u32[]{:S(2)}, u32[]{:S(2)}) collective-permute-start(bf16[2,224,1216]{2,1,0:T(8,128)(2,1)} %select_bitcast_fusion.2), channel_id=1, source_target_pairs={{0,8},{8,0},{16,24},{24,16},{1,9},{9,1},{17,25},{25,17},{2,10},{10... | collective-permute-start | bytes 3268616 | tf_op jit(solution)/shard_map/ppermute | solution.py:64
  400.9 6.6 collective-permute-start.44
  403.2 6.3 collective-permute-start.43
  403.2 6.3 collective-permute-start.42
  406.2 26.1 %collective-permute-start.57 = (bf16[2,152,896]{2,1,0:T(8,128)(2,1)}, bf16[2,152,896]{2,1,0:T(8,128)(2,1)}, u32[]{:S(2)}, u32[]{:S(2)}) collective-permute-start(bf16[2,152,896]{2,1,0:T(8,128)(2,1)} %fusion.42), channel_id=1, source_target_pairs={{0,8},{8,0},{16,24},{24,16},{1,9},{9,1},{17,25},{25,17},{2,10},{10... | collective-permute-start | bytes 1634312 | tf_op jit(solution)/shard_map/ppermute | solution.py:64
  424.2 14.2 %collective-permute-start.45 = (bf16[4,256,256]{1,2,0:T(8,128)(2,1)}, bf16[4,256,256]{1,2,0:T(8,128)(2,1)}, u32[]{:S(2)}, u32[]{:S(2)}) collective-permute-start(bf16[4,256,256]{1,2,0:T(8,128)(2,1)} %bitcast.379), channel_id=1, source_target_pairs={{0,1},{1,0},{2,3},{3,2},{4,5},{5,4},{6,7},{7,6},{8,9},{9,8},{10,11... | collective-permute-start | bytes 1572872 | tf_op jit(solution)/shard_map/ppermute | solution.py:64
  439.7 8.3 %collective-permute-start.48 = (bf16[1,256,256]{1,2,0:T(8,128)(2,1)S(1)}, bf16[1,256,256]{1,2,0:T(8,128)(2,1)S(1)}, u32[]{:S(2)}, u32[]{:S(2)}) collective-permute-start(bf16[1,256,256]{1,2,0:T(8,128)(2,1)S(1)} %get-tuple-element.114), channel_id=1, source_target_pairs={{0,6},{1,7},{2,4},{3,5},{4,2},{5,3},{6,0},{7,1},{8,14},{9,15},{10,... | collective-permute-start | bytes 393224 | tf_op jit(solution)/shard_map/ppermute | solution.py:64
  442.1 10.7 %collective-permute-start.47 = (bf16[1,256,256]{1,2,0:T(8,128)(2,1)S(1)}, bf16[1,256,256]{1,2,0:T(8,128)(2,1)S(1)}, u32[]{:S(2)}, u32[]{:S(2)}) collective-permute-start(bf16[1,256,256]{1,2,0:T(8,128)(2,1)S(1)} %get-tuple-element.115), channel_id=1, source_target_pairs={{0,4},{1,5},{2,6},{3,7},{4,0},{5,1},{6,2},{7,3},{8,12},{9,13},{10,... | collective-permute-start | bytes 393224 | tf_op jit(solution)/shard_map/ppermute | solution.py:64
  442.1 10.7 %collective-permute-start.46 = (bf16[1,256,256]{1,2,0:T(8,128)(2,1)S(1)}, bf16[1,256,256]{1,2,0:T(8,128)(2,1)S(1)}, u32[]{:S(2)}, u32[]{:S(2)}) collective-permute-start(bf16[1,256,256]{1,2,0:T(8,128)(2,1)S(1)} %get-tuple-element.113), channel_id=1, source_target_pairs={{0,2},{1,3},{2,0},{3,1},{4,6},{5,7},{6,4},{7,5},{8,10},{9,11},{10,... | collective-permute-start | bytes 393224 | tf_op jit(solution)/shard_map/ppermute | solution.py:64
  444.9 75.5 %collective-permute-start.58 = (bf16[152,896]{1,0:T(8,128)(2,1)}, bf16[152,896]{1,0:T(8,128)(2,1)}, u32[]{:S(2)}, u32[]{:S(2)}) collective-permute-start(bf16[152,896]{1,0:T(8,128)(2,1)} %select_bitcast_fusion.12), channel_id=1, source_target_pairs={{0,16},{8,24},{16,0},{24,8},{1,17},{9,25},{17,1},{25,9},{2,18},{10... | collective-permute-start | bytes 817160 | tf_op jit(solution)/shard_map/ppermute | solution.py:64
  454.3 10.2 %all-to-all-start.7 = ((bf16[8,32,112]{2,1,0:T(8,128)(2,1)}), bf16[8,32,112]{2,1,0:T(8,128)(2,1)S(1)}, u32[]{:S(2)}, u32[]{:S(2)}) async-start(bf16[8,32,112]{2,1,0:T(8,128)(2,1)} %bitcast.380), calls=%async_computation.7 | async-start | bytes 131072 | tf_op jit(solution)/shard_map/all_to_all | solution.py:94
  465.3 15.9 %all-to-all-start.8 = ((bf16[8,32,896]{2,1,0:T(8,128)(2,1)}), bf16[8,32,896]{2,1,0:T(8,128)(2,1)}, u32[]{:S(2)}, u32[]{:S(2)}) async-start(bf16[8,32,896]{2,1,0:T(8,128)(2,1)} %broadcast_in_dim.74), calls=%async_computation.8 | async-start | bytes 917504 | tf_op jit(solution)/shard_map/all_to_all | solution.py:94
  482.8 16.2 %all-to-all-start.5 = ((bf16[8,32,896]{2,1,0:T(8,128)(2,1)}), bf16[8,32,896]{2,1,0:T(8,128)(2,1)S(1)}, u32[]{:S(2)}, u32[]{:S(2)}) async-start(bf16[8,32,896]{2,1,0:T(8,128)(2,1)} %broadcast_in_dim.73), calls=%async_computation.5 | async-start | bytes 917504 | tf_op jit(solution)/shard_map/all_to_all | solution.py:94
  487.4 16.0 %collective-permute-start.54 = (bf16[224,1216]{1,0:T(8,128)(2,1)}, bf16[224,1216]{1,0:T(8,128)(2,1)}, u32[]{:S(2)}, u32[]{:S(2)}) collective-permute-start(bf16[224,1216]{1,0:T(8,128)(2,1)} %select_bitcast_fusion.7), channel_id=1, source_target_pairs={{0,16},{8,24},{16,0},{24,8},{1,17},{9,25},{17,1},{25,9},{2,18},{10... | collective-permute-start | bytes 1634312 | tf_op jit(solution)/shard_map/ppermute | solution.py:64
  499.8 16.1 %all-to-all-start.6 = ((bf16[8,112,256]{2,1,0:T(8,128)(2,1)}), bf16[8,112,256]{2,1,0:T(8,128)(2,1)S(1)}, u32[]{:S(2)}, u32[]{:S(2)}) async-start(bf16[8,112,256]{2,1,0:T(8,128)(2,1)} %bitcast.433), calls=%async_computation.6 | async-start | bytes 917504 | tf_op jit(solution)/shard_map/all_to_all | solution.py:94
  504.7 14.8 %collective-permute-start.55 = (bf16[224,1216]{1,0:T(8,128)(2,1)S(1)}, bf16[224,1216]{1,0:T(8,128)(2,1)S(1)}, u32[]{:S(2)}, u32[]{:S(2)}) collective-permute-start(bf16[224,1216]{1,0:T(8,128)(2,1)S(1)} %fusion.33), channel_id=1, source_target_pairs={{0,16},{8,24},{16,0},{24,8},{1,17},{9,25},{17,1},{25,9},{2,18},{10... | collective-permute-start | bytes 1634312 | tf_op jit(solution)/shard_map/ppermute | solution.py:64
  515.9 28.2 %all-to-all-start.3 = ((bf16[32,16,896]{2,1,0:T(8,128)(2,1)}), bf16[32,16,896]{2,1,0:T(8,128)(2,1)S(1)}, u32[]{:S(2)}, u32[]{:S(2)}) async-start(bf16[32,16,896]{2,1,0:T(8,128)(2,1)} %bitcast.93), calls=%async_computation.3 | async-start | bytes 1835008 | tf_op jit(solution)/shard_map/all_to_all | solution.py:94
  521.6 27.7 %collective-permute-start.59 = (bf16[152,896]{1,0:T(8,128)(2,1)S(1)}, bf16[152,896]{1,0:T(8,128)(2,1)S(1)}, u32[]{:S(2)}, u32[]{:S(2)}) collective-permute-start(bf16[152,896]{1,0:T(8,128)(2,1)S(1)} %fusion.44), channel_id=1, source_target_pairs={{0,16},{8,24},{16,0},{24,8},{1,17},{9,25},{17,1},{25,9},{2,18},{10... | collective-permute-start | bytes 817160 | tf_op jit(solution)/shard_map/ppermute | solution.py:64
  545.0 56.1 %all-to-all-start.9 = ((bf16[8,112,1216]{2,1,0:T(8,128)(2,1)}), bf16[8,112,1216]{2,1,0:T(8,128)(2,1)S(1)}, u32[]{:S(2)}, u32[]{:S(2)}) async-start(bf16[8,112,1216]{2,1,0:T(8,128)(2,1)} %bitcast.398), calls=%async_computation.9 | async-start | bytes 4587520 | tf_op jit(solution)/shard_map/all_to_all | solution.py:94
  548.7 5.1 collective-permute-start.50
  553.9 5.0 collective-permute-start.51
  (120 other events, 1728.8 us)
Sparse Core Ops, SparseCore 0:
  10.8 61.2 all-gather.2
  74.8 60.6 all-gather.4

commit v2 on v1

v2 whole, which is shorter than its diff:
```python
import functools

import jax
import jax.numpy as jnp
from jax import lax
from jax.experimental import pallas as pl
from jax.experimental.pallas import tpu as pltpu
from jax.sharding import PartitionSpec as P

H = 14
KV = 2
HD = 64
FF = 4864
STEP = 5


NORM_EPS = 1e-06
ROPE_BASE = 1000000.0
NEG_BIG = -1e30
EPS_LOW = 0.8
EPS_HIGH = 0.28
BETA_KL = 0.1
CLIP_NORM = 0.05
BETA_ONE = 0.9
BETA_TWO = 0.95
ADAM_EPS = 1e-08
DECAY = 0.1
LR_MATRIX = 0.02
LR_OUT = 0.12
LR_GAIN = 1.0
LR_BIAS = 0.5


def norm_rows(values, gain):
    return values * lax.rsqrt(jnp.mean(values * values, axis=-1, keepdims=True) + NORM_EPS) * gain


def partner(value, axis, mask):
    size = lax.axis_size(axis)
    return lax.ppermute(value, axis, [(place, place ^ mask) for place in range(size)])


def masks_of(size):
    masks, mask = [], 1
    while mask < size:
        masks.append(mask)
        mask *= 2
    return masks


def bit_of(axis, mask):
    return (lax.axis_index(axis) & mask) != 0


def xor_order(blocks, axis):
    bits = masks_of(blocks.shape[0])
    held = blocks.reshape((2,) * len(bits) + blocks.shape[1:])
    for at, bit in enumerate(reversed(bits)):
        held = jnp.where(bit_of(axis, bit), jnp.flip(held, at), held)
    return held.reshape(blocks.shape)


def after(value, *first):
    return lax.optimization_barrier((value, first))[0]


def together(*values):
    return lax.optimization_barrier(values)


def seq_stages_of(size):
    bits = masks_of(size)
    stages, rest = [], bits[1:]
    while rest:
        pair, rest = rest[:2], rest[2:]
        stages.append([pair[0], pair[1], pair[0] ^ pair[1]] if len(pair) == 2 else pair)
    return stages + [bits[:1]]


def spread(value, axis, stages):
    held = value[None]
    for masks in stages:
        held = jnp.concatenate([held] + [partner(held, axis, mask) for mask in masks])
    return held


def to_xor_order(blocks, axis, stages):
    bits = masks_of(blocks.shape[0])
    turned = xor_order(blocks, axis).reshape((2,) * len(bits) + blocks.shape[1:])
    place = {bit: at for at, bit in enumerate(reversed(bits))}
    order = [place[mask] for masks in reversed(stages) for mask in reversed(masks) if mask in bits]
    rest = list(range(len(bits), turned.ndim))
    return jnp.transpose(turned, order + rest).reshape(blocks.shape)


def to_index_order(blocks, axis, stages):
    bits = masks_of(blocks.shape[0])
    place = {bit: at for at, bit in enumerate(reversed(bits))}
    order = [place[mask] for masks in reversed(stages) for mask in reversed(masks) if mask in bits]
    back = [order.index(at) for at in range(len(bits))]
    held = blocks.reshape((2,) * len(bits) + blocks.shape[1:])
    held = jnp.transpose(held, back + list(range(len(bits), held.ndim)))
    return xor_order(held.reshape(blocks.shape), axis)


def exchange(value, axes):
    return lax.all_to_all(value, axes, split_axis=0, concat_axis=0, tiled=True)


def exchange_copies(value, axes):
    size = lax.axis_size(axes)
    return exchange(jnp.broadcast_to(value[None], (size,) + value.shape), axes)


def total_of(parts):
    total = parts[0].astype(jnp.float32)
    for part in parts[1:]:
        total = total + part.astype(jnp.float32)
    return total.astype(jnp.bfloat16)


def cut(first, second, axis, mask):
    own = bit_of(axis, mask)
    return jnp.where(own, second, first), partner(jnp.where(own, first, second), axis, mask)


def halve(first, second, axis, mask):
    return total_of(cut(first, second, axis, mask))


def double(value, axis, mask):
    own = bit_of(axis, mask)
    other = partner(value, axis, mask)
    return jnp.where(own, other, value), jnp.where(own, value, other)


def all_sum(value):
    for axis in ("batch", "seq"):
        for mask in masks_of(lax.axis_size(axis)):
            value = value + partner(value, axis, mask)
    return value


def sum_seq(blocks):
    held = blocks
    for mask in reversed(masks_of(blocks.shape[0])):
        half = held.shape[0] // 2
        held = halve(held[:half], held[half:], "seq", mask)
    return held[0]


def dot_nn(left, right):
    return jnp.dot(left, right, preferred_element_type=jnp.float32)


def dot_tn(left, right):
    return lax.dot_general(
        left, right, (((0,), (0,)), ((), ())), preferred_element_type=jnp.float32
    )


def dot_nt(left, right):
    return lax.dot_general(
        left, right, (((1,), (1,)), ((), ())), preferred_element_type=jnp.float32
    )


def squares_of(value):
    value = value.astype(jnp.float32)
    return jnp.sum(value * value)


def adam(weight, moment, second, gradient, learn_rate, decay_rate):
    moment = BETA_ONE * moment + (1.0 - BETA_ONE) * gradient
    second = BETA_TWO * second + (1.0 - BETA_TWO) * gradient * gradient
    corrected = moment / (1.0 - BETA_ONE**STEP)
    scaled = second / (1.0 - BETA_TWO**STEP)
    return (
        weight - learn_rate * (corrected / (jnp.sqrt(scaled) + ADAM_EPS) + decay_rate * weight),
        moment,
        second,
    )


LOW = jnp.bfloat16
F32 = jnp.float32
LANES = 128


def iota(shape, dim):
    return lax.broadcasted_iota(jnp.int32, shape, dim)


def in_hbm(*arrays):
    return tuple(pltpu.with_memory_space_constraint(array, pltpu.HBM) for array in arrays)


def like(shape, dtype=jnp.float32):
    return jax.ShapeDtypeStruct(shape, dtype)


def in_vmem(body, outs, args, name, flops=0, exps=0, limit=16, kept=(), scratch=()):
    moved = sum(a.size * a.dtype.itemsize for a in args) + sum(
        o.size * o.dtype.itemsize for o in outs
    )
    whole = lambda rank: lambda step: (0,) * rank
    near = pl.BlockSpec(memory_space=pltpu.VMEM)
    return pl.pallas_call(
        body,
        grid=(1,),
        in_specs=[
            pl.BlockSpec(a.shape, whole(a.ndim)) if at in kept else near
            for at, a in enumerate(args)
        ],
        out_specs=[near] * len(outs),
        out_shape=outs,
        scratch_shapes=scratch,
        compiler_params=pltpu.CompilerParams(vmem_limit_bytes=limit * 2**20),
        cost_estimate=pl.CostEstimate(flops=flops, bytes_accessed=moved, transcendentals=exps),
        name=name,
    )(*[in_hbm(a)[0] if at in kept else a for at, a in enumerate(args)])


def upright(row):
    count = row.shape[1]
    square = jnp.broadcast_to(row.astype(F32), (count, count))
    return jnp.sum(
        jnp.where(iota((count, count), 0) == iota((count, count), 1), square, 0.0),
        axis=1,
        keepdims=True,
    )


def turned(values, cosine, sine):
    tiles = []
    for at in range(0, values.shape[1], LANES):
        tile = values[:, at : at + LANES]
        front = iota(tile.shape, 1) % HD < HD // 2
        swapped = jnp.where(
            front, pltpu.roll(tile, LANES - HD // 2, 1), pltpu.roll(tile, HD // 2, 1)
        )
        tiles.append(tile * cosine + swapped * sine)
    return tiles[0] if len(tiles) == 1 else jnp.concatenate(tiles, axis=1)


def norm_back(values, gain, grad):
    inverse = lax.rsqrt(jnp.mean(values * values, axis=-1, keepdims=True) + NORM_EPS)
    scaled = grad * gain
    inner = jnp.mean(values * scaled, axis=-1, keepdims=True)
    into = inverse * scaled - values * (inverse * inverse * inverse * inner)
    return into, jnp.sum(grad * values * inverse, axis=0, keepdims=True)


def placed(pick_columns, values):
    high = values.astype(LOW)
    rest = (values - high.astype(F32)).astype(LOW)
    return dot_nn(pick_columns, high) + dot_nn(pick_columns, rest)


def coded(value):
    high = value.astype(LOW).astype(F32)
    middle = (value - high).astype(LOW).astype(F32)
    return high, middle, (value - high - middle).astype(LOW).astype(F32)


def coded_lanes(columns):
    parts = [part for column in columns for part in coded(column)]
    lane = iota((columns[0].shape[0], LANES), 1)
    tail = jnp.zeros(lane.shape, F32)
    for at, part in enumerate(parts):
        tail = jnp.where(lane == at, part, tail)
    return tail.astype(LOW)


def decoded(tail, at):
    tail = tail.astype(F32)
    lane = iota(tail.shape, tail.ndim - 1)
    return jnp.sum(
        jnp.where((lane >= 3 * at) & (lane < 3 * at + 3), tail, 0.0), axis=-1, keepdims=True
    )


def request_body(vrows, capacity, tokens_ref, requests_ref, placer_ref):
    row = tokens_ref[...].astype(F32)
    column = upright(tokens_ref[...])
    count = row.shape[1]
    owner_row = jnp.floor((row + 0.5) / vrows)
    owner = jnp.floor((column + 0.5) / vrows)
    earlier = (owner == owner_row) & (iota((count, count), 1) < iota((count, count), 0))
    slot = jnp.sum(jnp.where(earlier, 1.0, 0.0), axis=1, keepdims=True)
    hit = (owner * capacity + slot) == iota(placer_ref.shape, 1).astype(F32)
    placer_ref[...] = jnp.where(hit, 1.0, 0.0).astype(LOW)
    requests_ref[...] = jnp.sum(
        jnp.where(hit, column - owner * vrows, 0.0), axis=0, keepdims=True
    ).astype(jnp.int32)


def embed_body(
    rows_ref, placer_ref, w_ref, bias_ref, gain_ref, cos_ref, sin_ref, x_ref, normed_ref, kv_ref
):
    x_zero = dot_nn(placer_ref[...], rows_ref[...])
    x_ref[...] = x_zero.astype(LOW)
    normed = norm_rows(x_zero, gain_ref[...]).astype(LOW)
    normed_ref[...] = normed
    kv = dot_nn(normed, w_ref[...]) + bias_ref[...]
    width = KV * HD
    keys = turned(kv[:, :width], cos_ref[...], sin_ref[...]).astype(LOW)
    values = kv[:, width:].astype(LOW)
    for at in range(kv_ref.shape[0]):
        kv_ref[at, :, :width] = keys
        kv_ref[at, :, width:] = values


def pick_columns_of(picks, slots, shift):
    return jnp.where(
        iota((slots, picks.shape[1]), 0) == picks + shift, 1.0, 0.0
    ).astype(LOW)


def pick_body(
    x_ref, normed_ref, picks_ref, w_ref, bias_ref, cos_ref, sin_ref,
    picked_ref, target_ref, picked_normed_ref, query_ref,
):
    slots = x_ref.shape[0]
    here = pick_columns_of(picks_ref[...], slots, 0)
    after = pick_columns_of(picks_ref[...], slots, 1)
    picked_ref[...] = dot_tn(here, x_ref[...])
    target_ref[...] = dot_tn(after, x_ref[...])
    normed = dot_tn(here, normed_ref[...]).astype(LOW)
    picked_normed_ref[...] = normed
    query = dot_nn(normed, w_ref[...]) + bias_ref[...]
    query_ref[...] = turned(query, cos_ref[...], sin_ref[...]).astype(LOW)


def stacked_heads(values, first, count):
    return jnp.concatenate(
        [values[:, (first + at) * HD : (first + at + 1) * HD] for at in range(count)], axis=0
    )


CHUNK = 2048


def scores_of(queries, keys, places, count, start):
    scores = dot_nt(queries, keys) * HD ** (-0.5)
    reach = jnp.concatenate([places] * count, axis=0) - start
    return jnp.where(iota(scores.shape, 1) <= reach, scores, NEG_BIG)


def key_slices(kv_ref, head, start, size):
    rows = pl.ds(start, size)
    return (
        kv_ref[rows, head * HD : (head + 1) * HD],
        kv_ref[rows, (KV + head) * HD : (KV + head + 1) * HD],
    )


def over_keys(length, body, carry):
    if length <= CHUNK:
        return body(0, carry)
    return lax.fori_loop(
        0, length // CHUNK, lambda at, held: body(pl.multiple_of(at * CHUNK, CHUNK), held), carry
    )


def softmax_parts(queries, kv_ref, head, places, count):
    length = kv_ref.shape[0]
    size = min(length, CHUNK)
    if length <= CHUNK:

        def chances(start):
            scores = scores_of(queries, key_slices(kv_ref, head, 0, size)[0], places, count, 0)
            raised = jnp.exp(scores - jnp.max(scores, axis=1, keepdims=True))
            return raised * (1.0 / jnp.sum(raised, axis=1, keepdims=True))

        return chances

    def statistics(start, held):
        top, summed = held
        keys = key_slices(kv_ref, head, start, size)[0]
        scores = scores_of(queries, keys, places, count, start)
        now = jnp.maximum(top, jnp.max(scores, axis=1, keepdims=True))
        raised = jnp.exp(scores - now)
        return now, summed * jnp.exp(top - now) + jnp.sum(raised, axis=1, keepdims=True)

    rows = queries.shape[0]
    top, summed = over_keys(
        length, statistics, (jnp.full((rows, 1), NEG_BIG, F32), jnp.zeros((rows, 1), F32))
    )

    def chances_at(start):
        keys = key_slices(kv_ref, head, start, size)[0]
        return jnp.exp(scores_of(queries, keys, places, count, start) - top) * (1.0 / summed)

    return chances_at


def attend_body(
    query_ref, kv_ref, place_ref, w_ref, picked_ref, gain_ref,
    mixed_ref, attended_ref, one_ref, normed_ref,
):
    places = upright(place_ref[...]).astype(jnp.int32)
    picks = places.shape[0]
    group = H // KV
    length = kv_ref.shape[0]
    size = min(length, CHUNK)
    for head in range(KV):
        queries = stacked_heads(query_ref[...], head * group, group)
        chances = softmax_parts(queries, kv_ref, head, places, group)

        def add(start, total):
            values = key_slices(kv_ref, head, start, size)[1]
            return total + dot_nn(chances(start).astype(LOW), values)

        out = over_keys(length, add, jnp.zeros(queries.shape, F32))
        for at in range(group):
            spot = (head * group + at) * HD
            attended_ref[:, spot : spot + HD] = out[at * picks : (at + 1) * picks]
    mixed = attended_ref[...].astype(LOW)
    mixed_ref[...] = mixed
    one = picked_ref[...] + dot_nn(mixed, w_ref[...])
    one_ref[...] = one
    normed = norm_rows(one, gain_ref[...]).astype(LOW)
    for at in range(normed_ref.shape[0]):
        normed_ref[at] = normed


def feed_body(normed_ref, gate_w_ref, up_w_ref, down_w_ref, gate_ref, up_ref, hidden_ref, out_ref):
    normed = normed_ref[...]
    gate = dot_nn(normed, gate_w_ref[...])
    up = dot_nn(normed, up_w_ref[...])
    gate_ref[...] = gate
    up_ref[...] = up
    hidden = (gate * (1.0 / (1.0 + jnp.exp(-gate))) * up).astype(LOW)
    hidden_ref[...] = hidden
    out_ref[...] = dot_nn(hidden, down_w_ref[...]).astype(LOW)


def feed_sum_body(parts_ref, one_ref, gain_ref, two_ref, final_ref):
    two = one_ref[...] + jnp.sum(parts_ref[...].astype(F32), axis=0)
    two_ref[...] = two
    final_ref[...] = norm_rows(two, gain_ref[...]).astype(LOW)


def head_body(
    vrows, rows_ref, other_ref, table_ref, raised_ref, tops_ref, own_ref, send_ref, top, summed, total
):
    step = pl.program_id(0)
    block = table_ref.shape[0]
    width = table_ref.shape[1]
    half = own_ref.shape[0]

    @pl.when(step == 0)
    def _():
        top[...] = jnp.full(top.shape, NEG_BIG, F32)
        summed[...] = jnp.zeros(summed.shape, F32)
        total[...] = jnp.zeros(total.shape, F32)

    left = vrows - step * block
    entries = jnp.where(iota((block, 1), 0) < left, table_ref[...], 0.0).astype(LOW)
    inside = iota((1, block), 1) < left
    part = min(256, half)
    pieces = []
    for ref, start in ((rows_ref, 0), (other_ref, half)):
        tokens = ref[...].reshape(half, width)
        pieces += [
            (slice(start + at, start + at + part), tokens[at : at + part])
            for at in range(0, half, part)
        ]
    logits_of = [dot_nt(tokens, entries) for _, tokens in pieces]
    for (piece, _), logits in zip(pieces, logits_of):
        logits = jnp.where(inside, logits, NEG_BIG)
        before = top[piece, :1]
        now = jnp.maximum(before, jnp.max(logits, axis=1, keepdims=True))
        raised = jnp.exp(logits - now)
        shrink = jnp.exp(before - now)
        low = raised.astype(LOW)
        raised_ref[piece] = low
        summed[piece] = summed[piece] * shrink + jnp.sum(raised, axis=1, keepdims=True)
        total[piece] = total[piece] * shrink + dot_nn(low, entries)
        top[piece] = jnp.broadcast_to(now, (part, LANES))
        column = iota((part, LANES), 1) == step
        tops_ref[piece] = jnp.where(column, now, tops_ref[piece])

    @pl.when(step == pl.num_programs(0) - 1)
    def _():
        for ref, at in ((own_ref, 0), (send_ref, half)):
            here = slice(at, at + half)
            ref[:, :width] = (total[here] / summed[here, :1]).astype(LOW)
            ref[:, width:] = coded_lanes([top[here, :1] + jnp.log(summed[here, :1])])


def head_part(rows, other, group, table, block):
    seqs, _, picks, width = rows.shape
    half = seqs * picks
    vrows = table.shape[0]
    steps = -(-vrows // block)
    whole = lambda step: (0, 0)
    states = pl.BlockSpec((seqs, 1, picks, width), lambda step: (0, group, 0, 0))
    mean = pl.BlockSpec((half, width + LANES), whole)
    return pl.pallas_call(
        functools.partial(head_body, vrows),
        grid=(steps,),
        in_specs=[states, states, pl.BlockSpec((block, width), lambda step: (step, 0))],
        out_specs=[
            pl.BlockSpec((2 * half, block), lambda step: (0, step)),
            pl.BlockSpec((2 * half, LANES), whole),
            mean,
            mean,
        ],
        out_shape=[
            pltpu.HBM((2 * half, steps * block), LOW),
            like((2 * half, LANES)),
            like((half, width + LANES), LOW),
            like((half, width + LANES), LOW),
        ],
        scratch_shapes=[
            pltpu.VMEM((2 * half, LANES), F32),
            pltpu.VMEM((2 * half, LANES), F32),
            pltpu.VMEM((2 * half, width), F32),
        ],
        compiler_params=pltpu.CompilerParams(vmem_limit_bytes=(28 if half <= 256 else 60) * 2**20),
        cost_estimate=pl.CostEstimate(
            flops=8 * half * vrows * width,
            bytes_accessed=vrows * width * 4 + half * vrows * 4,
            transcendentals=2 * half * vrows,
        ),
        name="head_part",
    )(rows, other, *in_hbm(table))


def merge_values(parts):
    highest = parts[0][1]
    for _, log in parts[1:]:
        highest = jnp.maximum(highest, log)
    summed, total = 0.0, 0.0
    for mean, log in parts:
        share = jnp.exp(log - highest)
        summed = summed + share
        total = total + share * mean
    return total * (1.0 / summed), highest + jnp.log(summed)


def merge_body(*refs):
    out_ref = refs[-1]
    width = out_ref.shape[1] - LANES
    mean, log = merge_values(
        [(ref[:, :width].astype(F32), decoded(ref[:, width:], 0)) for ref in refs[:-1]]
    )
    out_ref[:, :width] = mean.astype(LOW)
    out_ref[:, width:] = coded_lanes([log])


def loss_body(
    parts_ref, final_ref, target_ref, two_ref, gain_ref, live_ref, old_ref, ref_ref, advantage_ref,
    message_ref, grad_ref, gain_grad_ref, added_ref, loss_ref,
):
    width = final_ref.shape[1]
    mean, log_total = merge_values(
        [
            (parts_ref[at, :, :width].astype(F32), decoded(parts_ref[at, :, width:], 0))
            for at in range(parts_ref.shape[0])
        ]
    )
    final = final_ref[...].astype(F32)
    target = target_ref[...]
    live = upright(live_ref[...])
    to_ref = jnp.sum(final * target, axis=1, keepdims=True) - log_total
    logp = to_ref
    to_ref = logp - upright(ref_ref[...])
    advantage = advantage_ref[...]
    weight = jnp.clip(jnp.exp(logp - upright(old_ref[...])), 1.0 - EPS_LOW, 1.0 + EPS_HIGH)
    coefficient = live * (-weight * advantage + BETA_KL * to_ref)
    loss = live * (-weight * advantage * logp + 0.5 * BETA_KL * to_ref * to_ref)
    loss_ref[...] = jnp.broadcast_to(jnp.sum(loss, axis=0, keepdims=True), loss_ref.shape)
    added_ref[...] = coefficient * final
    grad, gain_grad_ref[...] = norm_back(
        two_ref[...], gain_ref[...], coefficient * (target - mean)
    )
    grad_ref[...] = grad
    low = grad.astype(LOW)
    tail = coded_lanes([log_total, coefficient])
    for at in range(message_ref.shape[0]):
        message_ref[at, :, :width] = low
        message_ref[at, :, width:] = tail


def feed_back_body(
    message_ref, hidden_ref, gate_ref, up_ref, gate_w_ref, up_w_ref, down_w_ref,
    grad_gate_ref, grad_up_ref, out_ref,
):
    width = out_ref.shape[1]
    grad_hidden = dot_nt(message_ref[:, :width], down_w_ref[...])
    gate = gate_ref[...]
    up = up_ref[...]
    sigmoid = 1.0 / (1.0 + jnp.exp(-gate))
    grad_gate = (grad_hidden * up * sigmoid * (1.0 + gate * (1.0 - sigmoid))).astype(LOW)
    grad_up = (grad_hidden * gate * sigmoid).astype(LOW)
    grad_gate_ref[...] = grad_gate
    grad_up_ref[...] = grad_up
    out_ref[...] = (
        dot_nt(grad_gate, gate_w_ref[...]) + dot_nt(grad_up, up_w_ref[...])
    ).astype(LOW)


def one_back_body(parts_ref, one_ref, grad_two_ref, gain_ref, grad_ref, low_ref, gain_grad_ref):
    into, gain_grad_ref[...] = norm_back(
        one_ref[...], gain_ref[...], jnp.sum(parts_ref[...].astype(F32), axis=0)
    )
    grad = grad_two_ref[...] + into
    grad_ref[...] = grad
    low_ref[...] = grad.astype(LOW)


def attend_back_body(
    grad_ref, w_ref, query_ref, kv_ref, place_ref, attended_ref, cos_ref, sin_ref,
    kv_grad_ref, query_pre_ref, bias_ref, query_grad,
):
    places = upright(place_ref[...]).astype(jnp.int32)
    picks = places.shape[0]
    into = dot_nt(grad_ref[...], w_ref[...]).astype(LOW)
    group = H // KV
    length = kv_ref.shape[0]
    size = min(length, CHUNK)
    for head in range(KV):
        queries = stacked_heads(query_ref[...], head * group, group)
        grads = stacked_heads(into, head * group, group)
        inner = jnp.sum(
            grads.astype(F32) * stacked_heads(attended_ref[...], head * group, group),
            axis=1,
            keepdims=True,
        )
        chances = softmax_parts(queries, kv_ref, head, places, group)

        def add(start, total):
            keys, values = key_slices(kv_ref, head, start, size)
            chance = chances(start)
            scores = (chance * (dot_nt(grads, values) - inner)).astype(LOW)
            rows = pl.ds(start, size)
            kv_grad_ref[rows, head * HD : (head + 1) * HD] = (
                dot_tn(scores, queries) * HD ** (-0.5)
            ).astype(LOW)
            kv_grad_ref[rows, (KV + head) * HD : (KV + head + 1) * HD] = dot_tn(
                chance.astype(LOW), grads
            ).astype(LOW)
            return total + dot_nn(scores, keys) * HD ** (-0.5)

        query_part = over_keys(length, add, jnp.zeros(queries.shape, F32))
        for at in range(group):
            spot = (head * group + at) * HD
            query_grad[:, spot : spot + HD] = query_part[at * picks : (at + 1) * picks]
    query_pre = turned(query_grad[...], cos_ref[...], -sin_ref[...]).astype(LOW)
    query_pre_ref[...] = query_pre
    bias_ref[...] = jnp.sum(query_pre.astype(F32), axis=0, keepdims=True)


def zero_back_body(
    parts_ref, cos_ref, sin_ref, kv_w_ref, query_pre_ref, q_w_ref, picks_ref, x_ref, gain_ref,
    grad_one_ref, added_ref, placer_ref,
    kv_pre_ref, back_ref, gain_grad_ref, bias_ref,
):
    width = KV * HD
    slots = x_ref.shape[0]
    own = jnp.sum(parts_ref[...].astype(F32), axis=0)
    kv_pre_ref[:, :width] = turned(own[:, :width], cos_ref[...], -sin_ref[...]).astype(LOW)
    kv_pre_ref[:, width:] = own[:, width:].astype(LOW)
    kv_pre = kv_pre_ref[...]
    bias_ref[...] = jnp.sum(kv_pre.astype(F32), axis=0, keepdims=True)
    here = pick_columns_of(picks_ref[...], slots, 0)
    after = pick_columns_of(picks_ref[...], slots, 1)
    grad_normed = dot_nt(kv_pre, kv_w_ref[...]) + placed(
        here, dot_nt(query_pre_ref[...], q_w_ref[...])
    )
    into, gain_grad_ref[...] = norm_back(x_ref[...].astype(F32), gain_ref[...], grad_normed)
    grad = into + placed(here, grad_one_ref[...]) + placed(after, added_ref[...])
    back_ref[...] = dot_tn(placer_ref[...], grad.astype(LOW)).astype(LOW)


def layer_grads_body(
    core_ref, normed_ref, gate_ref, up_ref, hidden_ref, message_ref,
    own_ref, send_ref, own_down_ref, send_down_ref,
):
    second = core_ref[0] > 0
    gate, up = gate_ref[...], up_ref[...]
    normed = normed_ref[...]
    own_ref[...] = dot_tn(normed, jnp.where(second, up, gate)).astype(LOW)
    send_ref[...] = dot_tn(normed, jnp.where(second, gate, up)).astype(LOW)
    half = own_down_ref.shape[0]
    grads = message_ref[:, : own_down_ref.shape[1]]
    front, back = hidden_ref[:, :half], hidden_ref[:, half : 2 * half]
    own_down_ref[...] = dot_tn(jnp.where(second, back, front), grads).astype(LOW)
    send_down_ref[...] = dot_tn(jnp.where(second, front, back), grads).astype(LOW)


def summary_body(arrived_ref, rows_ref, names_ref, out_ref):
    arrived = arrived_ref[...]
    names = names_ref[...].astype(F32)
    cross = jnp.sum(arrived.astype(F32) * rows_ref[...].astype(F32), axis=0, keepdims=True)
    same = jnp.where(upright(names_ref[...]) == names, dot_nt(arrived, arrived), 0.0)
    out_ref[...] = 2.0 * jnp.sum(cross, axis=1, keepdims=True) + jnp.sum(
        jnp.sum(same, axis=0, keepdims=True), axis=1, keepdims=True
    )


def head_grad_body(
    span, first, far_ref, near_ref, far_tops_ref, near_tops_ref, rows_ref, other_ref, tails_ref, tails_other_ref,
    grad_ref, squares_ref,
):
    step = pl.program_id(0)
    block = step + first
    width = grad_ref.shape[1]
    half = far_ref.shape[0] // 2
    grad = 0.0
    for group, raised_ref, tops_ref in ((1, far_ref, far_tops_ref), (0, near_ref, near_tops_ref)):
        for at, (states_ref, tail_ref) in enumerate(
            ((rows_ref, tails_ref), (other_ref, tails_other_ref))
        ):
            here = slice(at * half, (at + 1) * half)
            tops = tops_ref[here]
            top = jnp.sum(
                jnp.where(iota(tops.shape, 1) == block // span, tops, 0.0), axis=1, keepdims=True
            )
            tail = tail_ref[group]
            scale = -decoded(tail, 1) * jnp.exp(top - decoded(tail, 0))
            states = states_ref[:, group].reshape(half, width).astype(F32)
            grad = grad + dot_tn(raised_ref[here], (states * scale).astype(LOW))
    grad_ref[...] = grad.astype(LOW)

    @pl.when(step == 0)
    def _():
        squares_ref[...] = jnp.zeros(squares_ref.shape, F32)

    squares_ref[...] += jnp.sum(grad * grad, axis=0, keepdims=True)


def head_grad(far, near, rows, other, tails, tails_other, vrows, block, span, first, steps, held):
    width = rows.shape[-1]
    tokens = far[0].shape[0]
    whole = lambda count: lambda step: (0,) * count
    raised = pl.BlockSpec((tokens, block), lambda step: (0, step + first))
    fixed = lambda array: pl.BlockSpec(array.shape, whole(array.ndim))
    return pl.pallas_call(
        lambda *refs: head_grad_body(span, first, *refs[:8], *refs[-2:]),
        grid=(steps,),
        in_specs=[
            raised,
            raised,
            fixed(far[1]),
            fixed(near[1]),
            fixed(rows),
            fixed(other),
            fixed(tails),
            fixed(tails_other),
        ]
        + [pl.BlockSpec(memory_space=pl.ANY)] * len(held),
        out_specs=[
            pl.BlockSpec((block, width), lambda step: (step + first, 0)),
            pl.BlockSpec((8, width), whole(2)),
        ],
        out_shape=[pltpu.HBM((vrows, width), LOW), like((8, width))],
        input_output_aliases={8 + at: at for at in range(len(held))},
        compiler_params=pltpu.CompilerParams(vmem_limit_bytes=(28 if tokens <= 512 else 60) * 2**20),
        cost_estimate=pl.CostEstimate(
            flops=4 * tokens * steps * block * width,
            bytes_accessed=steps * block * (4 * tokens + 2 * width),
            transcendentals=0,
        ),
        name="head_grad",
    )(*in_hbm(far[0], near[0], far[1], near[1], rows, other, tails, tails_other), *held)


def table_adam_body(first, scale_ref, names_ref, added_ref, grad_ref, w_ref, m_ref, v_ref, *refs):
    w_out, m_out, v_out = refs[-3:]
    rows = grad_ref.shape[0]
    here = iota((rows, names_ref.shape[1]), 0) + (pl.program_id(0) + first) * rows
    picker = jnp.where(here == names_ref[...], 1.0, 0.0).astype(LOW)
    grad = grad_ref[...].astype(F32) + dot_nn(picker, added_ref[...])
    w_out[...], m_out[...], v_out[...] = adam(
        w_ref[...], m_ref[...], v_ref[...], grad * scale_ref[0], LR_MATRIX, DECAY
    )


def table_adam(scale, names, added, grad, weight, moment, second, rows, first, steps, held):
    vrows, width = weight.shape
    whole = lambda step: (0, 0)
    here = pl.BlockSpec((rows, width), lambda step: (step + first, 0))
    return pl.pallas_call(
        functools.partial(table_adam_body, first),
        grid=(steps,),
        in_specs=[
            pl.BlockSpec(memory_space=pltpu.SMEM),
            pl.BlockSpec((1, names.shape[1]), whole),
            pl.BlockSpec(added.shape, whole),
            here,
            here,
            here,
            here,
        ]
        + [pl.BlockSpec(memory_space=pl.ANY)] * len(held),
        out_specs=[here, here, here],
        out_shape=[pltpu.HBM((vrows, width), F32)] * 3,
        input_output_aliases={7 + at: at for at in range(len(held))},
        compiler_params=pltpu.CompilerParams(vmem_limit_bytes=44 * 2**20),
        cost_estimate=pl.CostEstimate(
            flops=2 * names.shape[1] * steps * rows * width,
            bytes_accessed=steps * rows * width * 26,
            transcendentals=steps * rows * width,
        ),
        name="table_adam",
    )(scale, names, added, *in_hbm(grad, weight, moment, second), *held)


def per_device(
    token_ids,
    row_lengths,
    prompt_lengths,
    picks,
    old_logp,
    ref_logp,
    rewards,
    embed,
    embed_m,
    embed_v,
    w_qkv,
    w_qkv_m,
    w_qkv_v,
    w_out,
    w_out_m,
    w_out_v,
    w_gateup,
    w_gateup_m,
    w_gateup_v,
    w_down,
    w_down_m,
    w_down_v,
    gains,
    gains_m,
    gains_v,
    bias,
    bias_m,
    bias_v,
):
    both = ("batch", "seq")
    owners = lax.axis_size(both)
    seq_index = lax.axis_index("seq")
    row_index = lax.axis_index("batch")
    batch_count = lax.axis_size("batch")
    seq_count = lax.axis_size("seq")
    core_mask, far_mask = 1, 2
    on_core, on_far = bit_of("batch", core_mask), bit_of("batch", far_mask)
    low = LOW
    f32 = F32
    local_len = token_ids.shape[1]
    vrows, width = embed.shape
    shard = w_qkv.shape[0]
    half = shard // 2
    ff_part = FF // seq_count
    ff_wide = -(-ff_part // LANES) * LANES
    capacity = max(2, 2 * local_len // owners)
    kv_width = KV * HD
    q_width = H * HD
    n_picks = picks.shape[1]
    row_count = seq_count * n_picks

    requests, placer = in_vmem(
        functools.partial(request_body, vrows, capacity),
        [like((1, owners * capacity), jnp.int32), like((local_len, owners * capacity), low)],
        [token_ids],
        "requests",
    )
    sent_requests = exchange(requests.reshape(owners, capacity), both)

    core_row = lax.axis_index("batch") & core_mask
    qkv_cut = -(-(q_width + 2 * kv_width) // (2 * LANES)) * LANES
    out_cut = -(-width // (2 * LANES)) * LANES + LANES

    def part_of(value, columns):
        start = jnp.where(on_core, value.shape[1] - columns, 0)
        return lax.dynamic_slice(value, (jnp.where(on_far, half, 0), start), (half, columns)).astype(low)

    def widened(value):
        return jnp.pad(value, [(0, 0)] * (value.ndim - 1) + [(0, ff_wide - ff_part)])

    proj_parts = lax.all_gather(
        jnp.concatenate([part_of(w_qkv, qkv_cut), part_of(w_out, out_cut)], axis=1), "seq", axis=0
    )
    stages = seq_stages_of(seq_count)
    w_kv_full = spread(w_qkv[:, q_width:].astype(low), "seq", stages)
    pieces = jnp.transpose(part_of(w_gateup, FF).reshape(half, seq_count, ff_part), (1, 0, 2))
    pieces = xor_order(widened(pieces), "seq")
    w_down_low = jnp.pad(w_down.astype(low), ((0, ff_wide - ff_part), (0, 0)))
    sent_requests, pieces, w_down_low, w_kv_full = together(
        sent_requests, pieces, w_down_low, w_kv_full
    )
    w_kv_full = to_index_order(w_kv_full, "seq", stages).reshape(width, 2 * kv_width)

    def far_rows(value):
        return jnp.stack(double(value, "batch", far_mask), axis=1).reshape(width, -1)

    def core_columns(value, whole):
        first, second = double(value, "batch", core_mask)
        return jnp.concatenate([first, second[:, 2 * value.shape[1] - whole :]], axis=1)

    wanted = sent_requests.reshape(-1)
    found = embed.at[wanted].get(mode="promise_in_bounds").astype(low)
    returned = exchange(found.reshape(owners, capacity, width), both)
    pieces = [pieces[0]] + [partner(pieces[at], "seq", at) for at in range(1, seq_count)]
    returned, pieces, proj_parts, w_kv_full = together(returned, pieces, proj_parts, w_kv_full)
    returned = returned.reshape(owners * capacity, width)
    w_q_far = far_rows(proj_parts[..., :qkv_cut])
    w_q_full = core_columns(w_q_far, q_width + 2 * kv_width)[:, :q_width]
    out_short = out_cut - LANES
    out_parts = proj_parts[..., qkv_cut:]
    out_parts = jnp.where(on_core, out_parts[..., LANES:], out_parts[..., :out_short])
    w_out_far = far_rows(out_parts)

    places = seq_index * local_len + jnp.arange(local_len, dtype=jnp.int32)
    pick_places = seq_index * local_len + picks
    row_names = jnp.arange(batch_count, dtype=jnp.int32) == row_index
    prompt_here = jnp.sum(jnp.where(row_names, prompt_lengths, 0))
    length_here = jnp.sum(jnp.where(row_names, row_lengths, 0))
    live = ((pick_places >= prompt_here) & (pick_places + 1 < length_here)).astype(f32)
    advantage = (
        jnp.sum(jnp.where(row_names, rewards, 0.0)) - jnp.mean(rewards)
    ).reshape(1, 1)

    def rope_factors(slots):
        lane = jnp.arange(LANES, dtype=jnp.int32)
        frequency = ROPE_BASE ** (-2.0 * (lane % (HD // 2)).astype(f32) / HD)
        angles = slots.astype(f32)[:, None] * frequency[None, :]
        sign = jnp.where(lane % HD < HD // 2, -1.0, 1.0)
        return jnp.cos(angles), jnp.sin(angles) * sign[None, :]

    slot_cos, slot_sin = rope_factors(places)
    pick_cos, pick_sin = rope_factors(pick_places[0])
    bias_row = bias.reshape(1, -1)

    x_zero, normed_one, kv_low = in_vmem(
        embed_body,
        [like((local_len, width), low), like((local_len, width), low), like((seq_count, local_len, 2 * kv_width), low)],
        [returned, placer, w_kv_full, bias_row[:, q_width:], gains[:1], slot_cos, slot_sin],
        "keys_values",
        flops=2 * local_len * width * (owners * capacity + 2 * kv_width),
    )
    kv_all = exchange(kv_low, "seq")
    w_out_full = core_columns(w_out_far, width)
    gu_columns = xor_order(jnp.stack(pieces), "seq")
    picked_zero, target_rows, normed_picked, queries = in_vmem(
        pick_body,
        [
            like((n_picks, width)),
            like((n_picks, width)),
            like((n_picks, width), low),
            like((n_picks, q_width), low),
        ],
        [x_zero, normed_one, picks, w_q_full, bias_row[:, :q_width], pick_cos, pick_sin],
        "scored_queries",
        flops=2 * n_picks * width * (q_width + 3 * local_len),
    )
    kv_all, picked_zero, target_rows, normed_picked, queries, w_out_full, gu_columns = together(
        kv_all, picked_zero, target_rows, normed_picked, queries, w_out_full, gu_columns
    )
    gu_columns = far_rows(gu_columns)
    kv_all = kv_all.reshape(seq_count * local_len, 2 * kv_width)
    length = kv_all.shape[0]
    limit = 24
    mixed, attended, stream_one, normed_two = in_vmem(
        attend_body,
        [
            like((n_picks, q_width), low),
            like((n_picks, q_width)),
            like((n_picks, width)),
            like((seq_count, n_picks, width), low),
        ],
        [queries, kv_all, pick_places, w_out_full, picked_zero, gains[1:2]],
        "attention",
        flops=4 * n_picks * q_width * length + 2 * n_picks * q_width * width,
        exps=n_picks * H * length,
        limit=limit,
    )


    def shard_columns(value):
        return jnp.transpose(value.reshape(n_picks, seq_count, shard), (1, 0, 2))

    w_gate, w_up = double(gu_columns, "batch", core_mask)
    normed_two_all, w_gate, w_up, column_pieces = together(
        exchange(normed_two, "seq"),
        w_gate,
        w_up,
        jnp.concatenate([shard_columns(normed_picked), shard_columns(mixed)], axis=1),
    )
    normed_two_all = normed_two_all.reshape(row_count, width)
    gate_part, up_part, hidden, down_part = in_vmem(
        feed_body,
        [
            like((row_count, ff_wide)),
            like((row_count, ff_wide)),
            like((row_count, ff_wide), low),
            like((row_count, width), low),
        ],
        [normed_two_all, w_gate, w_up, w_down_low],
        "feed_forward",
        flops=6 * row_count * width * ff_part,
        limit=24,
        kept=(3,),
    )
    stream_two, final = in_vmem(
        feed_sum_body,
        [like((n_picks, width)), like((n_picks, width), low)],
        [exchange(down_part.reshape(seq_count, n_picks, width), "seq"), stream_one, gains[2:]],
        "final_norm",
    )

    near = jnp.stack([final, partner(final, "batch", far_mask)])
    rows = exchange_copies(near, "seq")
    other = partner(rows, "batch", core_mask)
    block = 1024

    gathered_columns = exchange(after(column_pieces, rows), "seq")

    def merge(*parts):
        return in_vmem(merge_body, [like(parts[0].shape, low)], parts, "merge_means")[0]

    far, gathered_columns = together(head_part(rows, other, 1, embed, block), gathered_columns)
    far_mean = merge(far[2], partner(far[3], "batch", core_mask))
    near_part, far_mean = together(
        head_part(after(rows, far_mean), other, 0, embed, block),
        partner(far_mean, "batch", far_mask),
    )
    means = merge(near_part[2], partner(near_part[3], "batch", core_mask), far_mean)
    mean_parts, gathered_columns = together(
        exchange(means.reshape(seq_count, n_picks, width + LANES), "seq"),
        to_xor_order(gathered_columns, "seq", stages),
    )
    message, grad_two, grad_gain_two, added, loss_here = in_vmem(
        loss_body,
        [
            like((seq_count, n_picks, width + LANES), low),
            like((n_picks, width)),
            like((1, width)),
            like((n_picks, width)),
            like((1, LANES)),
        ],
        [
            mean_parts,
            final,
            target_rows,
            stream_two,
            gains[2:],
            live,
            old_logp,
            ref_logp,
            advantage,
        ],
        "loss",
        kept=(2, 3, 4, 5, 6, 7),
    )

    messages = exchange(message, "seq").reshape(row_count, width + LANES)
    grad_gate, grad_up, normed_part = in_vmem(
        feed_back_body,
        [
            like((row_count, ff_wide), low),
            like((row_count, ff_wide), low),
            like((row_count, width), low),
        ],
        [messages, hidden, gate_part, up_part, w_gate, w_up, w_down_low],
        "feed_forward_back",
        flops=6 * row_count * width * ff_part,
        limit=28,
        kept=(1, 2, 3, 4, 5, 6),
    )
    normed_part = exchange(normed_part.reshape(seq_count, n_picks, width), "seq")

    layer_grads = in_vmem(
        layer_grads_body,
        [
            like((width, ff_wide), low),
            like((width, ff_wide), low),
            like((ff_part // 2, width), low),
            like((ff_part // 2, width), low),
        ],
        [
            core_row.reshape(1),
            normed_two_all,
            grad_gate,
            grad_up,
            hidden,
            messages,
        ],
        "layer_grads",
        flops=6 * row_count * width * ff_part,
        limit=24,
        kept=(1, 2, 3, 4, 5),
    )
    tails = messages[:, width:]
    tails = jnp.stack([tails, partner(tails, "batch", far_mask)])
    tails_other = partner(tails, "batch", core_mask)
    head_blocks = -(-vrows // (block // 2))
    head_args = (far, near_part, rows, other, tails, tails_other, vrows, block // 2, 2)
    head_cut = -(-head_blocks * 3 // 10)
    grad_head, head_squares = head_grad(*head_args, 0, head_cut, ())
    normed_part, layer_grads, grad_head, head_squares = together(
        normed_part, layer_grads, grad_head, head_squares
    )
    gu_own, gu_send, down_own, down_send = layer_grads
    gu_other = partner(gu_send, "batch", core_mask)
    down_other = partner(down_send, "batch", core_mask)
    grad_one, grad_one_low, grad_gain_one = in_vmem(
        one_back_body,
        [like((n_picks, width)), like((n_picks, width), low), like((1, width))],
        [
            normed_part,
            stream_one,
            grad_two,
            gains[1:2],
        ],
        "second_norm_back",
        kept=(1, 2, 3),
    )
    kv_grad, query_pre, query_bias = in_vmem(
        attend_back_body,
        [
            like((length, 2 * kv_width), low),
            like((n_picks, q_width), low),
            like((1, q_width)),
        ],
        [grad_one_low, w_out_full, queries, kv_all, pick_places, attended, pick_cos, pick_sin],
        "attention_back",
        flops=10 * n_picks * q_width * length,
        exps=n_picks * H * length,
        limit=limit + 4,
        kept=(1, 2, 3, 4, 5, 6, 7),
        scratch=[pltpu.VMEM((n_picks, q_width), f32)],
    )
    own_parts = exchange(kv_grad.reshape(seq_count, local_len, 2 * kv_width), "seq")

    def far_cut(value):
        return cut(value[..., 0, :, :], value[..., 1, :, :], "batch", far_mask)

    def far_sides(value):
        front, back = value[..., 0, :, :], value[..., 1, :, :]
        return jnp.where(on_far, back, front), jnp.where(on_far, front, back)

    gu_parts = far_sides(total_of([gu_own, gu_other]).reshape(seq_count, 2, half, ff_wide))
    down_parts = far_sides(total_of([down_own, down_other]).reshape(2, -1, width))
    grad_head, more_squares = head_grad(
        *head_args[:2], after(rows, kv_grad), *head_args[3:],
        head_cut, head_blocks - head_cut, (grad_head,),
    )
    late_rows = spread(jnp.concatenate([query_pre, grad_one_low], axis=0), "seq", stages)
    own_parts, gu_parts, down_parts, grad_head, more_squares, late_rows = together(
        own_parts, gu_parts, down_parts, grad_head, more_squares, late_rows
    )
    gu_parts = gu_parts[0], partner(gu_parts[1], "batch", far_mask)
    down_parts = down_parts[0], partner(down_parts[1], "batch", far_mask)
    kv_pre, sendback, grad_gain_zero, kv_bias = in_vmem(
        zero_back_body,
        [
            like((local_len, 2 * kv_width), low),
            like((owners * capacity, width), low),
            like((1, width)),
            like((1, 2 * kv_width)),
        ],
        [
            own_parts,
            slot_cos,
            slot_sin,
            w_kv_full,
            query_pre,
            w_q_full,
            picks,
            x_zero,
            gains[:1],
            grad_one,
            added,
            placer,
        ],
        "first_norm_back",
        kept=(1, 2, 3, 4, 5, 6, 7, 8, 9, 10, 11),
        flops=2 * local_len * width * (2 * kv_width + owners * capacity + 6 * n_picks),
    )
    gu_part, down_part_w = total_of(gu_parts), total_of(down_parts)

    grad_head, sendback = together(grad_head, sendback)
    arrived = exchange(sendback.reshape(owners, capacity, width), both)
    head_rows = grad_head.at[wanted].get(mode="promise_in_bounds")
    q_half = dot_tn(
        gathered_columns[:, :n_picks].reshape(row_count, shard),
        late_rows[:, :n_picks].reshape(row_count, q_width),
    )
    out_half = dot_tn(
        gathered_columns[:, n_picks:].reshape(row_count, shard),
        late_rows[:, n_picks:].reshape(row_count, width),
    )
    proj_part = halve(q_half.astype(low), out_half.astype(low), "batch", core_mask)
    proj_part = total_of(far_cut(proj_part.reshape(2, half, width)))
    kv_w_grad = dot_tn(normed_one, kv_pre).astype(low)
    kv_part = halve(kv_w_grad[:, :kv_width], kv_w_grad[:, kv_width:], "batch", core_mask)
    kv_part = sum_seq(total_of(far_cut(kv_part.reshape(seq_count, 2, half, kv_width))))
    own_squares = (
        squares_of(gu_part)
        + squares_of(down_part_w)
        + squares_of(proj_part)
        + squares_of(kv_part)
        + jnp.sum(head_squares[0])
        + jnp.sum(more_squares[0])
    )
    arrived, head_rows, own_squares, gu_part, down_part_w, proj_part, kv_part = together(
        arrived, head_rows, own_squares, gu_part, down_part_w, proj_part, kv_part
    )
    arrived = arrived.reshape(-1, width)
    row_squares = in_vmem(
        summary_body, [like((1, 1))], [arrived, head_rows, wanted[None]], "row_squares"
    )
    own_squares = own_squares + row_squares[0][0, 0]
    summary = jnp.concatenate(
        [
            grad_gain_zero[0],
            grad_gain_one[0],
            grad_gain_two[0],
            query_bias[0],
            kv_bias[0],
            jnp.stack([own_squares, loss_here[0, 0], jnp.sum(live)]),
            jnp.zeros((LANES - 3,), f32),
        ]
    ).reshape(-1, LANES)
    summary = jnp.sum(exchange_copies(summary, both), axis=0).reshape(-1)
    grad_gains = summary[: 3 * width].reshape(3, width)
    grad_bias_all = summary[3 * width : -LANES]
    squares, loss_sum = summary[-LANES], summary[1 - LANES]
    token_count = jnp.maximum(summary[2 - LANES], 1.0)
    grad_norm = (
        jnp.sqrt(
            squares + jnp.sum(grad_gains * grad_gains) + jnp.sum(grad_bias_all * grad_bias_all)
        )
        / token_count
    )
    factor = jnp.minimum(1.0, CLIP_NORM / (grad_norm + 1e-06)) / token_count

    block = 608
    blocks = -(-vrows // block)
    cuts = [0, -(-blocks * 3 // 8), -(-blocks * 6 // 8), blocks]

    def update_rows(at, held, first):
        return table_adam(
            after(factor.reshape(1), first),
            wanted[None],
            arrived,
            grad_head,
            embed,
            embed_m,
            embed_v,
            block,
            cuts[at],
            cuts[at + 1] - cuts[at],
            held,
        )

    def both_halves(value, axis, mask, at):
        return jnp.concatenate(double(value, axis, mask), axis=at)

    gu_rows = exchange(after(gu_part, factor), "seq")
    gu_rows, embed_new, down_part_w, proj_part, kv_part = together(
        gu_rows, update_rows(0, (), factor), down_part_w, proj_part, kv_part
    )
    gu_rows = jnp.transpose(gu_rows[..., :ff_part], (1, 0, 2)).reshape(half, FF)
    gu_far = both_halves(gu_rows, "batch", far_mask, 0)
    down_all = jnp.stack(double(down_part_w, "batch", far_mask), axis=0)
    small = both_halves(jnp.concatenate([proj_part, kv_part], axis=1), "batch", far_mask, 0)
    gu_far, down_all, small, embed_new = together(
        gu_far, down_all, small, update_rows(1, tuple(embed_new), gu_rows)
    )
    gu_all = both_halves(gu_far, "batch", core_mask, 1)
    down_all = jnp.stack(double(down_all, "batch", core_mask), axis=0).reshape(w_down.shape)
    first_small, second_small = double(small, "batch", core_mask)
    qkv_all = jnp.concatenate(
        [first_small[:, :width], first_small[:, width:], second_small[:, width:]], axis=1
    )
    out_all = second_small[:, :width]
    gu_all, down_all, qkv_all, out_all, embed_new = together(
        gu_all, down_all, qkv_all, out_all, update_rows(2, tuple(embed_new), gu_far)
    )

    def update(weight, moment, second, gradient, rate):
        return adam(weight, moment, second, gradient.astype(f32) * factor, rate, DECAY)

    qkv_new = update(w_qkv, w_qkv_m, w_qkv_v, qkv_all, LR_MATRIX)
    out_new = update(w_out, w_out_m, w_out_v, out_all, LR_OUT)
    gateup_new = update(w_gateup, w_gateup_m, w_gateup_v, gu_all, LR_MATRIX)
    down_new = update(w_down, w_down_m, w_down_v, down_all, LR_MATRIX)
    gains_new = adam(gains, gains_m, gains_v, grad_gains * factor, LR_GAIN, 0.0)
    bias_new = adam(bias, bias_m, bias_v, grad_bias_all * factor, LR_BIAS, 0.0)
    return (
        loss_sum,
        token_count,
        grad_norm,
        *embed_new,
        *qkv_new,
        *out_new,
        *gateup_new,
        *down_new,
        *gains_new,
        *bias_new,
    )


def solution(mesh):
    in_specs = (
        P("batch", "seq"),
        P(),
        P(),
        P("batch", "seq"),
        P("batch", "seq"),
        P("batch", "seq"),
        P(),
        P(("batch", "seq"), None),
        P(("batch", "seq"), None),
        P(("batch", "seq"), None),
        P("seq", None),
        P("seq", None),
        P("seq", None),
        P("seq", None),
        P("seq", None),
        P("seq", None),
        P("seq", None),
        P("seq", None),
        P("seq", None),
        P("seq", None),
        P("seq", None),
        P("seq", None),
        P(),
        P(),
        P(),
        P(),
        P(),
        P(),
    )
    out_specs = (
        P(),
        P(),
        P(),
        P(("batch", "seq"), None),
        P(("batch", "seq"), None),
        P(("batch", "seq"), None),
        P("seq", None),
        P("seq", None),
        P("seq", None),
        P("seq", None),
        P("seq", None),
        P("seq", None),
        P("seq", None),
        P("seq", None),
        P("seq", None),
        P("seq", None),
        P("seq", None),
        P("seq", None),
        P(),
        P(),
        P(),
        P(),
        P(),
        P(),
    )
    return jax.shard_map(
        per_device, mesh=mesh, in_specs=in_specs, out_specs=out_specs, check_vma=False
    )
```

time: 737 us -> 583 us (0.79)
  Pallas kernels: 0 us -> 142 us
  other arithmetic: 156 us -> 52.9 us
  matrix products: 98.2 us -> 1.53 us
  waiting for transfers between devices: 181 us -> 116 us
  local copies, waits for them, and re-layouts: 86.4 us -> 48.1 us
  blocking collectives: 66.9 us -> 79.9 us
    pallas_call x0 -> x22, Pallas kernels: none -> 142 us  [the longest x3 47.8 us: table_adam(): pl.pallas_call(functools.partial(table_adam_body, first), grid=(steps,),...]
    dot_general x23 -> x0, matrix products: 67.6 us -> none  [the longest x6 25.2 us: dot_nt(): lax.dot_general(left, right, (((1,), (1,)), ((), ())), preferred_element_...]
    all_to_all x1 -> x4, blocking collectives: 19.5 us -> 79.9 us  [exchange(): return lax.all_to_all(value, axes, split_axis=0, concat_axis=0, tiled=True)]
    all_gather x1 -> x0, blocking collectives: 47.4 us -> none  [per_device(): w_kv_full = lax.all_gather(w_kv_low, 'seq', axis=0, tiled=True)]
    sub x7 -> x6, other arithmetic: 60.7 us -> 14.1 us  [adam(): weight - learn_rate * (corrected / (jnp.sqrt(scaled) + ADAM_EPS) + decay_...]
    ppermute x61 -> x45, waiting for transfers between devices: 124 us -> 88.5 us  [partner(): lax.ppermute(value, axis, [(place, place ^ mask) for place in range(size)])]
    all_to_all x10, waiting for transfers between devices: 56.3 us -> 27.7 us  [exchange(): return lax.all_to_all(value, axes, split_axis=0, concat_axis=0, tiled=True)]
    dot_general x7 -> x3, matrix products: 26.3 us -> 1.53 us  [dot_tn(): lax.dot_general(left, right, (((0,), (0,)), ((), ())), preferred_element_...]
  transfers between devices with their start and end apart: 73 -> 56, of which waited for: 38 -> 21; matrix products, arithmetic and copies ran while one was open for 28% -> 11% of each run, Pallas kernels for 0% -> 20%
where the time goes in v2:
time: 583 us; the launch traced here: 576 us
  Pallas kernels  142 us (24%)
  waiting for transfers between devices  116 us (20%)
  starting transfers between devices  108 us (19%)
  blocking collectives  79.9 us (14%)
  other arithmetic  52.9 us (9%)
  local copies, waits for them, and re-layouts  48.1 us (8%)
  between operations  26.9 us (5%)
    ppermute x45, waiting for transfers between devices, partner(): lax.ppermute(value, axis, [(place, place ^ mask) for place in range(size)])  88.5 us
    all_to_all x4, blocking collectives, exchange(): return lax.all_to_all(value, axes, split_axis=0, concat_axis=0, tiled=True)  79.9 us
    ppermute x45, starting transfers between devices, partner(): lax.ppermute(value, axis, [(place, place ^ mask) for place in range(size)])  56.4 us
    all_to_all x10, starting transfers between devices, exchange(): return lax.all_to_all(value, axes, split_axis=0, concat_axis=0, tiled=True)  51.8 us
    pallas_call x3, Pallas kernels, table_adam(): pl.pallas_call(functools.partial(table_adam_body, first), grid=(steps,),...  47.8 us
    pallas_call x15, Pallas kernels, in_vmem(): pl.pallas_call(body, grid=(1,), in_specs=[pl.BlockSpec(a.shape, whole(a.n...  38 us
    pallas_call x2, Pallas kernels, head_part(): pl.pallas_call(functools.partial(head_body, vrows), grid=(steps,), in_spe...  34.3 us
    all_to_all x10, waiting for transfers between devices, exchange(): return lax.all_to_all(value, axes, split_axis=0, concat_axis=0, tiled=True)  27.7 us
  transfers between devices with their start and end apart: 56, of which 21 were waited for; matrix products, arithmetic and copies ran while one was open for 11% of the time, Pallas kernels for 20%

profile of v2, /device:TPU:0, one launch (start us, length us, event | category | flops | bytes accessed | tf_op | source)
XLA Modules:
  0.0 575.7 jit_solution(1570990602775979481)
XLA Ops:
  8.1 3.1 collective-permute-start
  11.2 2.6 collective-permute-start.1
  16.6 6.1 %all-to-all-start = ((s32[32,1,16]{2,1,0:T(1,128)}), s32[32,1,16]{2,1,0:T(1,128)S(1)}, u32[]{:S(2)}, u32[]{:S(2)}) async-start(s32[32,1,16]{2,1,0:T(1,128)} %bitcast), calls=%async_computation | async-start | bytes 32768 | tf_op jit(solution)/shard_map/all_to_all | solution.py:107
  29.1 2.4 fusion.31
  32.8 1.8 collective-permute-start.3
  34.6 7.5 %collective-permute-done.3 = bf16[4,112,256]{2,1,0:T(8,128)(2,1)S(1)} collective-permute-done((bf16[4,112,256]{2,1,0:T(8,128)(2,1)S(1)}, bf16[4,112,256]{2,1,0:T(8,128)(2,1)S(1)}, u32[]{:S(2)}, u32[]{:S(2)}) %collective-permute-start.3) | collective-permute-done | bytes 229408 | tf_op jit(solution)/shard_map/ppermute | solution.py:40
  42.3 9.1 %gather_fusion = bf16[512,896]{1,0:T(8,128)(2,1)} fusion(f32[4748,896]{1,0:T(8,128)} %w_ref.5, s32[1024]{0:T(1024)S(1)} %pad_clamp_fusion), kind=kCustom, calls=%fused_computation | custom fusion | bytes 1837056 | tf_op jit(solution)/shard_map/gather | solution.py:905
  51.4 5.7 all-to-all-start.1
  58.1 4.6 collective-permute-start.10
  63.5 2.9 collective-permute-start.6
  66.4 18.1 %collective-permute-done.10 = bf16[56,640]{1,0:T(8,128)(2,1)S(1)} collective-permute-done((bf16[56,640]{1,0:T(8,128)(2,1)S(1)}, bf16[56,640]{1,0:T(8,128)(2,1)S(1)}, u32[]{:S(2)}, u32[]{:S(2)}) %collective-permute-start.10) | collective-permute-done | bytes 71712 | tf_op jit(solution)/shard_map/ppermute | solution.py:40
  84.5 7.9 %collective-permute-start.8 = (bf16[56,640]{1,0:T(8,128)(2,1)S(1)}, bf16[56,640]{1,0:T(8,128)(2,1)S(1)}, u32[]{:S(2)}, u32[]{:S(2)}) collective-permute-start(bf16[56,640]{1,0:T(8,128)(2,1)S(1)} %get-tuple-element.375), channel_id=1, source_target_pairs={{0,5},{1,4},{2,7},{3,6},{4,1},{5,0},{6,3},{7,2},{8,13},{9,12},{10,... | collective-permute-start | bytes 215048 | tf_op jit(solution)/shard_map/ppermute | solution.py:40
  92.4 2.6 collective-permute-start.9
  95.6 3.4 collective-permute-done.9
  99.0 2.0 slice_select_fusion.2
  101.0 1.9 slice.183
  105.0 2.0 keys_values.1
  108.6 4.8 all-to-all-start.2
  113.7 3.1 collective-permute-done.13
  118.1 9.1 %collective-permute-done.11 = bf16[8,56,640]{2,1,0:T(8,128)(2,1)S(1)} collective-permute-done((bf16[8,56,640]{2,1,0:T(8,128)(2,1)}, bf16[8,56,640]{2,1,0:T(8,128)(2,1)S(1)}, u32[]{:S(2)}, u32[]{:S(2)}) %collective-permute-start.11) | collective-permute-done | bytes 573472 | tf_op jit(solution)/shard_map/ppermute | solution.py:40
  133.5 4.8 all-to-all-done.2
  139.7 11.2 %collective-permute-done.15 = bf16[8,56,640]{2,1,0:T(8,128)(2,1)S(1)} collective-permute-done((bf16[8,56,640]{2,1,0:T(8,128)(2,1)}, bf16[8,56,640]{2,1,0:T(8,128)(2,1)S(1)}, u32[]{:S(2)}, u32[]{:S(2)}) %collective-permute-start.15) | collective-permute-done | bytes 573472 | tf_op jit(solution)/shard_map/ppermute | solution.py:40
  153.5 4.8 attention.1
  158.9 6.0 %all-to-all-start.3 = ((bf16[8,32,896]{2,1,0:T(8,128)(2,1)}), bf16[8,32,896]{2,1,0:T(8,128)(2,1)S(1)}, u32[]{:S(2)}, u32[]{:S(2)}) async-start(bf16[8,32,896]{2,1,0:T(8,128)(2,1)} %get-tuple-element.202), calls=%async_computation.3 | async-start | bytes 917504 | tf_op jit(solution)/shard_map/all_to_all | solution.py:107
  165.9 1.8 broadcast_select_fusion.1
  167.7 10.8 %all-to-all-done.3 = bf16[8,32,896]{2,1,0:T(8,128)(2,1)S(1)} async-done(((bf16[8,32,896]{2,1,0:T(8,128)(2,1)}), bf16[8,32,896]{2,1,0:T(8,128)(2,1)S(1)}, u32[]{:S(2)}, u32[]{:S(2)}) %all-to-all-start.3) | async-done | bytes 458784 | tf_op jit(solution)/shard_map/all_to_all | solution.py:107
  178.5 2.8 feed_forward.1
  181.3 16.8 %all_to_all.77.parts_ref = bf16[8,32,896]{2,1,0:T(8,128)(2,1)S(1)} all-to-all(bf16[8,32,896]{2,1,0:T(8,128)(2,1)S(1)} %bitcast.194), channel_id=1, replica_groups=mesh['batch'=4,'seq'=8] {'seq'}, dimensions={0} | all-to-all | bytes 917504 | tf_op jit(solution)/shard_map/all_to_all | solution.py:107
  199.8 2.7 collective-permute-done.17
  202.7 25.2 %all_to_all.78.rows_ref.refs_4_ = bf16[8,2,32,896]{3,2,1,0:T(8,128)(2,1)S(1)} all-to-all(bf16[8,2,32,896]{3,2,1,0:T(8,128)(2,1)S(1)} %broadcast_in_dim.52), channel_id=1, replica_groups=mesh['batch'=4,'seq'=8] {'seq'}, dimensions={0} | all-to-all | bytes 1835008 | tf_op jit(solution)/shard_map/all_to_all | solution.py:107
  228.0 3.6 all-to-all-start.6
  231.7 17.3 %head_part.2 = (bf16[512,5120]{1,0:T(8,128)(2,1)}, f32[512,128]{1,0:T(8,128)S(1)}, bf16[256,1024]{1,0:T(8,128)(2,1)S(1)}, bf16[256,1024]{1,0:T(8,128)(2,1)S(1)}) custom-call(bf16[8,2,32,896]{3,2,1,0:T(8,128)(2,1)S(1)} %all_to_all.78.rows_ref.refs_4_, bf16[8,2,32,896]{3,2,1,0:T(8,128)(2,1)S(1)} %collective-permute-done.18.other_ref.refs_5_, f32[4748,896]{1,0:T(8,128)} %w_ref.5), custom_call_target="tpu_custom_call" | custom-call | flops 8712617984 | bytes 21878784 | tf_op jit(solution)/shard_map/head_part/pallas_call | solution.py:501
  254.7 17.0 %head_part.3 = (bf16[512,5120]{1,0:T(8,128)(2,1)}, f32[512,128]{1,0:T(8,128)S(1)}, bf16[256,1024]{1,0:T(8,128)(2,1)S(1)}, bf16[256,1024]{1,0:T(8,128)(2,1)S(1)}) custom-call(bf16[8,2,32,896]{3,2,1,0:T(8,128)(2,1)S(1)} %all_to_all.78.rows_ref.refs_4_, bf16[8,2,32,896]{3,2,1,0:T(8,128)(2,1)S(1)} %collective-permute-done.18.other_ref.refs_5_, f32[4748,896]{1,0:T(8,128)} %w_ref.5), custom_call_target="tpu_custom_call" | custom-call | flops 8712617984 | bytes 21878784 | tf_op jit(solution)/shard_map/head_part/pallas_call | solution.py:501
  275.0 5.9 %all-to-all-start.7 = ((bf16[8,32,1024]{2,1,0:T(8,128)(2,1)}), bf16[8,32,1024]{2,1,0:T(8,128)(2,1)S(1)}, u32[]{:S(2)}, u32[]{:S(2)}) async-start(bf16[8,32,1024]{2,1,0:T(8,128)(2,1)} %bitcast.48), calls=%async_computation.7 | async-start | bytes 1048576 | tf_op jit(solution)/shard_map/all_to_all | solution.py:107
  283.5 12.1 %all-to-all-done.7.parts_ref = bf16[8,32,1024]{2,1,0:T(8,128)(2,1)S(1)} async-done(((bf16[8,32,1024]{2,1,0:T(8,128)(2,1)}), bf16[8,32,1024]{2,1,0:T(8,128)(2,1)S(1)}, u32[]{:S(2)}, u32[]{:S(2)}) %all-to-all-start.7) | async-done | bytes 524320 | tf_op jit(solution)/shard_map/all_to_all | solution.py:107
  297.1 18.1 %all_to_all.79 = bf16[8,32,1024]{2,1,0:T(8,128)(2,1)S(1)} all-to-all(bf16[8,32,1024]{2,1,0:T(8,128)(2,1)S(1)} %get-tuple-element.233), channel_id=1, replica_groups=mesh['batch'=4,'seq'=8] {'seq'}, dimensions={0} | all-to-all | bytes 1048576 | tf_op jit(solution)/shard_map/all_to_all | solution.py:107
  315.2 4.9 feed_forward_back.1
  321.6 4.1 all-to-all-start.9
  326.3 3.7 collective-permute-done.22
  330.8 3.4 layer_grads.1
  334.9 7.7 %head_grad.2 = (bf16[4748,896]{1,0:T(8,128)(2,1)}, f32[8,896]{1,0:T(8,128)S(1)}) custom-call(bf16[512,5120]{1,0:T(8,128)(2,1)} %get-tuple-element.244.refs_0_, bf16[512,5120]{1,0:T(8,128)(2,1)} %get-tuple-element.245.refs_1_, f32[512,128]{1,0:T(8,128)} %copy-done.22, f32[512,128]{1,0:T(8,128)} %copy-done.23, bf16[8,2,32,896]{3,2,1,0:T(8,128)(2,1)} %copy-done.5, ...), custom_call_target="tpu_custom_call" | custom-call | flops 2818572288 | bytes 5898240 | tf_op jit(solution)/shard_map/head_grad/pallas_call | solution.py:742
  344.4 8.0 %attention_back.1 = (bf16[2048,256]{1,0:T(8,128)(2,1)}, bf16[32,896]{1,0:T(8,128)(2,1)S(1)}, f32[1,896]{1,0:T(1,128)S(1)}) custom-call(bf16[32,896]{1,0:T(8,128)(2,1)S(1)} %get-tuple-element.252.grad_ref, bf16[896,896]{1,0:T(8,128)(2,1)} %copy-done.1, bf16[32,896]{1,0:T(8,128)(2,1)} %copy-done.24, bf16[2048,256]{1,0:T(8,128)(2,1)} %bitcast.38.kv_ref, ...), custom_call_target="tpu_custom_call" | custom-call | flops 587202560 | bytes 4025984 | tf_op jit(solution)/shard_map/attention_back/pallas_call | solution.py:208
  353.0 2.0 collective-permute-start.26
  355.0 2.4 collective-permute-start.27
  358.6 6.2 %all-to-all-start.10 = ((bf16[8,256,256]{2,1,0:T(8,128)(2,1)}), bf16[8,256,256]{2,1,0:T(8,128)(2,1)S(1)}, u32[]{:S(2)}, u32[]{:S(2)}) async-start(bf16[8,256,256]{2,1,0:T(8,128)(2,1)} %bitcast.58), calls=%async_computation.10 | async-start | bytes 2097152 | tf_op jit(solution)/shard_map/all_to_all | solution.py:107
  364.8 14.1 %head_grad.3 = (bf16[4748,896]{1,0:T(8,128)(2,1)}, f32[8,896]{1,0:T(8,128)S(1)}) custom-call(bf16[512,5120]{1,0:T(8,128)(2,1)} %get-tuple-element.244.refs_0_, bf16[512,5120]{1,0:T(8,128)(2,1)} %get-tuple-element.245.refs_1_, f32[512,128]{1,0:T(8,128)} %copy-done.22, f32[512,128]{1,0:T(8,128)} %copy-done.23, ...), custom_call_target="tpu_custom_call", output_to_operand_aliasing={{0}: (8, {})} | custom-call | flops 6576668672 | bytes 13762560 | tf_op jit(solution)/shard_map/head_grad/pallas_call | solution.py:742
  381.9 2.1 collective-permute-start.29
  390.8 5.0 collective-permute-done.29
  400.1 5.2 first_norm_back.1
  410.1 7.0 %gather_fusion.1 = bf16[512,896]{1,0:T(8,128)(2,1)S(1)} fusion(bf16[4748,896]{1,0:T(8,128)(2,1)} %get-tuple-element.275.grad_ref, s32[1024]{0:T(1024)S(1)} %copy-done.73), kind=kCustom, calls=%fused_computation.1 | custom fusion | bytes 1837056 | tf_op jit(solution)/shard_map/gather | solution.py:1188
  417.2 5.7 all-to-all-start.11
  425.3 1.8 collective-permute-start.35
  428.1 10.9 %collective-permute-done.35 = bf16[8,56,128]{2,1,0:T(8,128)(2,1)S(1)} collective-permute-done((bf16[8,56,128]{2,1,0:T(8,128)(2,1)S(1)}, bf16[8,56,128]{2,1,0:T(8,128)(2,1)S(1)}, u32[]{:S(2)}, u32[]{:S(2)}) %collective-permute-start.35) | collective-permute-done | bytes 114720 | tf_op jit(solution)/shard_map/ppermute | solution.py:40
  439.0 5.1 collective-permute-start.36
  444.8 4.0 collective-permute-done.36
  450.7 2.1 collective-permute-done.37
  457.2 2.7 multiply_reduce_fusion
  466.7 19.8 %all_to_all.80 = f32[32,31,128]{2,1,0:T(8,128)S(1)} all-to-all(f32[32,31,128]{2,1,0:T(8,128)S(1)} %broadcast_in_dim.58), channel_id=1, replica_groups=mesh['batch'=4,'seq'=8] {'batch','seq'}, dimensions={0} | all-to-all | bytes 1015808 | tf_op jit(solution)/shard_map/all_to_all | solution.py:107
  491.1 3.8 all-to-all-start.13
  494.9 18.6 %table_adam.3 = (f32[4748,896]{1,0:T(8,128)}, f32[4748,896]{1,0:T(8,128)}, f32[4748,896]{1,0:T(8,128)}) custom-call(f32[1]{0:T(128)} %bitcast.84.scale_ref, s32[1,512]{1,0:T(1,128)S(1)} %broadcast_in_dim_reshape.2.names_ref, bf16[512,896]{1,0:T(8,128)(2,1)S(1)} %bitcast.183, bf16[4748,896]{1,0:T(8,128)(2,1)} %get-tuple-element.275.grad_ref, ...), custom_call_target="tpu_custom_call" | custom-call | flops 1673527296 | bytes 42491904 | tf_op jit(solution)/shard_map/table_adam/pallas_call | solution.py:787
  517.6 18.6 %table_adam.4 = (f32[4748,896]{1,0:T(8,128)}, f32[4748,896]{1,0:T(8,128)}, f32[4748,896]{1,0:T(8,128)}) custom-call(f32[1]{0:T(128)} %bitcast.84.scale_ref, s32[1,512]{1,0:T(1,128)S(1)} %broadcast_in_dim_reshape.2.names_ref, bf16[512,896]{1,0:T(8,128)(2,1)S(1)} %bitcast.184, ...), custom_call_target="tpu_custom_call", output_to_operand_aliasing={{0}: (7, {}), {1}: (8, {}), {2}: (9, {})} | custom-call | flops 1673527296 | bytes 42491904 | tf_op jit(solution)/shard_map/table_adam/pallas_call | solution.py:787
  538.7 10.5 %table_adam.5 = (f32[4748,896]{1,0:T(8,128)}, f32[4748,896]{1,0:T(8,128)}, f32[4748,896]{1,0:T(8,128)}) custom-call(f32[1]{0:T(128)} %bitcast.84.scale_ref, s32[1,512]{1,0:T(1,128)S(1)} %broadcast_in_dim_reshape.2.names_ref, bf16[512,896]{1,0:T(8,128)(2,1)S(1)} %bitcast.185, ...), custom_call_target="tpu_custom_call", output_to_operand_aliasing={{0}: (7, {}), {1}: (8, {}), {2}: (9, {})} | custom-call | flops 1115684864 | bytes 28327936 | tf_op jit(solution)/shard_map/table_adam/pallas_call | solution.py:787
  552.8 4.0 multiply_subtract_fusion.1
  556.9 6.3 %multiply_subtract_fusion = (f32[112,9728]{1,0:T(8,128)}, f32[112,9728]{1,0:T(8,128)}, f32[112,9728]{1,0:T(8,128)}) fusion(f32[112,9728]{1,0:T(8,128)S(1)} %bitcast.209, f32[]{:T(128)} %div.115, bf16[112,9728]{1,0:T(8,128)(2,1)S(1)} %pad_maximum_fusion, f32[112,9728]{1,0:T(8,128)S(1)} %bitcast.212, f32[112,9728]{1,0:T(8,128)S(1)} %bitcast.214), kind=kLoop, calls=%fused_computation.4 | loop fusion | flops 18522112 | bytes 28327940 | tf_op jit(solution)/shard_map/sub | solution.py:179
  (415 shorter events, 97.4 us)
Async XLA Ops:
  8.1 24.6 %collective-permute-start = (bf16[1,112,256]{2,1,0:T(8,128)(2,1)S(1)}, bf16[1,112,256]{2,1,0:T(8,128)(2,1)S(1)}, u32[]{:S(2)}, u32[]{:S(2)}) collective-permute-start(bf16[1,112,256]{2,1,0:T(8,128)(2,1)S(1)} %get-tuple-element.358), channel_id=1, source_target_pairs={{0,2},{1,3},{2,0},{3,1},{4,6},{5,7},{6,4},{7,5},{8,10},{9,11},{10,... | collective-permute-start | bytes 172040 | tf_op jit(solution)/shard_map/ppermute | solution.py:40
  11.2 21.5 %collective-permute-start.1 = (bf16[1,112,256]{2,1,0:T(8,128)(2,1)S(1)}, bf16[1,112,256]{2,1,0:T(8,128)(2,1)S(1)}, u32[]{:S(2)}, u32[]{:S(2)}) collective-permute-start(bf16[1,112,256]{2,1,0:T(8,128)(2,1)S(1)} %get-tuple-element.358), channel_id=1, source_target_pairs={{0,4},{1,5},{2,6},{3,7},{4,0},{5,1},{6,2},{7,3},{8,12},{9,13},{10,... | collective-permute-start | bytes 172040 | tf_op jit(solution)/shard_map/ppermute | solution.py:40
  13.8 18.9 %collective-permute-start.2 = (bf16[1,112,256]{2,1,0:T(8,128)(2,1)S(1)}, bf16[1,112,256]{2,1,0:T(8,128)(2,1)S(1)}, u32[]{:S(2)}, u32[]{:S(2)}) collective-permute-start(bf16[1,112,256]{2,1,0:T(8,128)(2,1)S(1)} %get-tuple-element.358), channel_id=1, source_target_pairs={{0,6},{1,7},{2,4},{3,5},{4,2},{5,3},{6,0},{7,1},{8,14},{9,15},{10,... | collective-permute-start | bytes 172040 | tf_op jit(solution)/shard_map/ppermute | solution.py:40
  14.7 90.3 %copy-start.15 = (bf16[256,512]{1,0:T(8,128)(2,1)}, bf16[256,512]{1,0:T(8,128)(2,1)S(1)}, u32[]{:S(2)}) copy-start(bf16[256,512]{1,0:T(8,128)(2,1)S(1)} %get-tuple-element.180.placer_ref) | copy-start | bytes 786436
  16.6 25.5 %all-to-all-start = ((s32[32,1,16]{2,1,0:T(1,128)}), s32[32,1,16]{2,1,0:T(1,128)S(1)}, u32[]{:S(2)}, u32[]{:S(2)}) async-start(s32[32,1,16]{2,1,0:T(1,128)} %bitcast), calls=%async_computation | async-start | bytes 32768 | tf_op jit(solution)/shard_map/all_to_all | solution.py:107
  22.7 76.2 %all-gather.3.cloned.1.call-start = ((), (), s32[]{:S(2)}) async-start(), calls=%async_computation.14 | async-start | bytes 1290240 | tf_op jit(solution)/shard_map/all_gather | solution.py:884
  31.5 120.9 %copy-start.39 = (s32[1,32]{1,0:T(1,128)}, s32[1,32]{1,0:T(1,128)S(1)}, u32[]{:S(2)}) copy-start(s32[1,32]{1,0:T(1,128)S(1)} %get-tuple-element.348.place_ref) | copy-start | bytes 388
  32.8 9.4 %collective-permute-start.3 = (bf16[4,112,256]{2,1,0:T(8,128)(2,1)S(1)}, bf16[4,112,256]{2,1,0:T(8,128)(2,1)S(1)}, u32[]{:S(2)}, u32[]{:S(2)}) collective-permute-start(bf16[4,112,256]{2,1,0:T(8,128)(2,1)S(1)} %pad_maximum_fusion.11), channel_id=1, source_target_pairs={{0,1},{1,0},{2,3},{3,2},{4,5},{5,4},{6,7},{7,6},{8,9},{9,8},{10,11... | collective-permute-start | bytes 688136 | tf_op jit(solution)/shard_map/ppermute | solution.py:40
  51.4 47.6 %all-to-all-start.1 = ((bf16[32,16,896]{2,1,0:T(8,128)(2,1)}), bf16[32,16,896]{2,1,0:T(8,128)(2,1)S(1)}, u32[]{:S(2)}, u32[]{:S(2)}) async-start(bf16[32,16,896]{2,1,0:T(8,128)(2,1)} %bitcast.6), calls=%async_computation.1 | async-start | bytes 1835008 | tf_op jit(solution)/shard_map/all_to_all | solution.py:107
  57.2 47.8 %copy-start.35 = (f32[1,896]{1,0:T(1,128)}, f32[1,896]{1,0:T(1,128)S(1)}, u32[]{:S(2)}) copy-start(f32[1,896]{1,0:T(1,128)S(1)} %get-tuple-element.396.gain_ref) | copy-start | bytes 10756
  57.2 95.2 %copy-start.36 = (f32[1,896]{1,0:T(1,128)}, f32[1,896]{1,0:T(1,128)S(1)}, u32[]{:S(2)}) copy-start(f32[1,896]{1,0:T(1,128)S(1)} %get-tuple-element.395.gain_ref) | copy-start | bytes 10756
  57.2 140.9 %copy-start.37 = (f32[1,896]{1,0:T(1,128)}, f32[1,896]{1,0:T(1,128)S(1)}, u32[]{:S(2)}) copy-start(f32[1,896]{1,0:T(1,128)S(1)} %get-tuple-element.394.gain_ref) | copy-start | bytes 10756
  57.4 73.5 %copy-start.25 = (f32[32,128]{1,0:T(8,128)}, f32[32,128]{1,0:T(8,128)S(1)}, u32[]{:S(2)}) copy-start(f32[32,128]{1,0:T(8,128)S(1)} %get-tuple-element.399.sin_ref) | copy-start | bytes 49156
  57.4 73.5 %copy-start.26 = (f32[32,128]{1,0:T(8,128)}, f32[32,128]{1,0:T(8,128)S(1)}, u32[]{:S(2)}) copy-start(f32[32,128]{1,0:T(8,128)S(1)} %get-tuple-element.400.cos_ref) | copy-start | bytes 49156
  58.0 47.1 %copy-start.13 = (f32[256,128]{1,0:T(8,128)}, f32[256,128]{1,0:T(8,128)S(1)}, u32[]{:S(2)}) copy-start(f32[256,128]{1,0:T(8,128)S(1)} %get-tuple-element.397.sin_ref) | copy-start | bytes 393220
  58.1 26.4 %collective-permute-start.10 = (bf16[56,640]{1,0:T(8,128)(2,1)S(1)}, bf16[56,640]{1,0:T(8,128)(2,1)S(1)}, u32[]{:S(2)}, u32[]{:S(2)}) collective-permute-start(bf16[56,640]{1,0:T(8,128)(2,1)S(1)} %get-tuple-element.373), channel_id=1, source_target_pairs={{0,7},{1,6},{2,5},{3,4},{4,3},{5,2},{6,1},{7,0},{8,15},{9,14},{10,... | collective-permute-start | bytes 215048 | tf_op jit(solution)/shard_map/ppermute | solution.py:40
  62.7 29.7 %collective-permute-start.4 = (bf16[56,640]{1,0:T(8,128)(2,1)S(1)}, bf16[56,640]{1,0:T(8,128)(2,1)S(1)}, u32[]{:S(2)}, u32[]{:S(2)}) collective-permute-start(bf16[56,640]{1,0:T(8,128)(2,1)S(1)} %get-tuple-element.379), channel_id=1, source_target_pairs={{0,1},{1,0},{2,3},{3,2},{4,5},{5,4},{6,7},{7,6},{8,9},{9,8},{10,11... | collective-permute-start | bytes 215048 | tf_op jit(solution)/shard_map/ppermute | solution.py:40
  63.4 31.8 %collective-permute-start.5 = (bf16[56,640]{1,0:T(8,128)(2,1)S(1)}, bf16[56,640]{1,0:T(8,128)(2,1)S(1)}, u32[]{:S(2)}, u32[]{:S(2)}) collective-permute-start(bf16[56,640]{1,0:T(8,128)(2,1)S(1)} %get-tuple-element.378), channel_id=1, source_target_pairs={{0,2},{1,3},{2,0},{3,1},{4,6},{5,7},{6,4},{7,5},{8,10},{9,11},{10,... | collective-permute-start | bytes 215048 | tf_op jit(solution)/shard_map/ppermute | solution.py:40
  63.5 31.7 %collective-permute-start.6 = (bf16[56,640]{1,0:T(8,128)(2,1)S(1)}, bf16[56,640]{1,0:T(8,128)(2,1)S(1)}, u32[]{:S(2)}, u32[]{:S(2)}) collective-permute-start(bf16[56,640]{1,0:T(8,128)(2,1)S(1)} %get-tuple-element.377), channel_id=1, source_target_pairs={{0,3},{1,2},{2,1},{3,0},{4,7},{5,6},{6,5},{7,4},{8,11},{9,10},{10,... | collective-permute-start | bytes 215048 | tf_op jit(solution)/shard_map/ppermute | solution.py:40
  66.4 28.8 %collective-permute-start.7 = (bf16[56,640]{1,0:T(8,128)(2,1)S(1)}, bf16[56,640]{1,0:T(8,128)(2,1)S(1)}, u32[]{:S(2)}, u32[]{:S(2)}) collective-permute-start(bf16[56,640]{1,0:T(8,128)(2,1)S(1)} %get-tuple-element.376), channel_id=1, source_target_pairs={{0,4},{1,5},{2,6},{3,7},{4,0},{5,1},{6,2},{7,3},{8,12},{9,13},{10,... | collective-permute-start | bytes 215048 | tf_op jit(solution)/shard_map/ppermute | solution.py:40
  84.5 11.1 %collective-permute-start.8 = (bf16[56,640]{1,0:T(8,128)(2,1)S(1)}, bf16[56,640]{1,0:T(8,128)(2,1)S(1)}, u32[]{:S(2)}, u32[]{:S(2)}) collective-permute-start(bf16[56,640]{1,0:T(8,128)(2,1)S(1)} %get-tuple-element.375), channel_id=1, source_target_pairs={{0,5},{1,4},{2,7},{3,6},{4,1},{5,0},{6,3},{7,2},{8,13},{9,12},{10,... | collective-permute-start | bytes 215048 | tf_op jit(solution)/shard_map/ppermute | solution.py:40
  92.4 6.5 %collective-permute-start.9 = (bf16[56,640]{1,0:T(8,128)(2,1)S(1)}, bf16[56,640]{1,0:T(8,128)(2,1)S(1)}, u32[]{:S(2)}, u32[]{:S(2)}) collective-permute-start(bf16[56,640]{1,0:T(8,128)(2,1)S(1)} %get-tuple-element.374), channel_id=1, source_target_pairs={{0,6},{1,7},{2,4},{3,5},{4,2},{5,3},{6,0},{7,1},{8,14},{9,15},{10,... | collective-permute-start | bytes 215048 | tf_op jit(solution)/shard_map/ppermute | solution.py:40
  102.9 13.8 %collective-permute-start.13 = (bf16[8,56,512]{2,1,0:T(8,128)(2,1)}, bf16[8,56,512]{2,1,0:T(8,128)(2,1)}, u32[]{:S(2)}, u32[]{:S(2)}) collective-permute-start(bf16[8,56,512]{2,1,0:T(8,128)(2,1)} %slice_select_fusion.2), channel_id=1, source_target_pairs={{0,16},{8,24},{16,0},{24,8},{1,17},{9,25},{17,1},{25,9},{2,18},{10... | collective-permute-start | bytes 1376264 | tf_op jit(solution)/shard_map/ppermute | solution.py:40
  104.4 22.8 %collective-permute-start.11 = (bf16[8,56,640]{2,1,0:T(8,128)(2,1)}, bf16[8,56,640]{2,1,0:T(8,128)(2,1)S(1)}, u32[]{:S(2)}, u32[]{:S(2)}) collective-permute-start(bf16[8,56,640]{2,1,0:T(8,128)(2,1)} %slice.183), channel_id=1, source_target_pairs={{0,16},{8,24},{16,0},{24,8},{1,17},{9,25},{17,1},{25,9},{2,18},{10... | collective-permute-start | bytes 1720328 | tf_op jit(solution)/shard_map/ppermute | solution.py:40
  108.6 29.7 %all-to-all-start.2 = ((bf16[8,256,256]{2,1,0:T(8,128)(2,1)}), bf16[8,256,256]{2,1,0:T(8,128)(2,1)}, u32[]{:S(2)}, u32[]{:S(2)}) async-start(bf16[8,256,256]{2,1,0:T(8,128)(2,1)} %get-tuple-element.182), calls=%async_computation.2 | async-start | bytes 2097152 | tf_op jit(solution)/shard_map/all_to_all | solution.py:107
  118.1 10.5 %collective-permute-start.14 = (bf16[896,512]{1,0:T(8,128)(2,1)S(1)}, bf16[896,512]{1,0:T(8,128)(2,1)S(1)}, u32[]{:S(2)}, u32[]{:S(2)}) collective-permute-start(bf16[896,512]{1,0:T(8,128)(2,1)S(1)} %bitcast.206), channel_id=1, source_target_pairs={{0,8},{8,0},{16,24},{24,16},{1,9},{9,1},{17,25},{25,17},{2,10},{10... | collective-permute-start | bytes 2752520 | tf_op jit(solution)/shard_map/ppermute | solution.py:40
  127.5 2.9 collective-permute-start.12
  138.3 12.6 %collective-permute-start.15 = (bf16[8,56,640]{2,1,0:T(8,128)(2,1)}, bf16[8,56,640]{2,1,0:T(8,128)(2,1)S(1)}, u32[]{:S(2)}, u32[]{:S(2)}) collective-permute-start(bf16[8,56,640]{2,1,0:T(8,128)(2,1)} %bitcast.216), channel_id=1, source_target_pairs={{0,16},{8,24},{16,0},{24,8},{1,17},{9,25},{17,1},{25,9},{2,18},{10... | collective-permute-start | bytes 1720328 | tf_op jit(solution)/shard_map/ppermute | solution.py:40
  152.3 13.5 %collective-permute-start.16 = (bf16[896,640]{1,0:T(8,128)(2,1)S(1)}, bf16[896,640]{1,0:T(8,128)(2,1)}, u32[]{:S(2)}, u32[]{:S(2)}) collective-permute-start(bf16[896,640]{1,0:T(8,128)(2,1)S(1)} %bitcast.210), channel_id=1, source_target_pairs={{0,8},{8,0},{16,24},{24,16},{1,9},{9,1},{17,25},{25,17},{2,10},{10... | collective-permute-start | bytes 3440648 | tf_op jit(solution)/shard_map/ppermute | solution.py:40
  158.9 19.6 %all-to-all-start.3 = ((bf16[8,32,896]{2,1,0:T(8,128)(2,1)}), bf16[8,32,896]{2,1,0:T(8,128)(2,1)S(1)}, u32[]{:S(2)}, u32[]{:S(2)}) async-start(bf16[8,32,896]{2,1,0:T(8,128)(2,1)} %get-tuple-element.202), calls=%async_computation.3 | async-start | bytes 917504 | tf_op jit(solution)/shard_map/all_to_all | solution.py:107
  198.3 4.2 collective-permute-start.17
  228.0 3.7 collective-permute-start.18
  228.0 22.5 %all-to-all-start.6 = ((bf16[8,64,112]{2,1,0:T(8,128)(2,1)}), bf16[8,64,112]{2,1,0:T(8,128)(2,1)S(1)}, u32[]{:S(2)}, u32[]{:S(2)}) async-start(bf16[8,64,112]{2,1,0:T(8,128)(2,1)} %pad_maximum_fusion.14), calls=%async_computation.6 | async-start | bytes 262144 | tf_op jit(solution)/shard_map/all_to_all | solution.py:107
  250.5 2.2 collective-permute-start.19
  253.1 18.5 %collective-permute-start.20 = (bf16[256,1024]{1,0:T(8,128)(2,1)S(1)}, bf16[256,1024]{1,0:T(8,128)(2,1)S(1)}, u32[]{:S(2)}, u32[]{:S(2)}) collective-permute-start(bf16[256,1024]{1,0:T(8,128)(2,1)S(1)} %merge_means.2), channel_id=1, source_target_pairs={{0,16},{8,24},{16,0},{24,8},{1,17},{9,25},{17,1},{25,9},{2,18},{10... | collective-permute-start | bytes 1572872 | tf_op jit(solution)/shard_map/ppermute | solution.py:40
  271.6 2.0 collective-permute-start.21
  275.0 20.6 %all-to-all-start.7 = ((bf16[8,32,1024]{2,1,0:T(8,128)(2,1)}), bf16[8,32,1024]{2,1,0:T(8,128)(2,1)S(1)}, u32[]{:S(2)}, u32[]{:S(2)}) async-start(bf16[8,32,1024]{2,1,0:T(8,128)(2,1)} %bitcast.48), calls=%async_computation.7 | async-start | bytes 1048576 | tf_op jit(solution)/shard_map/all_to_all | solution.py:107
  321.6 21.1 %all-to-all-start.9 = ((bf16[8,32,896]{2,1,0:T(8,128)(2,1)}), bf16[8,32,896]{2,1,0:T(8,128)(2,1)S(1)}, u32[]{:S(2)}, u32[]{:S(2)}) async-start(bf16[8,32,896]{2,1,0:T(8,128)(2,1)} %bitcast.54), calls=%async_computation.9 | async-start | bytes 917504 | tf_op jit(solution)/shard_map/all_to_all | solution.py:107
  325.7 4.3 collective-permute-start.22
  330.0 4.2 collective-permute-start.23
  353.0 27.7 %collective-permute-start.26 = (bf16[1,64,896]{2,1,0:T(8,128)(2,1)}, bf16[1,64,896]{2,1,0:T(8,128)(2,1)}, u32[]{:S(2)}, u32[]{:S(2)}) collective-permute-start(bf16[1,64,896]{2,1,0:T(8,128)(2,1)} %maximum_bitcast_fusion), channel_id=1, source_target_pairs={{0,2},{1,3},{2,0},{3,1},{4,6},{5,7},{6,4},{7,5},{8,10},{9,11},{10,... | collective-permute-start | bytes 344072 | tf_op jit(solution)/shard_map/ppermute | solution.py:40
  355.0 25.7 %collective-permute-start.27 = (bf16[1,64,896]{2,1,0:T(8,128)(2,1)}, bf16[1,64,896]{2,1,0:T(8,128)(2,1)}, u32[]{:S(2)}, u32[]{:S(2)}) collective-permute-start(bf16[1,64,896]{2,1,0:T(8,128)(2,1)} %maximum_bitcast_fusion), channel_id=1, source_target_pairs={{0,4},{1,5},{2,6},{3,7},{4,0},{5,1},{6,2},{7,3},{8,12},{9,13},{10,... | collective-permute-start | bytes 344072 | tf_op jit(solution)/shard_map/ppermute | solution.py:40
  357.4 23.3 %collective-permute-start.28 = (bf16[1,64,896]{2,1,0:T(8,128)(2,1)}, bf16[1,64,896]{2,1,0:T(8,128)(2,1)}, u32[]{:S(2)}, u32[]{:S(2)}) collective-permute-start(bf16[1,64,896]{2,1,0:T(8,128)(2,1)} %maximum_bitcast_fusion), channel_id=1, source_target_pairs={{0,6},{1,7},{2,4},{3,5},{4,2},{5,3},{6,0},{7,1},{8,14},{9,15},{10,... | collective-permute-start | bytes 344072 | tf_op jit(solution)/shard_map/ppermute | solution.py:40
  358.1 30.6 %collective-permute-start.25 = (bf16[304,896]{1,0:T(8,128)(2,1)S(1)}, bf16[304,896]{1,0:T(8,128)(2,1)}, u32[]{:S(2)}, u32[]{:S(2)}) collective-permute-start(bf16[304,896]{1,0:T(8,128)(2,1)S(1)} %get-tuple-element.258), channel_id=1, source_target_pairs={{0,8},{8,0},{16,24},{24,16},{1,9},{9,1},{17,25},{25,17},{2,10},{10... | collective-permute-start | bytes 1634312 | tf_op jit(solution)/shard_map/ppermute | solution.py:40
  358.1 38.7 %collective-permute-start.24 = (bf16[896,640]{1,0:T(8,128)(2,1)}, bf16[896,640]{1,0:T(8,128)(2,1)}, u32[]{:S(2)}, u32[]{:S(2)}) collective-permute-start(bf16[896,640]{1,0:T(8,128)(2,1)} %get-tuple-element.256), channel_id=1, source_target_pairs={{0,8},{8,0},{16,24},{24,16},{1,9},{9,1},{17,25},{25,17},{2,10},{10... | collective-permute-start | bytes 3440648 | tf_op jit(solution)/shard_map/ppermute | solution.py:40
  358.6 41.5 %all-to-all-start.10 = ((bf16[8,256,256]{2,1,0:T(8,128)(2,1)}), bf16[8,256,256]{2,1,0:T(8,128)(2,1)S(1)}, u32[]{:S(2)}, u32[]{:S(2)}) async-start(bf16[8,256,256]{2,1,0:T(8,128)(2,1)} %bitcast.58), calls=%async_computation.10 | async-start | bytes 2097152 | tf_op jit(solution)/shard_map/all_to_all | solution.py:107
  381.9 13.9 %collective-permute-start.29 = (bf16[4,64,896]{2,1,0:T(8,128)(2,1)S(1)}, bf16[4,64,896]{2,1,0:T(8,128)(2,1)S(1)}, u32[]{:S(2)}, u32[]{:S(2)}) collective-permute-start(bf16[4,64,896]{2,1,0:T(8,128)(2,1)S(1)} %pad_maximum_fusion.9), channel_id=1, source_target_pairs={{0,1},{1,0},{2,3},{3,2},{4,5},{5,4},{6,7},{7,6},{8,9},{9,8},{10,11... | collective-permute-start | bytes 1376264 | tf_op jit(solution)/shard_map/ppermute | solution.py:40
  406.4 17.7 %collective-permute-start.34 = (bf16[896,128]{1,0:T(8,128)(2,1)}, bf16[896,128]{1,0:T(8,128)(2,1)}, u32[]{:S(2)}, u32[]{:S(2)}) collective-permute-start(bf16[896,128]{1,0:T(8,128)(2,1)} %broadcast_select_fusion.12), channel_id=1, source_target_pairs={{0,8},{8,0},{16,24},{24,16},{1,9},{9,1},{17,25},{25,17},{2,10},{10... | collective-permute-start | bytes 688136 | tf_op jit(solution)/shard_map/ppermute | solution.py:40
  407.6 19.5 %collective-permute-start.32 = (bf16[112,896]{1,0:T(8,128)(2,1)}, bf16[112,896]{1,0:T(8,128)(2,1)}, u32[]{:S(2)}, u32[]{:S(2)}) collective-permute-start(bf16[112,896]{1,0:T(8,128)(2,1)} %get-tuple-element.401), channel_id=1, source_target_pairs={{0,8},{8,0},{16,24},{24,16},{1,9},{9,1},{17,25},{25,17},{2,10},{10... | collective-permute-start | bytes 602120 | tf_op jit(solution)/shard_map/ppermute | solution.py:40
  408.1 40.8 %collective-permute-start.31 = (bf16[152,896]{1,0:T(8,128)(2,1)S(1)}, bf16[152,896]{1,0:T(8,128)(2,1)}, u32[]{:S(2)}, u32[]{:S(2)}) collective-permute-start(bf16[152,896]{1,0:T(8,128)(2,1)S(1)} %copy-done.63), channel_id=1, source_target_pairs={{0,16},{8,24},{16,0},{24,8},{1,17},{9,25},{17,1},{25,9},{2,18},{10... | collective-permute-start | bytes 817160 | tf_op jit(solution)/shard_map/ppermute | solution.py:40
  408.7 48.5 %collective-permute-start.30 = (bf16[8,56,640]{2,1,0:T(8,128)(2,1)}, bf16[8,56,640]{2,1,0:T(8,128)(2,1)}, u32[]{:S(2)}, u32[]{:S(2)}) collective-permute-start(bf16[8,56,640]{2,1,0:T(8,128)(2,1)} %fusion.4), channel_id=1, source_target_pairs={{0,16},{8,24},{16,0},{24,8},{1,17},{9,25},{17,1},{25,9},{2,18},{10... | collective-permute-start | bytes 1720328 | tf_op jit(solution)/shard_map/ppermute | solution.py:40
  417.2 46.6 %all-to-all-start.11 = ((bf16[32,16,896]{2,1,0:T(8,128)(2,1)}), bf16[32,16,896]{2,1,0:T(8,128)(2,1)S(1)}, u32[]{:S(2)}, u32[]{:S(2)}) async-start(bf16[32,16,896]{2,1,0:T(8,128)(2,1)} %bitcast.67), calls=%async_computation.11 | async-start | bytes 1835008 | tf_op jit(solution)/shard_map/all_to_all | solution.py:107
  425.3 13.7 %collective-permute-start.35 = (bf16[8,56,128]{2,1,0:T(8,128)(2,1)S(1)}, bf16[8,56,128]{2,1,0:T(8,128)(2,1)S(1)}, u32[]{:S(2)}, u32[]{:S(2)}) collective-permute-start(bf16[8,56,128]{2,1,0:T(8,128)(2,1)S(1)} %select_bitcast_fusion.10), channel_id=1, source_target_pairs={{0,16},{8,24},{16,0},{24,8},{1,17},{9,25},{17,1},{25,9},{2,18},{10... | collective-permute-start | bytes 344072 | tf_op jit(solution)/shard_map/ppermute | solution.py:40
  439.0 9.8 %collective-permute-start.36 = (bf16[4,56,128]{2,1,0:T(8,128)(2,1)S(1)}, bf16[4,56,128]{2,1,0:T(8,128)(2,1)S(1)}, u32[]{:S(2)}, u32[]{:S(2)}) collective-permute-start(bf16[4,56,128]{2,1,0:T(8,128)(2,1)S(1)} %broadcast_select_fusion.17), channel_id=1, source_target_pairs={{0,4},{1,5},{2,6},{3,7},{4,0},{5,1},{6,2},{7,3},{8,12},{9,13},{10,... | collective-permute-start | bytes 172040 | tf_op jit(solution)/shard_map/ppermute | solution.py:40
  444.1 10.2 %collective-permute-start.33 = (bf16[56,896]{1,0:T(8,128)(2,1)S(1)}, bf16[56,896]{1,0:T(8,128)(2,1)S(1)}, u32[]{:S(2)}, u32[]{:S(2)}) collective-permute-start(bf16[56,896]{1,0:T(8,128)(2,1)S(1)} %broadcast_select_fusion.16), channel_id=1, source_target_pairs={{0,16},{8,24},{16,0},{24,8},{1,17},{9,25},{17,1},{25,9},{2,18},{10... | collective-permute-start | bytes 301064 | tf_op jit(solution)/shard_map/ppermute | solution.py:40
  448.8 3.9 collective-permute-start.37
  452.8 3.8 collective-permute-start.38
  491.1 23.1 %all-to-all-start.13 = ((bf16[8,56,640]{2,1,0:T(8,128)(2,1)}), bf16[8,56,640]{2,1,0:T(8,128)(2,1)S(1)}, u32[]{:S(2)}, u32[]{:S(2)}) async-start(bf16[8,56,640]{2,1,0:T(8,128)(2,1)} %get-tuple-element.290), calls=%async_computation.13 | async-start | bytes 1146880 | tf_op jit(solution)/shard_map/all_to_all | solution.py:107
  514.8 22.5 %collective-permute-start.39 = (bf16[56,4864]{1,0:T(8,128)(2,1)S(1)}, bf16[56,4864]{1,0:T(8,128)(2,1)S(1)}, u32[]{:S(2)}, u32[]{:S(2)}) collective-permute-start(bf16[56,4864]{1,0:T(8,128)(2,1)S(1)} %reshape.285), channel_id=1, source_target_pairs={{0,16},{8,24},{16,0},{24,8},{1,17},{9,25},{17,1},{25,9},{2,18},{10... | collective-permute-start | bytes 1634312 | tf_op jit(solution)/shard_map/ppermute | solution.py:40
  515.5 20.7 %collective-permute-start.41 = (bf16[56,1024]{1,0:T(8,128)(2,1)S(1)}, bf16[56,1024]{1,0:T(8,128)(2,1)S(1)}, u32[]{:S(2)}, u32[]{:S(2)}) collective-permute-start(bf16[56,1024]{1,0:T(8,128)(2,1)S(1)} %constant_dynamic-update-slice_fusion.10), channel_id=1, source_target_pairs={{0,16},{8,24},{16,0},{24,8},{1,17},{9,25},{17,1},{25,9},{2,18},{10... | collective-permute-start | bytes 344072 | tf_op jit(solution)/shard_map/ppermute | solution.py:40
  517.0 20.1 %collective-permute-start.40 = (bf16[152,896]{1,0:T(8,128)(2,1)S(1)}, bf16[152,896]{1,0:T(8,128)(2,1)S(1)}, u32[]{:S(2)}, u32[]{:S(2)}) collective-permute-start(bf16[152,896]{1,0:T(8,128)(2,1)S(1)} %get-tuple-element.299), channel_id=1, source_target_pairs={{0,16},{8,24},{16,0},{24,8},{1,17},{9,25},{17,1},{25,9},{2,18},{10... | collective-permute-start | bytes 817160 | tf_op jit(solution)/shard_map/ppermute | solution.py:40
  537.5 11.8 %collective-permute-start.44 = (bf16[112,1024]{1,0:T(8,128)(2,1)S(1)}, bf16[112,1024]{1,0:T(8,128)(2,1)S(1)}, u32[]{:S(2)}, u32[]{:S(2)}) collective-permute-start(bf16[112,1024]{1,0:T(8,128)(2,1)S(1)} %pad_maximum_fusion.12), channel_id=1, source_target_pairs={{0,8},{8,0},{16,24},{24,16},{1,9},{9,1},{17,25},{25,17},{2,10},{10... | collective-permute-start | bytes 688136 | tf_op jit(solution)/shard_map/ppermute | solution.py:40
  537.5 12.1 %collective-permute-start.42 = (bf16[112,4864]{1,0:T(8,128)(2,1)S(1)}, bf16[112,4864]{1,0:T(8,128)(2,1)S(1)}, u32[]{:S(2)}, u32[]{:S(2)}) collective-permute-start(bf16[112,4864]{1,0:T(8,128)(2,1)S(1)} %pad_maximum_fusion.5), channel_id=1, source_target_pairs={{0,8},{8,0},{16,24},{24,16},{1,9},{9,1},{17,25},{25,17},{2,10},{10... | collective-permute-start | bytes 3268616 | tf_op jit(solution)/shard_map/ppermute | solution.py:40
  538.7 10.6 %collective-permute-start.43 = (bf16[2,152,896]{2,1,0:T(8,128)(2,1)S(1)}, bf16[2,152,896]{2,1,0:T(8,128)(2,1)S(1)}, u32[]{:S(2)}, u32[]{:S(2)}) collective-permute-start(bf16[2,152,896]{2,1,0:T(8,128)(2,1)S(1)} %pad_maximum_fusion.8), channel_id=1, source_target_pairs={{0,8},{8,0},{16,24},{24,16},{1,9},{9,1},{17,25},{25,17},{2,10},{10... | collective-permute-start | bytes 1634312 | tf_op jit(solution)/shard_map/ppermute | solution.py:40
  (83 other events, 954.7 us)
Sparse Core Ops, SparseCore 0:
  26.3 54.6 all-gather.2

commit v3 on v2

--- a/solution.py
+++ b/solution.py
@@ -128,25 +128,24 @@
     return total_of(cut(first, second, axis, mask))
 
 
+def collect(blocks, axis, stages):
+    held = blocks
+    for masks in reversed(stages):
+        count = len(masks) + 1
+        held = held.reshape((count, held.shape[0] // count) + held.shape[1:])
+        held = total_of(
+            [held[0]] + [partner(held[at + 1], axis, mask) for at, mask in enumerate(masks)]
+        )
+    return held[0]
+
+
+def ordered(value, other, axis, mask):
+    own = bit_of(axis, mask)
+    return jnp.where(own, other, value), jnp.where(own, value, other)
+
+
 def double(value, axis, mask):
-    own = bit_of(axis, mask)
-    other = partner(value, axis, mask)
-    return jnp.where(own, other, value), jnp.where(own, value, other)
-
-
-def all_sum(value):
-    for axis in ("batch", "seq"):
-        for mask in masks_of(lax.axis_size(axis)):
-            value = value + partner(value, axis, mask)
-    return value
-
-
-def sum_seq(blocks):
-    held = blocks
-    for mask in reversed(masks_of(blocks.shape[0])):
-        half = held.shape[0] // 2
-        held = halve(held[:half], held[half:], "seq", mask)
-    return held[0]
+    return ordered(value, partner(value, axis, mask), axis, mask)
 
 
 def dot_nn(left, right):
@@ -700,6 +699,27 @@
     out_ref[...] = 2.0 * jnp.sum(cross, axis=1, keepdims=True) + jnp.sum(
         jnp.sum(same, axis=0, keepdims=True), axis=1, keepdims=True
     )
+
+
+def norm_body(parts_ref, totals_ref, stats_ref):
+    totals = jnp.sum(parts_ref[...], axis=0)
+    totals_ref[...] = totals
+    last = totals.shape[0] - 1
+    own = totals[last:]
+    lane = iota(own.shape, 1)
+
+    def entry(at):
+        return jnp.sum(jnp.where(lane == at, own, 0.0), axis=1, keepdims=True)
+
+    others = jnp.where(iota(totals.shape, 0) < last, totals * totals, 0.0)
+    squares = entry(0) + jnp.sum(
+        jnp.sum(others, axis=0, keepdims=True), axis=1, keepdims=True
+    )
+    count = jnp.maximum(entry(2), 1.0)
+    norm = jnp.sqrt(squares) / count
+    factor = jnp.minimum(1.0, CLIP_NORM / (norm + 1e-06)) / count
+    out = jnp.where(lane == 0, entry(1), jnp.where(lane == 1, count, norm))
+    stats_ref[...] = jnp.where(lane == 3, factor, out)
 
 
 def head_grad_body(
@@ -870,9 +890,10 @@
     )
     sent_requests = exchange(requests.reshape(owners, capacity), both)
 
+    stages = seq_stages_of(seq_count)
     core_row = lax.axis_index("batch") & core_mask
     qkv_cut = -(-(q_width + 2 * kv_width) // (2 * LANES)) * LANES
-    out_cut = -(-width // (2 * LANES)) * LANES + LANES
+    out_cut = -(-width // (2 * LANES)) * LANES
 
     def part_of(value, columns):
         start = jnp.where(on_core, value.shape[1] - columns, 0)
@@ -881,18 +902,24 @@
     def widened(value):
         return jnp.pad(value, [(0, 0)] * (value.ndim - 1) + [(0, ff_wide - ff_part)])
 
-    proj_parts = lax.all_gather(
-        jnp.concatenate([part_of(w_qkv, qkv_cut), part_of(w_out, out_cut)], axis=1), "seq", axis=0
-    )
-    stages = seq_stages_of(seq_count)
-    w_kv_full = spread(w_qkv[:, q_width:].astype(low), "seq", stages)
+    proj_parts = spread(
+        jnp.concatenate([part_of(w_qkv, qkv_cut), part_of(w_out, out_cut)], axis=1),
+        "seq",
+        stages[:-1],
+    )
+    my_kv = lax.dynamic_slice(
+        w_qkv, (0, jnp.where(on_core, q_width + kv_width, q_width)), (shard, kv_width)
+    ).astype(low)
+    my_kv = jnp.concatenate([my_kv[:half], my_kv[half:]], axis=1)
     pieces = jnp.transpose(part_of(w_gateup, FF).reshape(half, seq_count, ff_part), (1, 0, 2))
-    pieces = xor_order(widened(pieces), "seq")
+    pieces = jnp.concatenate(
+        [widened(pieces), jnp.broadcast_to(my_kv[None], (seq_count,) + my_kv.shape)], axis=2
+    )
     w_down_low = jnp.pad(w_down.astype(low), ((0, ff_wide - ff_part), (0, 0)))
-    sent_requests, pieces, w_down_low, w_kv_full = together(
-        sent_requests, pieces, w_down_low, w_kv_full
-    )
-    w_kv_full = to_index_order(w_kv_full, "seq", stages).reshape(width, 2 * kv_width)
+    sent_requests, pieces, w_down_low, proj_parts = together(
+        sent_requests, pieces, w_down_low, proj_parts
+    )
+    proj_others = [partner(proj_parts, "seq", mask) for mask in stages[-1]]
 
     def far_rows(value):
         return jnp.stack(double(value, "batch", far_mask), axis=1).reshape(width, -1)
@@ -903,16 +930,28 @@
 
     wanted = sent_requests.reshape(-1)
     found = embed.at[wanted].get(mode="promise_in_bounds").astype(low)
-    returned = exchange(found.reshape(owners, capacity, width), both)
-    pieces = [pieces[0]] + [partner(pieces[at], "seq", at) for at in range(1, seq_count)]
-    returned, pieces, proj_parts, w_kv_full = together(returned, pieces, proj_parts, w_kv_full)
+    found, pieces, proj_parts, proj_others = together(
+        found.reshape(owners, capacity, width), exchange(pieces, "seq"), proj_parts, proj_others
+    )
+    returned = exchange(found, both)
+    my_kv = pieces[..., ff_wide:].reshape(seq_count, half, 2, kv_width)
+    my_kv = jnp.transpose(my_kv, (0, 2, 1, 3)).reshape(width, kv_width)
+    other_kv = partner(my_kv, "batch", core_mask)
+    my_gu = pieces[..., :ff_wide]
+    proj_parts = to_index_order(jnp.concatenate([proj_parts] + proj_others), "seq", stages)
+    my_q = proj_parts[..., :qkv_cut]
+    other_q = partner(my_q, "batch", far_mask)
+    out_parts = proj_parts[..., qkv_cut:]
+    returned, my_kv, other_kv, my_gu, my_q, other_q, out_parts = together(
+        returned, my_kv, other_kv, my_gu, my_q, other_q, out_parts
+    )
+    w_kv_full = jnp.concatenate(ordered(my_kv, other_kv, "batch", core_mask), axis=1)
+    w_q_far = jnp.stack(ordered(my_q, other_q, "batch", far_mask), axis=1)
+    w_q_far = w_q_far.reshape(width, qkv_cut)
     returned = returned.reshape(owners * capacity, width)
-    w_q_far = far_rows(proj_parts[..., :qkv_cut])
     w_q_full = core_columns(w_q_far, q_width + 2 * kv_width)[:, :q_width]
-    out_short = out_cut - LANES
-    out_parts = proj_parts[..., qkv_cut:]
-    out_parts = jnp.where(on_core, out_parts[..., LANES:], out_parts[..., :out_short])
     w_out_far = far_rows(out_parts)
+    other_gu = partner(after(my_gu, w_out_far), "batch", far_mask)
 
     places = seq_index * local_len + jnp.arange(local_len, dtype=jnp.int32)
     pick_places = seq_index * local_len + picks
@@ -944,7 +983,6 @@
     )
     kv_all = exchange(kv_low, "seq")
     w_out_full = core_columns(w_out_far, width)
-    gu_columns = xor_order(jnp.stack(pieces), "seq")
     picked_zero, target_rows, normed_picked, queries = in_vmem(
         pick_body,
         [
@@ -957,10 +995,12 @@
         "scored_queries",
         flops=2 * n_picks * width * (q_width + 3 * local_len),
     )
-    kv_all, picked_zero, target_rows, normed_picked, queries, w_out_full, gu_columns = together(
-        kv_all, picked_zero, target_rows, normed_picked, queries, w_out_full, gu_columns
-    )
-    gu_columns = far_rows(gu_columns)
+    kv_all, picked_zero, target_rows, normed_picked, queries, w_out_full, my_gu, other_gu = together(
+        kv_all, picked_zero, target_rows, normed_picked, queries, w_out_full, my_gu, other_gu
+    )
+    gu_columns = jnp.stack(ordered(my_gu, other_gu, "batch", far_mask), axis=1)
+    gu_columns = gu_columns.reshape(width, ff_wide)
+    gu_others = partner(gu_columns, "batch", core_mask)
     kv_all = kv_all.reshape(seq_count * local_len, 2 * kv_width)
     length = kv_all.shape[0]
     limit = 24
@@ -983,13 +1023,13 @@
     def shard_columns(value):
         return jnp.transpose(value.reshape(n_picks, seq_count, shard), (1, 0, 2))
 
-    w_gate, w_up = double(gu_columns, "batch", core_mask)
-    normed_two_all, w_gate, w_up, column_pieces = together(
+    normed_two_all, gu_columns, gu_others, column_pieces = together(
         exchange(normed_two, "seq"),
-        w_gate,
-        w_up,
+        gu_columns,
+        gu_others,
         jnp.concatenate([shard_columns(normed_picked), shard_columns(mixed)], axis=1),
     )
+    w_gate, w_up = ordered(gu_columns, gu_others, "batch", core_mask)
     normed_two_all = normed_two_all.reshape(row_count, width)
     gate_part, up_part, hidden, down_part = in_vmem(
         feed_body,
@@ -1134,8 +1174,6 @@
         kept=(1, 2, 3, 4, 5, 6, 7),
         scratch=[pltpu.VMEM((n_picks, q_width), f32)],
     )
-    own_parts = exchange(kv_grad.reshape(seq_count, local_len, 2 * kv_width), "seq")
-
     def far_cut(value):
         return cut(value[..., 0, :, :], value[..., 1, :, :], "batch", far_mask)
 
@@ -1143,18 +1181,22 @@
         front, back = value[..., 0, :, :], value[..., 1, :, :]
         return jnp.where(on_far, back, front), jnp.where(on_far, front, back)
 
+    gu_own, down_own, kv_grad = together(gu_own, down_own, kv_grad)
+    own_parts = exchange(kv_grad.reshape(seq_count, local_len, 2 * kv_width), "seq")
     gu_parts = far_sides(total_of([gu_own, gu_other]).reshape(seq_count, 2, half, ff_wide))
     down_parts = far_sides(total_of([down_own, down_other]).reshape(2, -1, width))
-    grad_head, more_squares = head_grad(
-        *head_args[:2], after(rows, kv_grad), *head_args[3:],
-        head_cut, head_blocks - head_cut, (grad_head,),
-    )
-    late_rows = spread(jnp.concatenate([query_pre, grad_one_low], axis=0), "seq", stages)
-    own_parts, gu_parts, down_parts, grad_head, more_squares, late_rows = together(
-        own_parts, gu_parts, down_parts, grad_head, more_squares, late_rows
-    )
+    gu_parts, down_parts, rows_late = together(gu_parts, down_parts, rows)
     gu_parts = gu_parts[0], partner(gu_parts[1], "batch", far_mask)
     down_parts = down_parts[0], partner(down_parts[1], "batch", far_mask)
+    grad_head, more_squares = head_grad(
+        *head_args[:2], rows_late, *head_args[3:],
+        head_cut, head_blocks - head_cut, (grad_head,),
+    )
+    late_rows = spread(jnp.concatenate([query_pre, grad_one_low], axis=0), "seq", stages[:-1])
+    late_others = [partner(late_rows, "seq", mask) for mask in stages[-1]]
+    own_parts, gu_parts, down_parts, grad_head, more_squares, late_rows, late_others = together(
+        own_parts, gu_parts, down_parts, grad_head, more_squares, late_rows, late_others
+    )
     kv_pre, sendback, grad_gain_zero, kv_bias = in_vmem(
         zero_back_body,
         [
@@ -1186,6 +1228,7 @@
     grad_head, sendback = together(grad_head, sendback)
     arrived = exchange(sendback.reshape(owners, capacity, width), both)
     head_rows = grad_head.at[wanted].get(mode="promise_in_bounds")
+    late_rows = jnp.concatenate([late_rows] + late_others)
     q_half = dot_tn(
         gathered_columns[:, :n_picks].reshape(row_count, shard),
         late_rows[:, :n_picks].reshape(row_count, q_width),
@@ -1197,8 +1240,14 @@
     proj_part = halve(q_half.astype(low), out_half.astype(low), "batch", core_mask)
     proj_part = total_of(far_cut(proj_part.reshape(2, half, width)))
     kv_w_grad = dot_tn(normed_one, kv_pre).astype(low)
-    kv_part = halve(kv_w_grad[:, :kv_width], kv_w_grad[:, kv_width:], "batch", core_mask)
-    kv_part = sum_seq(total_of(far_cut(kv_part.reshape(seq_count, 2, half, kv_width))))
+    kv_blocks = jnp.transpose(
+        kv_w_grad.reshape(seq_count, 2, half, 2, kv_width), (1, 3, 0, 2, 4)
+    ).reshape(batch_count, seq_count, half, kv_width)
+    kv_blocks = xor_order(kv_blocks, "batch")
+    kv_part = total_of(
+        [kv_blocks[0]] + [partner(kv_blocks[at], "batch", at) for at in range(1, batch_count)]
+    )
+    kv_part = collect(to_xor_order(kv_part, "seq", stages), "seq", stages)
     own_squares = (
         squares_of(gu_part)
         + squares_of(down_part_w)
@@ -1226,18 +1275,16 @@
             jnp.zeros((LANES - 3,), f32),
         ]
     ).reshape(-1, LANES)
-    summary = jnp.sum(exchange_copies(summary, both), axis=0).reshape(-1)
-    grad_gains = summary[: 3 * width].reshape(3, width)
-    grad_bias_all = summary[3 * width : -LANES]
-    squares, loss_sum = summary[-LANES], summary[1 - LANES]
-    token_count = jnp.maximum(summary[2 - LANES], 1.0)
-    grad_norm = (
-        jnp.sqrt(
-            squares + jnp.sum(grad_gains * grad_gains) + jnp.sum(grad_bias_all * grad_bias_all)
-        )
-        / token_count
-    )
-    factor = jnp.minimum(1.0, CLIP_NORM / (grad_norm + 1e-06)) / token_count
+    totals, stats = in_vmem(
+        norm_body,
+        [like(summary.shape), like((1, LANES))],
+        [exchange_copies(summary, both)],
+        "grad_norm",
+    )
+    totals = totals.reshape(-1)
+    grad_gains = totals[: 3 * width].reshape(3, width)
+    grad_bias_all = totals[3 * width : -LANES]
+    loss_sum, token_count, grad_norm, factor = (stats[0, at] for at in range(4))
 
     block = 608
     blocks = -(-vrows // block)

time: 583 us -> 528 us (0.906)
  waiting for transfers between devices: 116 us -> 91.1 us
  between operations: 26.9 us -> 8.51 us
  starting transfers between devices: 108 us -> 99.6 us
    ppermute x45 -> x41, waiting for transfers between devices: 88.5 us -> 57.8 us  [partner(): lax.ppermute(value, axis, [(place, place ^ mask) for place in range(size)])]
    ppermute x45 -> x41, starting transfers between devices: 56.4 us -> 39.6 us  [partner(): lax.ppermute(value, axis, [(place, place ^ mask) for place in range(size)])]
    unnamed x198 -> x172, local copies, waits for them, and re-layouts: 20.5 us -> 11.7 us
    all_to_all x10 -> x11, starting transfers between devices: 51.8 us -> 60 us  [exchange(): return lax.all_to_all(value, axes, split_axis=0, concat_axis=0, tiled=True)]
    all_to_all x10 -> x11, waiting for transfers between devices: 27.7 us -> 33.4 us  [exchange(): return lax.all_to_all(value, axes, split_axis=0, concat_axis=0, tiled=True)]
    pallas_call x15 -> x16, Pallas kernels: 38 us -> 37.4 us  [in_vmem(): pl.pallas_call(body, grid=(1,), in_specs=[pl.BlockSpec(a.shape, whole(a.n...]
  transfers between devices with their start and end apart: 56 -> 52, of which waited for: 21 -> 17; matrix products, arithmetic and copies ran while one was open for 11% -> 11% of each run, Pallas kernels for 20% -> 24%
where the time goes in v3:
time: 528 us; the launch traced here: 520 us
  Pallas kernels  143 us (27%)
  starting transfers between devices  99.6 us (19%)
  waiting for transfers between devices  91.1 us (17%)
  blocking collectives  80 us (15%)
  other arithmetic  53.2 us (10%)
  local copies, waits for them, and re-layouts  42.8 us (8%)
  between operations  8.51 us (2%)
    all_to_all x4, blocking collectives, exchange(): return lax.all_to_all(value, axes, split_axis=0, concat_axis=0, tiled=True)  80 us
    all_to_all x11, starting transfers between devices, exchange(): return lax.all_to_all(value, axes, split_axis=0, concat_axis=0, tiled=True)  60 us
    ppermute x41, waiting for transfers between devices, partner(): lax.ppermute(value, axis, [(place, place ^ mask) for place in range(size)])  57.8 us
    pallas_call x3, Pallas kernels, table_adam(): pl.pallas_call(functools.partial(table_adam_body, first), grid=(steps,),...  49.7 us
    ppermute x41, starting transfers between devices, partner(): lax.ppermute(value, axis, [(place, place ^ mask) for place in range(size)])  39.6 us
    pallas_call x16, Pallas kernels, in_vmem(): pl.pallas_call(body, grid=(1,), in_specs=[pl.BlockSpec(a.shape, whole(a.n...  37.4 us
    pallas_call x2, Pallas kernels, head_part(): pl.pallas_call(functools.partial(head_body, vrows), grid=(steps,), in_spe...  34.3 us
    all_to_all x11, waiting for transfers between devices, exchange(): return lax.all_to_all(value, axes, split_axis=0, concat_axis=0, tiled=True)  33.4 us
  transfers between devices with their start and end apart: 52, of which 17 were waited for; matrix products, arithmetic and copies ran while one was open for 11% of the time, Pallas kernels for 24%

profile of v3, /device:TPU:0, one launch (start us, length us, event | category | flops | bytes accessed | tf_op | source)
XLA Modules:
  0.0 520.1 jit_solution(7072374656443801736)
XLA Ops:
  2.6 3.1 collective-permute-start
  5.6 2.6 collective-permute-start.1
  11.1 6.1 %all-to-all-start = ((s32[32,1,16]{2,1,0:T(1,128)}), s32[32,1,16]{2,1,0:T(1,128)S(1)}, u32[]{:S(2)}, u32[]{:S(2)}) async-start(s32[32,1,16]{2,1,0:T(1,128)} %bitcast), calls=%async_computation | async-start | bytes 32768 | tf_op jit(solution)/shard_map/all_to_all | solution.py:107
  18.0 2.1 dynamic_slice.20
  20.1 2.0 reshape.262
  25.5 5.8 %all-to-all-start.1 = ((bf16[8,56,896]{2,1,0:T(8,128)(2,1)}), bf16[8,56,896]{2,1,0:T(8,128)(2,1)S(1)}, u32[]{:S(2)}, u32[]{:S(2)}) async-start(bf16[8,56,896]{2,1,0:T(8,128)(2,1)} %fusion.5), calls=%async_computation.1 | async-start | bytes 1605632 | tf_op jit(solution)/shard_map/all_to_all | solution.py:107
  32.0 2.1 collective-permute-start.3
  34.1 2.4 fusion.36
  36.6 9.1 %gather_fusion = bf16[512,896]{1,0:T(8,128)(2,1)} fusion(f32[4748,896]{1,0:T(8,128)} %w_ref.5, s32[1024]{0:T(1024)S(1)} %pad_clamp_fusion), kind=kCustom, calls=%fused_computation | custom fusion | bytes 1837056 | tf_op jit(solution)/shard_map/gather | solution.py:932
  45.7 8.0 %collective-permute-done.3 = bf16[4,56,1152]{2,1,0:T(8,128)(2,1)S(1)} collective-permute-done((bf16[4,56,1152]{2,1,0:T(8,128)(2,1)S(1)}, bf16[4,56,1152]{2,1,0:T(8,128)(2,1)S(1)}, u32[]{:S(2)}, u32[]{:S(2)}) %collective-permute-start.3) | collective-permute-done | bytes 516128 | tf_op jit(solution)/shard_map/ppermute | solution.py:40
  53.7 4.5 all-to-all-start.2
  59.0 1.8 collective-permute-start.5
  63.2 20.1 %collective-permute-done.5 = bf16[8,56,640]{2,1,0:T(8,128)(2,1)} collective-permute-done((bf16[8,56,640]{2,1,0:T(8,128)(2,1)S(1)}, bf16[8,56,640]{2,1,0:T(8,128)(2,1)}, u32[]{:S(2)}, u32[]{:S(2)}) %collective-permute-start.5) | collective-permute-done | bytes 573472 | tf_op jit(solution)/shard_map/ppermute | solution.py:40
  86.2 2.0 keys_values.1
  89.0 5.9 %all-to-all-start.3 = ((bf16[8,256,256]{2,1,0:T(8,128)(2,1)}), bf16[8,256,256]{2,1,0:T(8,128)(2,1)S(1)}, u32[]{:S(2)}, u32[]{:S(2)}) async-start(bf16[8,256,256]{2,1,0:T(8,128)(2,1)} %get-tuple-element.199), calls=%async_computation.3 | async-start | bytes 2097152 | tf_op jit(solution)/shard_map/all_to_all | solution.py:107
  104.2 8.7 %collective-permute-done.9 = bf16[8,56,640]{2,1,0:T(8,128)(2,1)} collective-permute-done((bf16[8,56,640]{2,1,0:T(8,128)(2,1)}, bf16[8,56,640]{2,1,0:T(8,128)(2,1)}, u32[]{:S(2)}, u32[]{:S(2)}) %collective-permute-start.9) | collective-permute-done | bytes 573472 | tf_op jit(solution)/shard_map/ppermute | solution.py:40
  112.9 8.5 %all-to-all-done.3 = bf16[8,256,256]{2,1,0:T(8,128)(2,1)S(1)} async-done(((bf16[8,256,256]{2,1,0:T(8,128)(2,1)}), bf16[8,256,256]{2,1,0:T(8,128)(2,1)S(1)}, u32[]{:S(2)}, u32[]{:S(2)}) %all-to-all-start.3) | async-done | bytes 1048608 | tf_op jit(solution)/shard_map/all_to_all | solution.py:107
  121.4 1.7 select_bitcast_fusion.1
  124.3 3.5 attention.1
  128.5 3.7 all-to-all-start.4
  133.2 12.8 %all-to-all-done.4 = bf16[8,32,896]{2,1,0:T(8,128)(2,1)S(1)} async-done(((bf16[8,32,896]{2,1,0:T(8,128)(2,1)}), bf16[8,32,896]{2,1,0:T(8,128)(2,1)S(1)}, u32[]{:S(2)}, u32[]{:S(2)}) %all-to-all-start.4) | async-done | bytes 458784 | tf_op jit(solution)/shard_map/all_to_all | solution.py:107
  146.0 2.0 broadcast_select_fusion.1
  148.0 3.4 feed_forward.1
  151.5 16.8 %all_to_all.82.parts_ref = bf16[8,32,896]{2,1,0:T(8,128)(2,1)S(1)} all-to-all(bf16[8,32,896]{2,1,0:T(8,128)(2,1)S(1)} %bitcast.165), channel_id=1, replica_groups=mesh['batch'=4,'seq'=8] {'seq'}, dimensions={0} | all-to-all | bytes 917504 | tf_op jit(solution)/shard_map/all_to_all | solution.py:107
  170.0 2.7 collective-permute-done.11
  172.8 25.2 %all_to_all.83.rows_ref.refs_4_ = bf16[8,2,32,896]{3,2,1,0:T(8,128)(2,1)S(1)} all-to-all(bf16[8,2,32,896]{3,2,1,0:T(8,128)(2,1)S(1)} %broadcast_in_dim.59), channel_id=1, replica_groups=mesh['batch'=4,'seq'=8] {'seq'}, dimensions={0} | all-to-all | bytes 1835008 | tf_op jit(solution)/shard_map/all_to_all | solution.py:107
  198.2 3.6 all-to-all-start.7
  201.8 17.3 %head_part.2 = (bf16[512,5120]{1,0:T(8,128)(2,1)}, f32[512,128]{1,0:T(8,128)S(1)}, bf16[256,1024]{1,0:T(8,128)(2,1)S(1)}, bf16[256,1024]{1,0:T(8,128)(2,1)S(1)}) custom-call(bf16[8,2,32,896]{3,2,1,0:T(8,128)(2,1)S(1)} %all_to_all.83.rows_ref.refs_4_, bf16[8,2,32,896]{3,2,1,0:T(8,128)(2,1)S(1)} %collective-permute-done.12.other_ref.refs_5_, f32[4748,896]{1,0:T(8,128)} %w_ref.5), custom_call_target="tpu_custom_call" | custom-call | flops 8712617984 | bytes 21878784 | tf_op jit(solution)/shard_map/head_part/pallas_call | solution.py:500
  223.8 17.0 %head_part.3 = (bf16[512,5120]{1,0:T(8,128)(2,1)}, f32[512,128]{1,0:T(8,128)S(1)}, bf16[256,1024]{1,0:T(8,128)(2,1)S(1)}, bf16[256,1024]{1,0:T(8,128)(2,1)S(1)}) custom-call(bf16[8,2,32,896]{3,2,1,0:T(8,128)(2,1)S(1)} %all_to_all.83.rows_ref.refs_4_, bf16[8,2,32,896]{3,2,1,0:T(8,128)(2,1)S(1)} %collective-permute-done.12.other_ref.refs_5_, f32[4748,896]{1,0:T(8,128)} %w_ref.5), custom_call_target="tpu_custom_call" | custom-call | flops 8712617984 | bytes 21878784 | tf_op jit(solution)/shard_map/head_part/pallas_call | solution.py:500
  241.0 1.8 collective-permute-done.15.refs_1_
  244.1 5.8 %all-to-all-start.8 = ((bf16[8,32,1024]{2,1,0:T(8,128)(2,1)}), bf16[8,32,1024]{2,1,0:T(8,128)(2,1)S(1)}, u32[]{:S(2)}, u32[]{:S(2)}) async-start(bf16[8,32,1024]{2,1,0:T(8,128)(2,1)} %bitcast.31), calls=%async_computation.8 | async-start | bytes 1048576 | tf_op jit(solution)/shard_map/all_to_all | solution.py:107
  252.7 12.1 %all-to-all-done.8.parts_ref = bf16[8,32,1024]{2,1,0:T(8,128)(2,1)S(1)} async-done(((bf16[8,32,1024]{2,1,0:T(8,128)(2,1)}), bf16[8,32,1024]{2,1,0:T(8,128)(2,1)S(1)}, u32[]{:S(2)}, u32[]{:S(2)}) %all-to-all-start.8) | async-done | bytes 524320 | tf_op jit(solution)/shard_map/all_to_all | solution.py:107
  266.2 18.1 %all_to_all.84 = bf16[8,32,1024]{2,1,0:T(8,128)(2,1)S(1)} all-to-all(bf16[8,32,1024]{2,1,0:T(8,128)(2,1)S(1)} %get-tuple-element.247), channel_id=1, replica_groups=mesh['batch'=4,'seq'=8] {'seq'}, dimensions={0} | all-to-all | bytes 1048576 | tf_op jit(solution)/shard_map/all_to_all | solution.py:107
  284.3 4.9 feed_forward_back.1
  290.7 4.1 all-to-all-start.10
  295.4 3.7 collective-permute-done.16
  299.2 3.4 layer_grads.1
  303.3 7.7 %head_grad.2 = (bf16[4748,896]{1,0:T(8,128)(2,1)}, f32[8,896]{1,0:T(8,128)S(1)}) custom-call(bf16[512,5120]{1,0:T(8,128)(2,1)} %get-tuple-element.258.refs_0_, bf16[512,5120]{1,0:T(8,128)(2,1)} %get-tuple-element.259.refs_1_, f32[512,128]{1,0:T(8,128)} %copy-done.21, f32[512,128]{1,0:T(8,128)} %copy-done.22, bf16[8,2,32,896]{3,2,1,0:T(8,128)(2,1)} %copy-done.6, ...), custom_call_target="tpu_custom_call" | custom-call | flops 2818572288 | bytes 5898240 | tf_op jit(solution)/shard_map/head_grad/pallas_call | solution.py:762
  313.5 8.0 %attention_back.1 = (bf16[2048,256]{1,0:T(8,128)(2,1)}, bf16[32,896]{1,0:T(8,128)(2,1)S(1)}, f32[1,896]{1,0:T(1,128)S(1)}) custom-call(bf16[32,896]{1,0:T(8,128)(2,1)S(1)} %get-tuple-element.268.grad_ref, bf16[896,896]{1,0:T(8,128)(2,1)} %copy-done.1, bf16[32,896]{1,0:T(8,128)(2,1)} %copy-done.24, bf16[2048,256]{1,0:T(8,128)(2,1)} %bitcast.158, ...), custom_call_target="tpu_custom_call" | custom-call | flops 587202560 | bytes 4025984 | tf_op jit(solution)/shard_map/attention_back/pallas_call | solution.py:207
  321.5 2.1 collective-permute-start.22
  323.6 2.4 collective-permute-start.23
  326.1 6.1 %all-to-all-start.11 = ((bf16[8,256,256]{2,1,0:T(8,128)(2,1)}), bf16[8,256,256]{2,1,0:T(8,128)(2,1)S(1)}, u32[]{:S(2)}, u32[]{:S(2)}) async-start(bf16[8,256,256]{2,1,0:T(8,128)(2,1)} %bitcast.41), calls=%async_computation.11 | async-start | bytes 2097152 | tf_op jit(solution)/shard_map/all_to_all | solution.py:107
  332.9 2.6 collective-permute-done.23
  340.1 1.6 add_convert_fusion
  344.7 14.1 %head_grad.3 = (bf16[4748,896]{1,0:T(8,128)(2,1)}, f32[8,896]{1,0:T(8,128)S(1)}) custom-call(bf16[512,5120]{1,0:T(8,128)(2,1)} %get-tuple-element.258.refs_0_, bf16[512,5120]{1,0:T(8,128)(2,1)} %get-tuple-element.259.refs_1_, f32[512,128]{1,0:T(8,128)} %copy-done.21, f32[512,128]{1,0:T(8,128)} %copy-done.22, ...), custom_call_target="tpu_custom_call", output_to_operand_aliasing={{0}: (8, {})} | custom-call | flops 6576668672 | bytes 13762560 | tf_op jit(solution)/shard_map/head_grad/pallas_call | solution.py:762
  358.8 2.9 collective-permute-done.21
  362.5 5.2 first_norm_back.1
  372.7 10.6 %all-to-all-start.12 = ((bf16[32,16,896]{2,1,0:T(8,128)(2,1)}), bf16[32,16,896]{2,1,0:T(8,128)(2,1)S(1)}, u32[]{:S(2)}, u32[]{:S(2)}) async-start(bf16[32,16,896]{2,1,0:T(8,128)(2,1)} %bitcast.50), calls=%async_computation.12 | async-start | bytes 1835008 | tf_op jit(solution)/shard_map/all_to_all | solution.py:107
  383.3 2.7 multiply_reduce_fusion
  386.8 7.1 %gather_fusion.1 = bf16[512,896]{1,0:T(8,128)(2,1)S(1)} fusion(bf16[4748,896]{1,0:T(8,128)(2,1)} %get-tuple-element.296.grad_ref, s32[1024]{0:T(1024)S(1)} %pad_clamp_fusion), kind=kCustom, calls=%fused_computation.1 | custom fusion | bytes 1837056 | tf_op jit(solution)/shard_map/gather | solution.py:1230
  396.4 1.8 collective-permute-start.31
  398.8 1.8 collective-permute-done.31
  400.7 2.0 collective-permute-start.32
  402.7 3.3 collective-permute-start.33
  408.5 2.9 collective-permute-done.34
  418.2 19.8 %all_to_all.85.parts_ref = f32[32,31,128]{2,1,0:T(8,128)S(1)} all-to-all(f32[32,31,128]{2,1,0:T(8,128)S(1)} %broadcast_in_dim.65), channel_id=1, replica_groups=mesh['batch'=4,'seq'=8] {'batch','seq'}, dimensions={0} | all-to-all | bytes 1015808 | tf_op jit(solution)/shard_map/all_to_all | solution.py:107
  438.8 3.8 all-to-all-start.14
  443.3 19.3 %table_adam.3 = (f32[4748,896]{1,0:T(8,128)}, f32[4748,896]{1,0:T(8,128)}, f32[4748,896]{1,0:T(8,128)}) custom-call(f32[1]{0:T(128)} %bitcast.74.scale_ref, s32[1,512]{1,0:T(1,128)S(1)} %broadcast_in_dim_reshape.2.names_ref, bf16[512,896]{1,0:T(8,128)(2,1)S(1)} %bitcast.154, bf16[4748,896]{1,0:T(8,128)(2,1)} %get-tuple-element.296.grad_ref, ...), custom_call_target="tpu_custom_call" | custom-call | flops 1673527296 | bytes 42491904 | tf_op jit(solution)/shard_map/table_adam/pallas_call | solution.py:807
  466.6 19.3 %table_adam.4 = (f32[4748,896]{1,0:T(8,128)}, f32[4748,896]{1,0:T(8,128)}, f32[4748,896]{1,0:T(8,128)}) custom-call(f32[1]{0:T(128)} %bitcast.74.scale_ref, s32[1,512]{1,0:T(1,128)S(1)} %broadcast_in_dim_reshape.2.names_ref, bf16[512,896]{1,0:T(8,128)(2,1)S(1)} %bitcast.155, ...), custom_call_target="tpu_custom_call", output_to_operand_aliasing={{0}: (7, {}), {1}: (8, {}), {2}: (9, {})} | custom-call | flops 1673527296 | bytes 42491904 | tf_op jit(solution)/shard_map/table_adam/pallas_call | solution.py:807
  488.6 11.2 %table_adam.5 = (f32[4748,896]{1,0:T(8,128)}, f32[4748,896]{1,0:T(8,128)}, f32[4748,896]{1,0:T(8,128)}) custom-call(f32[1]{0:T(128)} %bitcast.74.scale_ref, s32[1,512]{1,0:T(1,128)S(1)} %broadcast_in_dim_reshape.2.names_ref, bf16[512,896]{1,0:T(8,128)(2,1)S(1)} %bitcast.156, ...), custom_call_target="tpu_custom_call", output_to_operand_aliasing={{0}: (7, {}), {1}: (8, {}), {2}: (9, {})} | custom-call | flops 1115684864 | bytes 28327936 | tf_op jit(solution)/shard_map/table_adam/pallas_call | solution.py:807
  503.3 5.4 %multiply_subtract_fusion.1 = (f32[608,896]{1,0:T(8,128)}, f32[608,896]{1,0:T(8,128)}, f32[608,896]{1,0:T(8,128)}) fusion(f32[608,896]{1,0:T(8,128)S(1)} %copy-done.42, f32[]{:T(128)} %bitcast.73, bf16[608,896]{1,0:T(8,128)(2,1)S(1)} %bitcast.179, f32[608,896]{1,0:T(8,128)S(1)} %copy-done.44, f32[608,896]{1,0:T(8,128)S(1)} %copy-done.45), kind=kLoop, calls=%fused_computation.11 | loop fusion | flops 9261056 | bytes 14163972 | tf_op jit(solution)/shard_map/sub | solution.py:178
  508.8 7.0 %multiply_subtract_fusion = (f32[112,9728]{1,0:T(8,128)}, f32[112,9728]{1,0:T(8,128)}, f32[112,9728]{1,0:T(8,128)}) fusion(f32[112,9728]{1,0:T(8,128)S(1)} %bitcast.174, f32[]{:T(128)} %bitcast.73, bf16[112,9728]{1,0:T(8,128)(2,1)S(1)} %pad_maximum_fusion, f32[112,9728]{1,0:T(8,128)S(1)} %bitcast.176, f32[112,9728]{1,0:T(8,128)S(1)} %bitcast.178), kind=kLoop, calls=%fused_computation.4 | loop fusion | flops 18522112 | bytes 28327940 | tf_op jit(solution)/shard_map/sub | solution.py:178
  515.8 2.0 multiply_subtract_fusion.3
  517.8 2.0 multiply_subtract_fusion.2
  (381 shorter events, 78.4 us)
Async XLA Ops:
  2.6 21.9 %collective-permute-start = (bf16[1,56,1152]{2,1,0:T(8,128)(2,1)S(1)}, bf16[1,56,1152]{2,1,0:T(8,128)(2,1)S(1)}, u32[]{:S(2)}, u32[]{:S(2)}) collective-permute-start(bf16[1,56,1152]{2,1,0:T(8,128)(2,1)S(1)} %maximum_bitcast_fusion), channel_id=1, source_target_pairs={{0,2},{1,3},{2,0},{3,1},{4,6},{5,7},{6,4},{7,5},{8,10},{9,11},{10,... | collective-permute-start | bytes 387080 | tf_op jit(solution)/shard_map/ppermute | solution.py:40
  5.6 18.8 %collective-permute-start.1 = (bf16[1,56,1152]{2,1,0:T(8,128)(2,1)S(1)}, bf16[1,56,1152]{2,1,0:T(8,128)(2,1)S(1)}, u32[]{:S(2)}, u32[]{:S(2)}) collective-permute-start(bf16[1,56,1152]{2,1,0:T(8,128)(2,1)S(1)} %maximum_bitcast_fusion), channel_id=1, source_target_pairs={{0,4},{1,5},{2,6},{3,7},{4,0},{5,1},{6,2},{7,3},{8,12},{9,13},{10,... | collective-permute-start | bytes 387080 | tf_op jit(solution)/shard_map/ppermute | solution.py:40
  8.2 16.2 %collective-permute-start.2 = (bf16[1,56,1152]{2,1,0:T(8,128)(2,1)S(1)}, bf16[1,56,1152]{2,1,0:T(8,128)(2,1)}, u32[]{:S(2)}, u32[]{:S(2)}) collective-permute-start(bf16[1,56,1152]{2,1,0:T(8,128)(2,1)S(1)} %maximum_bitcast_fusion), channel_id=1, source_target_pairs={{0,6},{1,7},{2,4},{3,5},{4,2},{5,3},{6,0},{7,1},{8,14},{9,15},{10,... | collective-permute-start | bytes 387080 | tf_op jit(solution)/shard_map/ppermute | solution.py:40
  9.2 77.0 %copy-start.15 = (bf16[256,512]{1,0:T(8,128)(2,1)}, bf16[256,512]{1,0:T(8,128)(2,1)S(1)}, u32[]{:S(2)}) copy-start(bf16[256,512]{1,0:T(8,128)(2,1)S(1)} %get-tuple-element.196.placer_ref) | copy-start | bytes 786436
  11.1 14.4 %all-to-all-start = ((s32[32,1,16]{2,1,0:T(1,128)}), s32[32,1,16]{2,1,0:T(1,128)S(1)}, u32[]{:S(2)}, u32[]{:S(2)}) async-start(s32[32,1,16]{2,1,0:T(1,128)} %bitcast), calls=%async_computation | async-start | bytes 32768 | tf_op jit(solution)/shard_map/all_to_all | solution.py:107
  25.5 28.2 %all-to-all-start.1 = ((bf16[8,56,896]{2,1,0:T(8,128)(2,1)}), bf16[8,56,896]{2,1,0:T(8,128)(2,1)S(1)}, u32[]{:S(2)}, u32[]{:S(2)}) async-start(bf16[8,56,896]{2,1,0:T(8,128)(2,1)} %fusion.5), calls=%async_computation.1 | async-start | bytes 1605632 | tf_op jit(solution)/shard_map/all_to_all | solution.py:107
  32.0 54.2 %copy-start.33 = (f32[1,896]{1,0:T(1,128)}, f32[1,896]{1,0:T(1,128)S(1)}, u32[]{:S(2)}) copy-start(f32[1,896]{1,0:T(1,128)S(1)} %get-tuple-element.419.gain_ref) | copy-start | bytes 10756
  32.0 92.3 %copy-start.34 = (f32[1,896]{1,0:T(1,128)}, f32[1,896]{1,0:T(1,128)S(1)}, u32[]{:S(2)}) copy-start(f32[1,896]{1,0:T(1,128)S(1)} %get-tuple-element.418.gain_ref) | copy-start | bytes 10756
  32.0 136.3 %copy-start.35 = (f32[1,896]{1,0:T(1,128)}, f32[1,896]{1,0:T(1,128)S(1)}, u32[]{:S(2)}) copy-start(f32[1,896]{1,0:T(1,128)S(1)} %get-tuple-element.417.gain_ref) | copy-start | bytes 10756
  32.0 21.6 %collective-permute-start.3 = (bf16[4,56,1152]{2,1,0:T(8,128)(2,1)S(1)}, bf16[4,56,1152]{2,1,0:T(8,128)(2,1)S(1)}, u32[]{:S(2)}, u32[]{:S(2)}) collective-permute-start(bf16[4,56,1152]{2,1,0:T(8,128)(2,1)S(1)} %pad_maximum_fusion.10), channel_id=1, source_target_pairs={{0,1},{1,0},{2,3},{3,2},{4,5},{5,4},{6,7},{7,6},{8,9},{9,8},{10,11... | collective-permute-start | bytes 1548296 | tf_op jit(solution)/shard_map/ppermute | solution.py:40
  36.5 87.8 %copy-start.37 = (s32[1,32]{1,0:T(1,128)}, s32[1,32]{1,0:T(1,128)S(1)}, u32[]{:S(2)}) copy-start(s32[1,32]{1,0:T(1,128)S(1)} %get-tuple-element.372.place_ref) | copy-start | bytes 388
  53.7 29.6 %all-to-all-start.2 = ((bf16[32,16,896]{2,1,0:T(8,128)(2,1)}), bf16[32,16,896]{2,1,0:T(8,128)(2,1)S(1)}, u32[]{:S(2)}, u32[]{:S(2)}) async-start(bf16[32,16,896]{2,1,0:T(8,128)(2,1)} %bitcast.5), calls=%async_computation.2 | async-start | bytes 1835008 | tf_op jit(solution)/shard_map/all_to_all | solution.py:107
  59.0 24.3 %collective-permute-start.5 = (bf16[8,56,640]{2,1,0:T(8,128)(2,1)S(1)}, bf16[8,56,640]{2,1,0:T(8,128)(2,1)}, u32[]{:S(2)}, u32[]{:S(2)}) collective-permute-start(bf16[8,56,640]{2,1,0:T(8,128)(2,1)S(1)} %slice.212), channel_id=1, source_target_pairs={{0,16},{8,24},{16,0},{24,8},{1,17},{9,25},{17,1},{25,9},{2,18},{10... | collective-permute-start | bytes 1720328 | tf_op jit(solution)/shard_map/ppermute | solution.py:40
  60.9 1.6 collective-permute-start.4
  61.5 24.7 %copy-start.13 = (f32[256,128]{1,0:T(8,128)}, f32[256,128]{1,0:T(8,128)S(1)}, u32[]{:S(2)}) copy-start(f32[256,128]{1,0:T(8,128)S(1)} %get-tuple-element.420.sin_ref) | copy-start | bytes 393220
  61.6 24.7 %copy-start.14 = (f32[256,128]{1,0:T(8,128)}, f32[256,128]{1,0:T(8,128)S(1)}, u32[]{:S(2)}) copy-start(f32[256,128]{1,0:T(8,128)S(1)} %get-tuple-element.421.cos_ref) | copy-start | bytes 393220
  62.5 23.6 %copy-start.71 = (f32[1152]{0:T(1024)S(1)}, f32[1152]{0:T(1024)}, u32[]{:S(2)}) copy-start(f32[1152]{0:T(1024)} %param.53) | copy-start | bytes 13828
  83.3 12.2 %collective-permute-start.7 = (bf16[8,56,512]{2,1,0:T(8,128)(2,1)S(1)}, bf16[8,56,512]{2,1,0:T(8,128)(2,1)}, u32[]{:S(2)}, u32[]{:S(2)}) collective-permute-start(bf16[8,56,512]{2,1,0:T(8,128)(2,1)S(1)} %slice.213), channel_id=1, source_target_pairs={{0,16},{8,24},{16,0},{24,8},{1,17},{9,25},{17,1},{25,9},{2,18},{10... | collective-permute-start | bytes 1376264 | tf_op jit(solution)/shard_map/ppermute | solution.py:40
  86.0 12.3 %collective-permute-start.6 = (bf16[896,640]{1,0:T(8,128)(2,1)}, bf16[896,640]{1,0:T(8,128)(2,1)}, u32[]{:S(2)}, u32[]{:S(2)}) collective-permute-start(bf16[896,640]{1,0:T(8,128)(2,1)} %bitcast.16), channel_id=1, source_target_pairs={{0,8},{8,0},{16,24},{24,16},{1,9},{9,1},{17,25},{25,17},{2,10},{10... | collective-permute-start | bytes 3440648 | tf_op jit(solution)/shard_map/ppermute | solution.py:40
  89.0 32.3 %all-to-all-start.3 = ((bf16[8,256,256]{2,1,0:T(8,128)(2,1)}), bf16[8,256,256]{2,1,0:T(8,128)(2,1)S(1)}, u32[]{:S(2)}, u32[]{:S(2)}) async-start(bf16[8,256,256]{2,1,0:T(8,128)(2,1)} %get-tuple-element.199), calls=%async_computation.3 | async-start | bytes 2097152 | tf_op jit(solution)/shard_map/all_to_all | solution.py:107
  96.9 6.9 %collective-permute-start.8 = (bf16[896,512]{1,0:T(8,128)(2,1)S(1)}, bf16[896,512]{1,0:T(8,128)(2,1)S(1)}, u32[]{:S(2)}, u32[]{:S(2)}) collective-permute-start(bf16[896,512]{1,0:T(8,128)(2,1)S(1)} %bitcast.171), channel_id=1, source_target_pairs={{0,8},{8,0},{16,24},{24,16},{1,9},{9,1},{17,25},{25,17},{2,10},{10... | collective-permute-start | bytes 2752520 | tf_op jit(solution)/shard_map/ppermute | solution.py:40
  97.1 15.8 %collective-permute-start.9 = (bf16[8,56,640]{2,1,0:T(8,128)(2,1)}, bf16[8,56,640]{2,1,0:T(8,128)(2,1)}, u32[]{:S(2)}, u32[]{:S(2)}) collective-permute-start(bf16[8,56,640]{2,1,0:T(8,128)(2,1)} %slice.162), channel_id=1, source_target_pairs={{0,16},{8,24},{16,0},{24,8},{1,17},{9,25},{17,1},{25,9},{2,18},{10... | collective-permute-start | bytes 1720328 | tf_op jit(solution)/shard_map/ppermute | solution.py:40
  124.3 21.6 %collective-permute-start.10 = (bf16[896,640]{1,0:T(8,128)(2,1)}, bf16[896,640]{1,0:T(8,128)(2,1)}, u32[]{:S(2)}, u32[]{:S(2)}) collective-permute-start(bf16[896,640]{1,0:T(8,128)(2,1)} %bitcast.24), channel_id=1, source_target_pairs={{0,8},{8,0},{16,24},{24,16},{1,9},{9,1},{17,25},{25,17},{2,10},{10... | collective-permute-start | bytes 3440648 | tf_op jit(solution)/shard_map/ppermute | solution.py:40
  128.5 39.8 %copy-start.19 = (f32[32,896]{1,0:T(8,128)}, f32[32,896]{1,0:T(8,128)S(1)}, u32[]{:S(2)}) copy-start(f32[32,896]{1,0:T(8,128)S(1)} %get-tuple-element.225.one_ref) | copy-start | bytes 344068
  128.5 17.4 %all-to-all-start.4 = ((bf16[8,32,896]{2,1,0:T(8,128)(2,1)}), bf16[8,32,896]{2,1,0:T(8,128)(2,1)S(1)}, u32[]{:S(2)}, u32[]{:S(2)}) async-start(bf16[8,32,896]{2,1,0:T(8,128)(2,1)} %get-tuple-element.215), calls=%async_computation.4 | async-start | bytes 917504 | tf_op jit(solution)/shard_map/all_to_all | solution.py:107
  151.4 46.6 %copy-start.17 = (f32[256,640]{1,0:T(8,128)}, f32[256,640]{1,0:T(8,128)S(1)}, u32[]{:S(2)}) copy-start(f32[256,640]{1,0:T(8,128)S(1)} %get-tuple-element.249.gate_ref) | copy-start | bytes 1966084
  151.4 46.6 %copy-start.18 = (f32[256,640]{1,0:T(8,128)}, f32[256,640]{1,0:T(8,128)S(1)}, u32[]{:S(2)}) copy-start(f32[256,640]{1,0:T(8,128)S(1)} %get-tuple-element.250.up_ref) | copy-start | bytes 1966084
  168.5 4.2 collective-permute-start.11
  198.1 25.7 %copy-start.6 = (bf16[8,2,32,896]{3,2,1,0:T(8,128)(2,1)}, bf16[8,2,32,896]{3,2,1,0:T(8,128)(2,1)S(1)}, u32[]{:S(2)}) copy-start(bf16[8,2,32,896]{3,2,1,0:T(8,128)(2,1)S(1)} %all_to_all.83.rows_ref.refs_4_) | copy-start | bytes 2752516
  198.1 3.7 collective-permute-start.12
  198.2 21.7 %all-to-all-start.7 = ((bf16[8,64,112]{2,1,0:T(8,128)(2,1)}), bf16[8,64,112]{2,1,0:T(8,128)(2,1)S(1)}, u32[]{:S(2)}, u32[]{:S(2)}) async-start(bf16[8,64,112]{2,1,0:T(8,128)(2,1)} %pad_maximum_fusion.15), calls=%async_computation.7 | async-start | bytes 262144 | tf_op jit(solution)/shard_map/all_to_all | solution.py:107
  219.8 2.0 collective-permute-start.13
  222.2 18.6 %collective-permute-start.14 = (bf16[256,1024]{1,0:T(8,128)(2,1)S(1)}, bf16[256,1024]{1,0:T(8,128)(2,1)S(1)}, u32[]{:S(2)}, u32[]{:S(2)}) collective-permute-start(bf16[256,1024]{1,0:T(8,128)(2,1)S(1)} %merge_means.2), channel_id=1, source_target_pairs={{0,16},{8,24},{16,0},{24,8},{1,17},{9,25},{17,1},{25,9},{2,18},{10... | collective-permute-start | bytes 1572872 | tf_op jit(solution)/shard_map/ppermute | solution.py:40
  240.8 2.0 collective-permute-start.15
  244.1 20.6 %all-to-all-start.8 = ((bf16[8,32,1024]{2,1,0:T(8,128)(2,1)}), bf16[8,32,1024]{2,1,0:T(8,128)(2,1)S(1)}, u32[]{:S(2)}, u32[]{:S(2)}) async-start(bf16[8,32,1024]{2,1,0:T(8,128)(2,1)} %bitcast.31), calls=%async_computation.8 | async-start | bytes 1048576 | tf_op jit(solution)/shard_map/all_to_all | solution.py:107
  290.7 20.4 %all-to-all-start.10 = ((bf16[8,32,896]{2,1,0:T(8,128)(2,1)}), bf16[8,32,896]{2,1,0:T(8,128)(2,1)S(1)}, u32[]{:S(2)}, u32[]{:S(2)}) async-start(bf16[8,32,896]{2,1,0:T(8,128)(2,1)} %bitcast.37), calls=%async_computation.10 | async-start | bytes 917504 | tf_op jit(solution)/shard_map/all_to_all | solution.py:107
  294.8 4.3 collective-permute-start.16
  299.1 3.5 collective-permute-start.17
  311.1 29.0 %collective-permute-start.18 = (bf16[896,640]{1,0:T(8,128)(2,1)}, bf16[896,640]{1,0:T(8,128)(2,1)}, u32[]{:S(2)}, u32[]{:S(2)}) collective-permute-start(bf16[896,640]{1,0:T(8,128)(2,1)} %get-tuple-element.273), channel_id=1, source_target_pairs={{0,8},{8,0},{16,24},{24,16},{1,9},{9,1},{17,25},{25,17},{2,10},{10... | collective-permute-start | bytes 3440648 | tf_op jit(solution)/shard_map/ppermute | solution.py:40
  311.6 26.5 %collective-permute-start.19 = (bf16[304,896]{1,0:T(8,128)(2,1)S(1)}, bf16[304,896]{1,0:T(8,128)(2,1)}, u32[]{:S(2)}, u32[]{:S(2)}) collective-permute-start(bf16[304,896]{1,0:T(8,128)(2,1)S(1)} %get-tuple-element.275), channel_id=1, source_target_pairs={{0,8},{8,0},{16,24},{24,16},{1,9},{9,1},{17,25},{25,17},{2,10},{10... | collective-permute-start | bytes 1634312 | tf_op jit(solution)/shard_map/ppermute | solution.py:40
  321.5 11.4 %collective-permute-start.22 = (bf16[1,64,896]{2,1,0:T(8,128)(2,1)S(1)}, bf16[1,64,896]{2,1,0:T(8,128)(2,1)}, u32[]{:S(2)}, u32[]{:S(2)}) collective-permute-start(bf16[1,64,896]{2,1,0:T(8,128)(2,1)S(1)} %maximum_bitcast_fusion.1), channel_id=1, source_target_pairs={{0,2},{1,3},{2,0},{3,1},{4,6},{5,7},{6,4},{7,5},{8,10},{9,11},{10,... | collective-permute-start | bytes 344072 | tf_op jit(solution)/shard_map/ppermute | solution.py:40
  323.6 11.9 %collective-permute-start.23 = (bf16[1,64,896]{2,1,0:T(8,128)(2,1)S(1)}, bf16[1,64,896]{2,1,0:T(8,128)(2,1)}, u32[]{:S(2)}, u32[]{:S(2)}) collective-permute-start(bf16[1,64,896]{2,1,0:T(8,128)(2,1)S(1)} %maximum_bitcast_fusion.1), channel_id=1, source_target_pairs={{0,4},{1,5},{2,6},{3,7},{4,0},{5,1},{6,2},{7,3},{8,12},{9,13},{10,... | collective-permute-start | bytes 344072 | tf_op jit(solution)/shard_map/ppermute | solution.py:40
  325.9 9.6 %collective-permute-start.24 = (bf16[1,64,896]{2,1,0:T(8,128)(2,1)S(1)}, bf16[1,64,896]{2,1,0:T(8,128)(2,1)}, u32[]{:S(2)}, u32[]{:S(2)}) collective-permute-start(bf16[1,64,896]{2,1,0:T(8,128)(2,1)S(1)} %maximum_bitcast_fusion.1), channel_id=1, source_target_pairs={{0,6},{1,7},{2,4},{3,5},{4,2},{5,3},{6,0},{7,1},{8,14},{9,15},{10,... | collective-permute-start | bytes 344072 | tf_op jit(solution)/shard_map/ppermute | solution.py:40
  326.1 35.6 %all-to-all-start.11 = ((bf16[8,256,256]{2,1,0:T(8,128)(2,1)}), bf16[8,256,256]{2,1,0:T(8,128)(2,1)S(1)}, u32[]{:S(2)}, u32[]{:S(2)}) async-start(bf16[8,256,256]{2,1,0:T(8,128)(2,1)} %bitcast.41), calls=%async_computation.11 | async-start | bytes 2097152 | tf_op jit(solution)/shard_map/all_to_all | solution.py:107
  336.6 22.2 %collective-permute-start.25 = (bf16[4,64,896]{2,1,0:T(8,128)(2,1)S(1)}, bf16[4,64,896]{2,1,0:T(8,128)(2,1)S(1)}, u32[]{:S(2)}, u32[]{:S(2)}) collective-permute-start(bf16[4,64,896]{2,1,0:T(8,128)(2,1)S(1)} %pad_maximum_fusion.12), channel_id=1, source_target_pairs={{0,1},{1,0},{2,3},{3,2},{4,5},{5,4},{6,7},{7,6},{8,9},{9,8},{10,11... | collective-permute-start | bytes 1376264 | tf_op jit(solution)/shard_map/ppermute | solution.py:40
  342.6 19.1 %collective-permute-start.20 = (bf16[8,56,640]{2,1,0:T(8,128)(2,1)S(1)}, bf16[8,56,640]{2,1,0:T(8,128)(2,1)S(1)}, u32[]{:S(2)}, u32[]{:S(2)}) collective-permute-start(bf16[8,56,640]{2,1,0:T(8,128)(2,1)S(1)} %fusion.6), channel_id=1, source_target_pairs={{0,16},{8,24},{16,0},{24,8},{1,17},{9,25},{17,1},{25,9},{2,18},{10... | collective-permute-start | bytes 1720328 | tf_op jit(solution)/shard_map/ppermute | solution.py:40
  343.2 18.5 %collective-permute-start.21 = (bf16[152,896]{1,0:T(8,128)(2,1)S(1)}, bf16[152,896]{1,0:T(8,128)(2,1)S(1)}, u32[]{:S(2)}, u32[]{:S(2)}) collective-permute-start(bf16[152,896]{1,0:T(8,128)(2,1)S(1)} %get-tuple-element.279), channel_id=1, source_target_pairs={{0,16},{8,24},{16,0},{24,8},{1,17},{9,25},{17,1},{25,9},{2,18},{10... | collective-permute-start | bytes 817160 | tf_op jit(solution)/shard_map/ppermute | solution.py:40
  369.2 26.0 %collective-permute-start.28 = (bf16[8,56,128]{2,1,0:T(8,128)(2,1)}, bf16[8,56,128]{2,1,0:T(8,128)(2,1)}, u32[]{:S(2)}, u32[]{:S(2)}) collective-permute-start(bf16[8,56,128]{2,1,0:T(8,128)(2,1)} %get-tuple-element.403), channel_id=1, source_target_pairs={{0,8},{8,0},{16,24},{24,16},{1,9},{9,1},{17,25},{25,17},{2,10},{10... | collective-permute-start | bytes 344072 | tf_op jit(solution)/shard_map/ppermute | solution.py:40
  369.2 26.0 %collective-permute-start.29 = (bf16[8,56,128]{2,1,0:T(8,128)(2,1)}, bf16[8,56,128]{2,1,0:T(8,128)(2,1)}, u32[]{:S(2)}, u32[]{:S(2)}) collective-permute-start(bf16[8,56,128]{2,1,0:T(8,128)(2,1)} %get-tuple-element.405), channel_id=1, source_target_pairs={{0,16},{8,24},{16,0},{24,8},{1,17},{9,25},{17,1},{25,9},{2,18},{10... | collective-permute-start | bytes 344072 | tf_op jit(solution)/shard_map/ppermute | solution.py:40
  369.8 25.4 %collective-permute-start.30 = (bf16[8,56,128]{2,1,0:T(8,128)(2,1)}, bf16[8,56,128]{2,1,0:T(8,128)(2,1)}, u32[]{:S(2)}, u32[]{:S(2)}) collective-permute-start(bf16[8,56,128]{2,1,0:T(8,128)(2,1)} %get-tuple-element.404), channel_id=1, source_target_pairs={{0,24},{8,16},{16,8},{24,0},{1,25},{9,17},{17,9},{25,1},{2,26},{10... | collective-permute-start | bytes 344072 | tf_op jit(solution)/shard_map/ppermute | solution.py:40
  372.4 34.9 %collective-permute-start.26 = (bf16[112,896]{1,0:T(8,128)(2,1)}, bf16[112,896]{1,0:T(8,128)(2,1)S(1)}, u32[]{:S(2)}, u32[]{:S(2)}) collective-permute-start(bf16[112,896]{1,0:T(8,128)(2,1)} %get-tuple-element.428), channel_id=1, source_target_pairs={{0,8},{8,0},{16,24},{24,16},{1,9},{9,1},{17,25},{25,17},{2,10},{10... | collective-permute-start | bytes 602120 | tf_op jit(solution)/shard_map/ppermute | solution.py:40
  372.7 42.7 %all-to-all-start.12 = ((bf16[32,16,896]{2,1,0:T(8,128)(2,1)}), bf16[32,16,896]{2,1,0:T(8,128)(2,1)S(1)}, u32[]{:S(2)}, u32[]{:S(2)}) async-start(bf16[32,16,896]{2,1,0:T(8,128)(2,1)} %bitcast.50), calls=%async_computation.12 | async-start | bytes 1835008 | tf_op jit(solution)/shard_map/all_to_all | solution.py:107
  396.4 4.2 collective-permute-start.31
  400.7 7.8 %collective-permute-start.32 = (bf16[1,56,128]{2,1,0:T(8,128)(2,1)S(1)}, bf16[1,56,128]{2,1,0:T(8,128)(2,1)S(1)}, u32[]{:S(2)}, u32[]{:S(2)}) collective-permute-start(bf16[1,56,128]{2,1,0:T(8,128)(2,1)S(1)} %get-tuple-element.412), channel_id=1, source_target_pairs={{0,2},{1,3},{2,0},{3,1},{4,6},{5,7},{6,4},{7,5},{8,10},{9,11},{10,... | collective-permute-start | bytes 43016 | tf_op jit(solution)/shard_map/ppermute | solution.py:40
  402.7 5.8 %collective-permute-start.33 = (bf16[1,56,128]{2,1,0:T(8,128)(2,1)S(1)}, bf16[1,56,128]{2,1,0:T(8,128)(2,1)S(1)}, u32[]{:S(2)}, u32[]{:S(2)}) collective-permute-start(bf16[1,56,128]{2,1,0:T(8,128)(2,1)S(1)} %get-tuple-element.414), channel_id=1, source_target_pairs={{0,4},{1,5},{2,6},{3,7},{4,0},{5,1},{6,2},{7,3},{8,12},{9,13},{10,... | collective-permute-start | bytes 43016 | tf_op jit(solution)/shard_map/ppermute | solution.py:40
  405.9 5.5 %collective-permute-start.34 = (bf16[1,56,128]{2,1,0:T(8,128)(2,1)S(1)}, bf16[1,56,128]{2,1,0:T(8,128)(2,1)S(1)}, u32[]{:S(2)}, u32[]{:S(2)}) collective-permute-start(bf16[1,56,128]{2,1,0:T(8,128)(2,1)S(1)} %get-tuple-element.413), channel_id=1, source_target_pairs={{0,6},{1,7},{2,4},{3,5},{4,2},{5,3},{6,0},{7,1},{8,14},{9,15},{10,... | collective-permute-start | bytes 43016 | tf_op jit(solution)/shard_map/ppermute | solution.py:40
  407.4 4.7 collective-permute-start.27
  438.8 24.4 %all-to-all-start.14 = ((bf16[8,56,640]{2,1,0:T(8,128)(2,1)}), bf16[8,56,640]{2,1,0:T(8,128)(2,1)S(1)}, u32[]{:S(2)}, u32[]{:S(2)}) async-start(bf16[8,56,640]{2,1,0:T(8,128)(2,1)} %get-tuple-element.313), calls=%async_computation.14 | async-start | bytes 1146880 | tf_op jit(solution)/shard_map/all_to_all | solution.py:107
  463.8 22.5 %collective-permute-start.35 = (bf16[56,4864]{1,0:T(8,128)(2,1)S(1)}, bf16[56,4864]{1,0:T(8,128)(2,1)S(1)}, u32[]{:S(2)}, u32[]{:S(2)}) collective-permute-start(bf16[56,4864]{1,0:T(8,128)(2,1)S(1)} %reshape.292), channel_id=1, source_target_pairs={{0,16},{8,24},{16,0},{24,8},{1,17},{9,25},{17,1},{25,9},{2,18},{10... | collective-permute-start | bytes 1634312 | tf_op jit(solution)/shard_map/ppermute | solution.py:40
  464.5 21.4 %collective-permute-start.37 = (bf16[56,1024]{1,0:T(8,128)(2,1)S(1)}, bf16[56,1024]{1,0:T(8,128)(2,1)S(1)}, u32[]{:S(2)}, u32[]{:S(2)}) collective-permute-start(bf16[56,1024]{1,0:T(8,128)(2,1)S(1)} %constant_dynamic-update-slice_fusion.2), channel_id=1, source_target_pairs={{0,16},{8,24},{16,0},{24,8},{1,17},{9,25},{17,1},{25,9},{2,18},{10... | collective-permute-start | bytes 344072 | tf_op jit(solution)/shard_map/ppermute | solution.py:40
  466.0 20.1 %collective-permute-start.36 = (bf16[152,896]{1,0:T(8,128)(2,1)S(1)}, bf16[152,896]{1,0:T(8,128)(2,1)S(1)}, u32[]{:S(2)}, u32[]{:S(2)}) collective-permute-start(bf16[152,896]{1,0:T(8,128)(2,1)S(1)} %get-tuple-element.322), channel_id=1, source_target_pairs={{0,16},{8,24},{16,0},{24,8},{1,17},{9,25},{17,1},{25,9},{2,18},{10... | collective-permute-start | bytes 817160 | tf_op jit(solution)/shard_map/ppermute | solution.py:40
  486.5 13.3 %collective-permute-start.40 = (bf16[112,1024]{1,0:T(8,128)(2,1)S(1)}, bf16[112,1024]{1,0:T(8,128)(2,1)S(1)}, u32[]{:S(2)}, u32[]{:S(2)}) collective-permute-start(bf16[112,1024]{1,0:T(8,128)(2,1)S(1)} %pad_maximum_fusion.14), channel_id=1, source_target_pairs={{0,8},{8,0},{16,24},{24,16},{1,9},{9,1},{17,25},{25,17},{2,10},{10... | collective-permute-start | bytes 688136 | tf_op jit(solution)/shard_map/ppermute | solution.py:40
  486.6 13.6 %collective-permute-start.38 = (bf16[112,4864]{1,0:T(8,128)(2,1)S(1)}, bf16[112,4864]{1,0:T(8,128)(2,1)S(1)}, u32[]{:S(2)}, u32[]{:S(2)}) collective-permute-start(bf16[112,4864]{1,0:T(8,128)(2,1)S(1)} %pad_maximum_fusion.5), channel_id=1, source_target_pairs={{0,8},{8,0},{16,24},{24,16},{1,9},{9,1},{17,25},{25,17},{2,10},{10... | collective-permute-start | bytes 3268616 | tf_op jit(solution)/shard_map/ppermute | solution.py:40
  488.6 11.3 %collective-permute-start.39 = (bf16[2,152,896]{2,1,0:T(8,128)(2,1)S(1)}, bf16[2,152,896]{2,1,0:T(8,128)(2,1)S(1)}, u32[]{:S(2)}, u32[]{:S(2)}) collective-permute-start(bf16[2,152,896]{2,1,0:T(8,128)(2,1)S(1)} %pad_maximum_fusion.9), channel_id=1, source_target_pairs={{0,8},{8,0},{16,24},{24,16},{1,9},{9,1},{17,25},{25,17},{2,10},{10... | collective-permute-start | bytes 1634312 | tf_op jit(solution)/shard_map/ppermute | solution.py:40
  (73 other events, 585.8 us)

commit v4 on v3

--- a/solution.py
+++ b/solution.py
@@ -1288,7 +1288,7 @@
 
     block = 608
     blocks = -(-vrows // block)
-    cuts = [0, -(-blocks * 3 // 8), -(-blocks * 6 // 8), blocks]
+    cuts = [0, -(-blocks // 2), blocks]
 
     def update_rows(at, held, first):
         return table_adam(
@@ -1308,27 +1308,27 @@
     def both_halves(value, axis, mask, at):
         return jnp.concatenate(double(value, axis, mask), axis=at)
 
-    gu_rows = exchange(after(gu_part, factor), "seq")
-    gu_rows, embed_new, down_part_w, proj_part, kv_part = together(
-        gu_rows, update_rows(0, (), factor), down_part_w, proj_part, kv_part
+    gu_part, down_part_w, proj_part, kv_part, factor = together(
+        gu_part, down_part_w, proj_part, kv_part, factor
+    )
+    gu_rows = exchange(gu_part, "seq")
+    down_all = jnp.stack(double(down_part_w, "batch", far_mask), axis=0)
+    small = both_halves(jnp.concatenate([proj_part, kv_part], axis=1), "batch", far_mask, 0)
+    gu_rows, embed_new, down_all, small = together(
+        gu_rows, update_rows(0, (), factor), down_all, small
     )
     gu_rows = jnp.transpose(gu_rows[..., :ff_part], (1, 0, 2)).reshape(half, FF)
     gu_far = both_halves(gu_rows, "batch", far_mask, 0)
-    down_all = jnp.stack(double(down_part_w, "batch", far_mask), axis=0)
-    small = both_halves(jnp.concatenate([proj_part, kv_part], axis=1), "batch", far_mask, 0)
-    gu_far, down_all, small, embed_new = together(
-        gu_far, down_all, small, update_rows(1, tuple(embed_new), gu_rows)
-    )
-    gu_all = both_halves(gu_far, "batch", core_mask, 1)
     down_all = jnp.stack(double(down_all, "batch", core_mask), axis=0).reshape(w_down.shape)
     first_small, second_small = double(small, "batch", core_mask)
     qkv_all = jnp.concatenate(
         [first_small[:, :width], first_small[:, width:], second_small[:, width:]], axis=1
     )
     out_all = second_small[:, :width]
-    gu_all, down_all, qkv_all, out_all, embed_new = together(
-        gu_all, down_all, qkv_all, out_all, update_rows(2, tuple(embed_new), gu_far)
-    )
+    gu_far, down_all, qkv_all, out_all, embed_new = together(
+        gu_far, down_all, qkv_all, out_all, update_rows(1, tuple(embed_new), gu_rows)
+    )
+    gu_all = both_halves(gu_far, "batch", core_mask, 1)
 
     def update(weight, moment, second, gradient, rate):
         return adam(weight, moment, second, gradient.astype(f32) * factor, rate, DECAY)

time: 528 us -> 519 us (0.983)
  Pallas kernels: 143 us -> 137 us
    pallas_call x3 -> x2, Pallas kernels: 49.7 us -> 42.9 us  [table_adam(): pl.pallas_call(functools.partial(table_adam_body, first), grid=(steps,),...]
    unnamed x172 -> x174, local copies, waits for them, and re-layouts: 11.7 us -> 9.91 us
  transfers between devices with their start and end apart: 52 -> 52, of which waited for: 17 -> 16; matrix products, arithmetic and copies ran while one was open for 11% -> 13% of each run, Pallas kernels for 24% -> 23%
where the time goes in v4:
time: 519 us; the launch traced here: 512 us
  Pallas kernels  137 us (26%)
  starting transfers between devices  99.6 us (19%)
  waiting for transfers between devices  90.9 us (18%)
  blocking collectives  80 us (15%)
  other arithmetic  53.4 us (10%)
  local copies, waits for them, and re-layouts  41.1 us (8%)
  between operations  8.54 us (2%)
    all_to_all x4, blocking collectives, exchange(): return lax.all_to_all(value, axes, split_axis=0, concat_axis=0, tiled=True)  80 us
    all_to_all x11, starting transfers between devices, exchange(): return lax.all_to_all(value, axes, split_axis=0, concat_axis=0, tiled=True)  60.1 us
    ppermute x41, waiting for transfers between devices, partner(): lax.ppermute(value, axis, [(place, place ^ mask) for place in range(size)])  57.5 us
    pallas_call x2, Pallas kernels, table_adam(): pl.pallas_call(functools.partial(table_adam_body, first), grid=(steps,),...  42.9 us
    ppermute x41, starting transfers between devices, partner(): lax.ppermute(value, axis, [(place, place ^ mask) for place in range(size)])  39.6 us
    pallas_call x16, Pallas kernels, in_vmem(): pl.pallas_call(body, grid=(1,), in_specs=[pl.BlockSpec(a.shape, whole(a.n...  37.4 us
    pallas_call x2, Pallas kernels, head_part(): pl.pallas_call(functools.partial(head_body, vrows), grid=(steps,), in_spe...  34.4 us
    all_to_all x11, waiting for transfers between devices, exchange(): return lax.all_to_all(value, axes, split_axis=0, concat_axis=0, tiled=True)  33.4 us
  transfers between devices with their start and end apart: 52, of which 16 were waited for; matrix products, arithmetic and copies ran while one was open for 13% of the time, Pallas kernels for 23%

profile of v4, /device:TPU:0, one launch (start us, length us, event | category | flops | bytes accessed | tf_op | source)
XLA Modules:
  0.0 511.5 jit_solution(12036813489597128618)
XLA Ops:
  2.6 3.1 collective-permute-start
  5.6 2.6 collective-permute-start.1
  11.1 6.1 %all-to-all-start = ((s32[32,1,16]{2,1,0:T(1,128)}), s32[32,1,16]{2,1,0:T(1,128)S(1)}, u32[]{:S(2)}, u32[]{:S(2)}) async-start(s32[32,1,16]{2,1,0:T(1,128)} %bitcast), calls=%async_computation | async-start | bytes 32768 | tf_op jit(solution)/shard_map/all_to_all | solution.py:107
  18.0 2.1 dynamic_slice.20
  20.1 2.0 reshape.266
  25.5 5.8 %all-to-all-start.1 = ((bf16[8,56,896]{2,1,0:T(8,128)(2,1)}), bf16[8,56,896]{2,1,0:T(8,128)(2,1)S(1)}, u32[]{:S(2)}, u32[]{:S(2)}) async-start(bf16[8,56,896]{2,1,0:T(8,128)(2,1)} %fusion.5), calls=%async_computation.1 | async-start | bytes 1605632 | tf_op jit(solution)/shard_map/all_to_all | solution.py:107
  32.0 2.1 collective-permute-start.3
  34.1 2.4 fusion.36
  36.6 9.1 %gather_fusion = bf16[512,896]{1,0:T(8,128)(2,1)} fusion(f32[4748,896]{1,0:T(8,128)} %w_ref.3, s32[1024]{0:T(1024)S(1)} %pad_clamp_fusion), kind=kCustom, calls=%fused_computation | custom fusion | bytes 1837056 | tf_op jit(solution)/shard_map/gather | solution.py:932
  45.7 7.9 %collective-permute-done.3 = bf16[4,56,1152]{2,1,0:T(8,128)(2,1)S(1)} collective-permute-done((bf16[4,56,1152]{2,1,0:T(8,128)(2,1)S(1)}, bf16[4,56,1152]{2,1,0:T(8,128)(2,1)S(1)}, u32[]{:S(2)}, u32[]{:S(2)}) %collective-permute-start.3) | collective-permute-done | bytes 516128 | tf_op jit(solution)/shard_map/ppermute | solution.py:40
  53.6 4.5 all-to-all-start.2
  59.0 1.8 collective-permute-start.5
  63.2 20.1 %collective-permute-done.5 = bf16[8,56,640]{2,1,0:T(8,128)(2,1)} collective-permute-done((bf16[8,56,640]{2,1,0:T(8,128)(2,1)S(1)}, bf16[8,56,640]{2,1,0:T(8,128)(2,1)}, u32[]{:S(2)}, u32[]{:S(2)}) %collective-permute-start.5) | collective-permute-done | bytes 573472 | tf_op jit(solution)/shard_map/ppermute | solution.py:40
  86.2 2.0 keys_values.1
  89.0 5.9 %all-to-all-start.3 = ((bf16[8,256,256]{2,1,0:T(8,128)(2,1)}), bf16[8,256,256]{2,1,0:T(8,128)(2,1)S(1)}, u32[]{:S(2)}, u32[]{:S(2)}) async-start(bf16[8,256,256]{2,1,0:T(8,128)(2,1)} %get-tuple-element.192), calls=%async_computation.3 | async-start | bytes 2097152 | tf_op jit(solution)/shard_map/all_to_all | solution.py:107
  98.3 1.6 slice_select_fusion
  104.1 8.7 %collective-permute-done.9 = bf16[8,56,640]{2,1,0:T(8,128)(2,1)} collective-permute-done((bf16[8,56,640]{2,1,0:T(8,128)(2,1)}, bf16[8,56,640]{2,1,0:T(8,128)(2,1)}, u32[]{:S(2)}, u32[]{:S(2)}) %collective-permute-start.9) | collective-permute-done | bytes 573472 | tf_op jit(solution)/shard_map/ppermute | solution.py:40
  112.9 8.5 %all-to-all-done.3 = bf16[8,256,256]{2,1,0:T(8,128)(2,1)S(1)} async-done(((bf16[8,256,256]{2,1,0:T(8,128)(2,1)}), bf16[8,256,256]{2,1,0:T(8,128)(2,1)S(1)}, u32[]{:S(2)}, u32[]{:S(2)}) %all-to-all-start.3) | async-done | bytes 1048608 | tf_op jit(solution)/shard_map/all_to_all | solution.py:107
  121.3 1.7 select_bitcast_fusion.1
  124.3 3.5 attention.1
  128.5 3.7 all-to-all-start.4
  133.2 12.8 %all-to-all-done.4 = bf16[8,32,896]{2,1,0:T(8,128)(2,1)S(1)} async-done(((bf16[8,32,896]{2,1,0:T(8,128)(2,1)}), bf16[8,32,896]{2,1,0:T(8,128)(2,1)S(1)}, u32[]{:S(2)}, u32[]{:S(2)}) %all-to-all-start.4) | async-done | bytes 458784 | tf_op jit(solution)/shard_map/all_to_all | solution.py:107
  145.9 2.0 broadcast_select_fusion.1
  148.0 3.4 feed_forward.1
  151.4 16.8 %all_to_all.82.parts_ref = bf16[8,32,896]{2,1,0:T(8,128)(2,1)S(1)} all-to-all(bf16[8,32,896]{2,1,0:T(8,128)(2,1)S(1)} %bitcast.164), channel_id=1, replica_groups=mesh['batch'=4,'seq'=8] {'seq'}, dimensions={0} | all-to-all | bytes 917504 | tf_op jit(solution)/shard_map/all_to_all | solution.py:107
  170.0 2.7 collective-permute-done.11
  172.8 25.2 %all_to_all.83.rows_ref.refs_4_ = bf16[8,2,32,896]{3,2,1,0:T(8,128)(2,1)S(1)} all-to-all(bf16[8,2,32,896]{3,2,1,0:T(8,128)(2,1)S(1)} %broadcast_in_dim.59), channel_id=1, replica_groups=mesh['batch'=4,'seq'=8] {'seq'}, dimensions={0} | all-to-all | bytes 1835008 | tf_op jit(solution)/shard_map/all_to_all | solution.py:107
  198.2 3.6 all-to-all-start.7
  201.8 17.3 %head_part.2 = (bf16[512,5120]{1,0:T(8,128)(2,1)}, f32[512,128]{1,0:T(8,128)S(1)}, bf16[256,1024]{1,0:T(8,128)(2,1)S(1)}, bf16[256,1024]{1,0:T(8,128)(2,1)S(1)}) custom-call(bf16[8,2,32,896]{3,2,1,0:T(8,128)(2,1)S(1)} %all_to_all.83.rows_ref.refs_4_, bf16[8,2,32,896]{3,2,1,0:T(8,128)(2,1)S(1)} %collective-permute-done.12.other_ref.refs_5_, f32[4748,896]{1,0:T(8,128)} %w_ref.3), custom_call_target="tpu_custom_call" | custom-call | flops 8712617984 | bytes 21878784 | tf_op jit(solution)/shard_map/head_part/pallas_call | solution.py:500
  222.2 1.6 collective-permute-start.14
  223.8 17.0 %head_part.3 = (bf16[512,5120]{1,0:T(8,128)(2,1)}, f32[512,128]{1,0:T(8,128)S(1)}, bf16[256,1024]{1,0:T(8,128)(2,1)S(1)}, bf16[256,1024]{1,0:T(8,128)(2,1)S(1)}) custom-call(bf16[8,2,32,896]{3,2,1,0:T(8,128)(2,1)S(1)} %all_to_all.83.rows_ref.refs_4_, bf16[8,2,32,896]{3,2,1,0:T(8,128)(2,1)S(1)} %collective-permute-done.12.other_ref.refs_5_, f32[4748,896]{1,0:T(8,128)} %w_ref.3), custom_call_target="tpu_custom_call" | custom-call | flops 8712617984 | bytes 21878784 | tf_op jit(solution)/shard_map/head_part/pallas_call | solution.py:500
  241.0 1.8 collective-permute-done.15.refs_1_
  244.1 5.8 %all-to-all-start.8 = ((bf16[8,32,1024]{2,1,0:T(8,128)(2,1)}), bf16[8,32,1024]{2,1,0:T(8,128)(2,1)S(1)}, u32[]{:S(2)}, u32[]{:S(2)}) async-start(bf16[8,32,1024]{2,1,0:T(8,128)(2,1)} %bitcast.31), calls=%async_computation.8 | async-start | bytes 1048576 | tf_op jit(solution)/shard_map/all_to_all | solution.py:107
  252.7 12.1 %all-to-all-done.8.parts_ref = bf16[8,32,1024]{2,1,0:T(8,128)(2,1)S(1)} async-done(((bf16[8,32,1024]{2,1,0:T(8,128)(2,1)}), bf16[8,32,1024]{2,1,0:T(8,128)(2,1)S(1)}, u32[]{:S(2)}, u32[]{:S(2)}) %all-to-all-start.8) | async-done | bytes 524320 | tf_op jit(solution)/shard_map/all_to_all | solution.py:107
  266.2 18.1 %all_to_all.84 = bf16[8,32,1024]{2,1,0:T(8,128)(2,1)S(1)} all-to-all(bf16[8,32,1024]{2,1,0:T(8,128)(2,1)S(1)} %get-tuple-element.240), channel_id=1, replica_groups=mesh['batch'=4,'seq'=8] {'seq'}, dimensions={0} | all-to-all | bytes 1048576 | tf_op jit(solution)/shard_map/all_to_all | solution.py:107
  284.3 4.9 feed_forward_back.1
  290.7 4.1 all-to-all-start.10
  295.4 3.7 collective-permute-done.16
  299.2 3.4 layer_grads.1
  303.3 7.7 %head_grad.2 = (bf16[4748,896]{1,0:T(8,128)(2,1)}, f32[8,896]{1,0:T(8,128)S(1)}) custom-call(bf16[512,5120]{1,0:T(8,128)(2,1)} %get-tuple-element.251.refs_0_, bf16[512,5120]{1,0:T(8,128)(2,1)} %get-tuple-element.252.refs_1_, f32[512,128]{1,0:T(8,128)} %copy-done.21, f32[512,128]{1,0:T(8,128)} %copy-done.22, bf16[8,2,32,896]{3,2,1,0:T(8,128)(2,1)} %copy-done.6, ...), custom_call_target="tpu_custom_call" | custom-call | flops 2818572288 | bytes 5898240 | tf_op jit(solution)/shard_map/head_grad/pallas_call | solution.py:762
  313.5 8.0 %attention_back.1 = (bf16[2048,256]{1,0:T(8,128)(2,1)}, bf16[32,896]{1,0:T(8,128)(2,1)S(1)}, f32[1,896]{1,0:T(1,128)S(1)}) custom-call(bf16[32,896]{1,0:T(8,128)(2,1)S(1)} %get-tuple-element.261.grad_ref, bf16[896,896]{1,0:T(8,128)(2,1)} %copy-done.1, bf16[32,896]{1,0:T(8,128)(2,1)} %copy-done.24, bf16[2048,256]{1,0:T(8,128)(2,1)} %bitcast.157, ...), custom_call_target="tpu_custom_call" | custom-call | flops 587202560 | bytes 4025984 | tf_op jit(solution)/shard_map/attention_back/pallas_call | solution.py:207
  321.5 2.1 collective-permute-start.22
  323.5 2.4 collective-permute-start.23
  326.1 6.1 %all-to-all-start.11 = ((bf16[8,256,256]{2,1,0:T(8,128)(2,1)}), bf16[8,256,256]{2,1,0:T(8,128)(2,1)S(1)}, u32[]{:S(2)}, u32[]{:S(2)}) async-start(bf16[8,256,256]{2,1,0:T(8,128)(2,1)} %bitcast.41), calls=%async_computation.11 | async-start | bytes 2097152 | tf_op jit(solution)/shard_map/all_to_all | solution.py:107
  332.9 2.6 collective-permute-done.23
  344.6 14.1 %head_grad.3 = (bf16[4748,896]{1,0:T(8,128)(2,1)}, f32[8,896]{1,0:T(8,128)S(1)}) custom-call(bf16[512,5120]{1,0:T(8,128)(2,1)} %get-tuple-element.251.refs_0_, bf16[512,5120]{1,0:T(8,128)(2,1)} %get-tuple-element.252.refs_1_, f32[512,128]{1,0:T(8,128)} %copy-done.21, f32[512,128]{1,0:T(8,128)} %copy-done.22, ...), custom_call_target="tpu_custom_call", output_to_operand_aliasing={{0}: (8, {})} | custom-call | flops 6576668672 | bytes 13762560 | tf_op jit(solution)/shard_map/head_grad/pallas_call | solution.py:762
  358.7 2.9 collective-permute-done.21
  362.5 5.2 %first_norm_back.1 = (bf16[256,256]{1,0:T(8,128)(2,1)S(1)}, bf16[512,896]{1,0:T(8,128)(2,1)}, f32[1,896]{1,0:T(1,128)S(1)}, f32[1,256]{1,0:T(1,128)S(1)}) custom-call(bf16[8,256,256]{2,1,0:T(8,128)(2,1)S(1)} %all-to-all-done.11.parts_ref, f32[256,128]{1,0:T(8,128)} %copy-done.14, f32[256,128]{1,0:T(8,128)} %copy-done.13, bf16[896,256]{1,0:T(8,128)(2,1)} %copy-done.5, ...), custom_call_target="tpu_custom_call" | custom-call | flops 440401920 | bytes 5439616 | tf_op jit(solution)/shard_map/first_norm_back/pallas_call | solution.py:207
  372.6 10.6 %all-to-all-start.12 = ((bf16[32,16,896]{2,1,0:T(8,128)(2,1)}), bf16[32,16,896]{2,1,0:T(8,128)(2,1)S(1)}, u32[]{:S(2)}, u32[]{:S(2)}) async-start(bf16[32,16,896]{2,1,0:T(8,128)(2,1)} %bitcast.50), calls=%async_computation.12 | async-start | bytes 1835008 | tf_op jit(solution)/shard_map/all_to_all | solution.py:107
  383.3 2.7 multiply_reduce_fusion
  386.7 7.1 %gather_fusion.1 = bf16[512,896]{1,0:T(8,128)(2,1)S(1)} fusion(bf16[4748,896]{1,0:T(8,128)(2,1)} %get-tuple-element.289.grad_ref, s32[1024]{0:T(1024)S(1)} %copy-done.72), kind=kCustom, calls=%fused_computation.1 | custom fusion | bytes 1837056 | tf_op jit(solution)/shard_map/gather | solution.py:1230
  396.3 1.8 collective-permute-start.31
  398.8 1.8 collective-permute-done.31
  400.6 2.0 collective-permute-start.32
  402.6 3.3 collective-permute-start.33
  408.4 2.9 collective-permute-done.34
  418.2 19.9 %all_to_all.85.parts_ref = f32[32,31,128]{2,1,0:T(8,128)S(1)} all-to-all(f32[32,31,128]{2,1,0:T(8,128)S(1)} %broadcast_in_dim.65), channel_id=1, replica_groups=mesh['batch'=4,'seq'=8] {'batch','seq'}, dimensions={0} | all-to-all | bytes 1015808 | tf_op jit(solution)/shard_map/all_to_all | solution.py:107
  441.0 3.8 all-to-all-start.14
  447.3 21.6 %table_adam.2 = (f32[4748,896]{1,0:T(8,128)}, f32[4748,896]{1,0:T(8,128)}, f32[4748,896]{1,0:T(8,128)}) custom-call(f32[1]{0:T(128)} %bitcast.74.scale_ref, s32[1,512]{1,0:T(1,128)S(1)} %broadcast_in_dim_reshape.2.names_ref, bf16[512,896]{1,0:T(8,128)(2,1)S(1)} %bitcast.154, bf16[4748,896]{1,0:T(8,128)(2,1)} %get-tuple-element.289.grad_ref, ...), custom_call_target="tpu_custom_call" | custom-call | flops 2231369728 | bytes 56655872 | tf_op jit(solution)/shard_map/table_adam/pallas_call | solution.py:807
  470.7 21.3 %table_adam.3 = (f32[4748,896]{1,0:T(8,128)}, f32[4748,896]{1,0:T(8,128)}, f32[4748,896]{1,0:T(8,128)}) custom-call(f32[1]{0:T(128)} %bitcast.74.scale_ref, s32[1,512]{1,0:T(1,128)S(1)} %broadcast_in_dim_reshape.2.names_ref, bf16[512,896]{1,0:T(8,128)(2,1)S(1)} %bitcast.155, ...), custom_call_target="tpu_custom_call", output_to_operand_aliasing={{0}: (7, {}), {1}: (8, {}), {2}: (9, {})} | custom-call | flops 2231369728 | bytes 56655872 | tf_op jit(solution)/shard_map/table_adam/pallas_call | solution.py:807
  494.1 2.8 multiply_subtract_fusion.2
  496.9 2.0 multiply_subtract_fusion.3
  499.0 5.4 %multiply_subtract_fusion.1 = (f32[608,896]{1,0:T(8,128)}, f32[608,896]{1,0:T(8,128)}, f32[608,896]{1,0:T(8,128)}) fusion(f32[608,896]{1,0:T(8,128)S(1)} %copy-done.42, f32[]{:T(128)} %bitcast.73, bf16[608,896]{1,0:T(8,128)(2,1)S(1)} %bitcast.178, f32[608,896]{1,0:T(8,128)S(1)} %copy-done.44, f32[608,896]{1,0:T(8,128)S(1)} %copy-done.45), kind=kLoop, calls=%fused_computation.11 | loop fusion | flops 9261056 | bytes 14163972 | tf_op jit(solution)/shard_map/sub | solution.py:178
  504.7 6.6 %multiply_subtract_fusion = (f32[112,9728]{1,0:T(8,128)}, f32[112,9728]{1,0:T(8,128)}, f32[112,9728]{1,0:T(8,128)}) fusion(f32[112,9728]{1,0:T(8,128)S(1)} %bitcast.173, f32[]{:T(128)} %bitcast.73, bf16[112,4864]{1,0:T(8,128)(2,1)S(1)} %get-tuple-element.370, bf16[112,4864]{1,0:T(8,128)(2,1)S(1)} %get-tuple-element.369, f32[112,9728]{1,0:T(8,128)S(1)} %bitcast.175, ...), kind=kLoop, calls=%fused_computation.4 | loop fusion | flops 21790720 | bytes 28327940 | tf_op jit(solution)/shard_map/sub | solution.py:178
  (381 shorter events, 74.5 us)
Async XLA Ops:
  2.6 21.9 %collective-permute-start = (bf16[1,56,1152]{2,1,0:T(8,128)(2,1)S(1)}, bf16[1,56,1152]{2,1,0:T(8,128)(2,1)S(1)}, u32[]{:S(2)}, u32[]{:S(2)}) collective-permute-start(bf16[1,56,1152]{2,1,0:T(8,128)(2,1)S(1)} %maximum_bitcast_fusion), channel_id=1, source_target_pairs={{0,2},{1,3},{2,0},{3,1},{4,6},{5,7},{6,4},{7,5},{8,10},{9,11},{10,... | collective-permute-start | bytes 387080 | tf_op jit(solution)/shard_map/ppermute | solution.py:40
  5.6 18.8 %collective-permute-start.1 = (bf16[1,56,1152]{2,1,0:T(8,128)(2,1)S(1)}, bf16[1,56,1152]{2,1,0:T(8,128)(2,1)S(1)}, u32[]{:S(2)}, u32[]{:S(2)}) collective-permute-start(bf16[1,56,1152]{2,1,0:T(8,128)(2,1)S(1)} %maximum_bitcast_fusion), channel_id=1, source_target_pairs={{0,4},{1,5},{2,6},{3,7},{4,0},{5,1},{6,2},{7,3},{8,12},{9,13},{10,... | collective-permute-start | bytes 387080 | tf_op jit(solution)/shard_map/ppermute | solution.py:40
  8.2 16.2 %collective-permute-start.2 = (bf16[1,56,1152]{2,1,0:T(8,128)(2,1)S(1)}, bf16[1,56,1152]{2,1,0:T(8,128)(2,1)}, u32[]{:S(2)}, u32[]{:S(2)}) collective-permute-start(bf16[1,56,1152]{2,1,0:T(8,128)(2,1)S(1)} %maximum_bitcast_fusion), channel_id=1, source_target_pairs={{0,6},{1,7},{2,4},{3,5},{4,2},{5,3},{6,0},{7,1},{8,14},{9,15},{10,... | collective-permute-start | bytes 387080 | tf_op jit(solution)/shard_map/ppermute | solution.py:40
  9.2 77.0 %copy-start.15 = (bf16[256,512]{1,0:T(8,128)(2,1)}, bf16[256,512]{1,0:T(8,128)(2,1)S(1)}, u32[]{:S(2)}) copy-start(bf16[256,512]{1,0:T(8,128)(2,1)S(1)} %get-tuple-element.189.placer_ref) | copy-start | bytes 786436
  11.1 14.4 %all-to-all-start = ((s32[32,1,16]{2,1,0:T(1,128)}), s32[32,1,16]{2,1,0:T(1,128)S(1)}, u32[]{:S(2)}, u32[]{:S(2)}) async-start(s32[32,1,16]{2,1,0:T(1,128)} %bitcast), calls=%async_computation | async-start | bytes 32768 | tf_op jit(solution)/shard_map/all_to_all | solution.py:107
  25.5 28.2 %all-to-all-start.1 = ((bf16[8,56,896]{2,1,0:T(8,128)(2,1)}), bf16[8,56,896]{2,1,0:T(8,128)(2,1)S(1)}, u32[]{:S(2)}, u32[]{:S(2)}) async-start(bf16[8,56,896]{2,1,0:T(8,128)(2,1)} %fusion.5), calls=%async_computation.1 | async-start | bytes 1605632 | tf_op jit(solution)/shard_map/all_to_all | solution.py:107
  32.0 54.2 %copy-start.33 = (f32[1,896]{1,0:T(1,128)}, f32[1,896]{1,0:T(1,128)S(1)}, u32[]{:S(2)}) copy-start(f32[1,896]{1,0:T(1,128)S(1)} %get-tuple-element.405.gain_ref) | copy-start | bytes 10756
  32.0 92.3 %copy-start.34 = (f32[1,896]{1,0:T(1,128)}, f32[1,896]{1,0:T(1,128)S(1)}, u32[]{:S(2)}) copy-start(f32[1,896]{1,0:T(1,128)S(1)} %get-tuple-element.404.gain_ref) | copy-start | bytes 10756
  32.0 136.3 %copy-start.35 = (f32[1,896]{1,0:T(1,128)}, f32[1,896]{1,0:T(1,128)S(1)}, u32[]{:S(2)}) copy-start(f32[1,896]{1,0:T(1,128)S(1)} %get-tuple-element.403.gain_ref) | copy-start | bytes 10756
  32.0 21.6 %collective-permute-start.3 = (bf16[4,56,1152]{2,1,0:T(8,128)(2,1)S(1)}, bf16[4,56,1152]{2,1,0:T(8,128)(2,1)S(1)}, u32[]{:S(2)}, u32[]{:S(2)}) collective-permute-start(bf16[4,56,1152]{2,1,0:T(8,128)(2,1)S(1)} %pad_maximum_fusion.10), channel_id=1, source_target_pairs={{0,1},{1,0},{2,3},{3,2},{4,5},{5,4},{6,7},{7,6},{8,9},{9,8},{10,11... | collective-permute-start | bytes 1548296 | tf_op jit(solution)/shard_map/ppermute | solution.py:40
  36.5 87.8 %copy-start.37 = (s32[1,32]{1,0:T(1,128)}, s32[1,32]{1,0:T(1,128)S(1)}, u32[]{:S(2)}) copy-start(s32[1,32]{1,0:T(1,128)S(1)} %get-tuple-element.358.place_ref) | copy-start | bytes 388
  53.6 29.6 %all-to-all-start.2 = ((bf16[32,16,896]{2,1,0:T(8,128)(2,1)}), bf16[32,16,896]{2,1,0:T(8,128)(2,1)S(1)}, u32[]{:S(2)}, u32[]{:S(2)}) async-start(bf16[32,16,896]{2,1,0:T(8,128)(2,1)} %bitcast.5), calls=%async_computation.2 | async-start | bytes 1835008 | tf_op jit(solution)/shard_map/all_to_all | solution.py:107
  59.0 24.3 %collective-permute-start.5 = (bf16[8,56,640]{2,1,0:T(8,128)(2,1)S(1)}, bf16[8,56,640]{2,1,0:T(8,128)(2,1)}, u32[]{:S(2)}, u32[]{:S(2)}) collective-permute-start(bf16[8,56,640]{2,1,0:T(8,128)(2,1)S(1)} %slice.212), channel_id=1, source_target_pairs={{0,16},{8,24},{16,0},{24,8},{1,17},{9,25},{17,1},{25,9},{2,18},{10... | collective-permute-start | bytes 1720328 | tf_op jit(solution)/shard_map/ppermute | solution.py:40
  60.9 1.6 collective-permute-start.4
  83.3 12.2 %collective-permute-start.7 = (bf16[8,56,512]{2,1,0:T(8,128)(2,1)S(1)}, bf16[8,56,512]{2,1,0:T(8,128)(2,1)}, u32[]{:S(2)}, u32[]{:S(2)}) collective-permute-start(bf16[8,56,512]{2,1,0:T(8,128)(2,1)S(1)} %slice.213), channel_id=1, source_target_pairs={{0,16},{8,24},{16,0},{24,8},{1,17},{9,25},{17,1},{25,9},{2,18},{10... | collective-permute-start | bytes 1376264 | tf_op jit(solution)/shard_map/ppermute | solution.py:40
  86.0 12.3 %collective-permute-start.6 = (bf16[896,640]{1,0:T(8,128)(2,1)}, bf16[896,640]{1,0:T(8,128)(2,1)}, u32[]{:S(2)}, u32[]{:S(2)}) collective-permute-start(bf16[896,640]{1,0:T(8,128)(2,1)} %bitcast.16), channel_id=1, source_target_pairs={{0,8},{8,0},{16,24},{24,16},{1,9},{9,1},{17,25},{25,17},{2,10},{10... | collective-permute-start | bytes 3440648 | tf_op jit(solution)/shard_map/ppermute | solution.py:40
  89.0 32.3 %all-to-all-start.3 = ((bf16[8,256,256]{2,1,0:T(8,128)(2,1)}), bf16[8,256,256]{2,1,0:T(8,128)(2,1)S(1)}, u32[]{:S(2)}, u32[]{:S(2)}) async-start(bf16[8,256,256]{2,1,0:T(8,128)(2,1)} %get-tuple-element.192), calls=%async_computation.3 | async-start | bytes 2097152 | tf_op jit(solution)/shard_map/all_to_all | solution.py:107
  96.9 6.9 %collective-permute-start.8 = (bf16[896,512]{1,0:T(8,128)(2,1)S(1)}, bf16[896,512]{1,0:T(8,128)(2,1)S(1)}, u32[]{:S(2)}, u32[]{:S(2)}) collective-permute-start(bf16[896,512]{1,0:T(8,128)(2,1)S(1)} %bitcast.170), channel_id=1, source_target_pairs={{0,8},{8,0},{16,24},{24,16},{1,9},{9,1},{17,25},{25,17},{2,10},{10... | collective-permute-start | bytes 2752520 | tf_op jit(solution)/shard_map/ppermute | solution.py:40
  97.1 15.8 %collective-permute-start.9 = (bf16[8,56,640]{2,1,0:T(8,128)(2,1)}, bf16[8,56,640]{2,1,0:T(8,128)(2,1)}, u32[]{:S(2)}, u32[]{:S(2)}) collective-permute-start(bf16[8,56,640]{2,1,0:T(8,128)(2,1)} %slice.162), channel_id=1, source_target_pairs={{0,16},{8,24},{16,0},{24,8},{1,17},{9,25},{17,1},{25,9},{2,18},{10... | collective-permute-start | bytes 1720328 | tf_op jit(solution)/shard_map/ppermute | solution.py:40
  124.3 21.6 %collective-permute-start.10 = (bf16[896,640]{1,0:T(8,128)(2,1)}, bf16[896,640]{1,0:T(8,128)(2,1)}, u32[]{:S(2)}, u32[]{:S(2)}) collective-permute-start(bf16[896,640]{1,0:T(8,128)(2,1)} %bitcast.24), channel_id=1, source_target_pairs={{0,8},{8,0},{16,24},{24,16},{1,9},{9,1},{17,25},{25,17},{2,10},{10... | collective-permute-start | bytes 3440648 | tf_op jit(solution)/shard_map/ppermute | solution.py:40
  128.5 39.8 %copy-start.19 = (f32[32,896]{1,0:T(8,128)}, f32[32,896]{1,0:T(8,128)S(1)}, u32[]{:S(2)}) copy-start(f32[32,896]{1,0:T(8,128)S(1)} %get-tuple-element.218.one_ref) | copy-start | bytes 344068
  128.5 17.4 %all-to-all-start.4 = ((bf16[8,32,896]{2,1,0:T(8,128)(2,1)}), bf16[8,32,896]{2,1,0:T(8,128)(2,1)S(1)}, u32[]{:S(2)}, u32[]{:S(2)}) async-start(bf16[8,32,896]{2,1,0:T(8,128)(2,1)} %get-tuple-element.208), calls=%async_computation.4 | async-start | bytes 917504 | tf_op jit(solution)/shard_map/all_to_all | solution.py:107
  151.4 46.6 %copy-start.17 = (f32[256,640]{1,0:T(8,128)}, f32[256,640]{1,0:T(8,128)S(1)}, u32[]{:S(2)}) copy-start(f32[256,640]{1,0:T(8,128)S(1)} %get-tuple-element.242.gate_ref) | copy-start | bytes 1966084
  151.4 46.6 %copy-start.18 = (f32[256,640]{1,0:T(8,128)}, f32[256,640]{1,0:T(8,128)S(1)}, u32[]{:S(2)}) copy-start(f32[256,640]{1,0:T(8,128)S(1)} %get-tuple-element.243.up_ref) | copy-start | bytes 1966084
  168.5 4.2 collective-permute-start.11
  198.1 3.7 collective-permute-start.12
  198.2 21.7 %all-to-all-start.7 = ((bf16[8,64,112]{2,1,0:T(8,128)(2,1)}), bf16[8,64,112]{2,1,0:T(8,128)(2,1)S(1)}, u32[]{:S(2)}, u32[]{:S(2)}) async-start(bf16[8,64,112]{2,1,0:T(8,128)(2,1)} %pad_maximum_fusion.15), calls=%async_computation.7 | async-start | bytes 262144 | tf_op jit(solution)/shard_map/all_to_all | solution.py:107
  219.8 2.0 collective-permute-start.13
  222.2 18.6 %collective-permute-start.14 = (bf16[256,1024]{1,0:T(8,128)(2,1)S(1)}, bf16[256,1024]{1,0:T(8,128)(2,1)S(1)}, u32[]{:S(2)}, u32[]{:S(2)}) collective-permute-start(bf16[256,1024]{1,0:T(8,128)(2,1)S(1)} %merge_means.2), channel_id=1, source_target_pairs={{0,16},{8,24},{16,0},{24,8},{1,17},{9,25},{17,1},{25,9},{2,18},{10... | collective-permute-start | bytes 1572872 | tf_op jit(solution)/shard_map/ppermute | solution.py:40
  240.8 2.0 collective-permute-start.15
  244.1 20.6 %all-to-all-start.8 = ((bf16[8,32,1024]{2,1,0:T(8,128)(2,1)}), bf16[8,32,1024]{2,1,0:T(8,128)(2,1)S(1)}, u32[]{:S(2)}, u32[]{:S(2)}) async-start(bf16[8,32,1024]{2,1,0:T(8,128)(2,1)} %bitcast.31), calls=%async_computation.8 | async-start | bytes 1048576 | tf_op jit(solution)/shard_map/all_to_all | solution.py:107
  290.7 20.4 %all-to-all-start.10 = ((bf16[8,32,896]{2,1,0:T(8,128)(2,1)}), bf16[8,32,896]{2,1,0:T(8,128)(2,1)S(1)}, u32[]{:S(2)}, u32[]{:S(2)}) async-start(bf16[8,32,896]{2,1,0:T(8,128)(2,1)} %bitcast.37), calls=%async_computation.10 | async-start | bytes 917504 | tf_op jit(solution)/shard_map/all_to_all | solution.py:107
  294.8 4.3 collective-permute-start.16
  299.2 3.5 collective-permute-start.17
  311.1 29.0 %collective-permute-start.18 = (bf16[896,640]{1,0:T(8,128)(2,1)}, bf16[896,640]{1,0:T(8,128)(2,1)}, u32[]{:S(2)}, u32[]{:S(2)}) collective-permute-start(bf16[896,640]{1,0:T(8,128)(2,1)} %get-tuple-element.266), channel_id=1, source_target_pairs={{0,8},{8,0},{16,24},{24,16},{1,9},{9,1},{17,25},{25,17},{2,10},{10... | collective-permute-start | bytes 3440648 | tf_op jit(solution)/shard_map/ppermute | solution.py:40
  311.6 26.5 %collective-permute-start.19 = (bf16[304,896]{1,0:T(8,128)(2,1)S(1)}, bf16[304,896]{1,0:T(8,128)(2,1)}, u32[]{:S(2)}, u32[]{:S(2)}) collective-permute-start(bf16[304,896]{1,0:T(8,128)(2,1)S(1)} %get-tuple-element.268), channel_id=1, source_target_pairs={{0,8},{8,0},{16,24},{24,16},{1,9},{9,1},{17,25},{25,17},{2,10},{10... | collective-permute-start | bytes 1634312 | tf_op jit(solution)/shard_map/ppermute | solution.py:40
  321.5 11.4 %collective-permute-start.22 = (bf16[1,64,896]{2,1,0:T(8,128)(2,1)S(1)}, bf16[1,64,896]{2,1,0:T(8,128)(2,1)}, u32[]{:S(2)}, u32[]{:S(2)}) collective-permute-start(bf16[1,64,896]{2,1,0:T(8,128)(2,1)S(1)} %maximum_bitcast_fusion.1), channel_id=1, source_target_pairs={{0,2},{1,3},{2,0},{3,1},{4,6},{5,7},{6,4},{7,5},{8,10},{9,11},{10,... | collective-permute-start | bytes 344072 | tf_op jit(solution)/shard_map/ppermute | solution.py:40
  323.5 11.9 %collective-permute-start.23 = (bf16[1,64,896]{2,1,0:T(8,128)(2,1)S(1)}, bf16[1,64,896]{2,1,0:T(8,128)(2,1)}, u32[]{:S(2)}, u32[]{:S(2)}) collective-permute-start(bf16[1,64,896]{2,1,0:T(8,128)(2,1)S(1)} %maximum_bitcast_fusion.1), channel_id=1, source_target_pairs={{0,4},{1,5},{2,6},{3,7},{4,0},{5,1},{6,2},{7,3},{8,12},{9,13},{10,... | collective-permute-start | bytes 344072 | tf_op jit(solution)/shard_map/ppermute | solution.py:40
  325.9 9.6 %collective-permute-start.24 = (bf16[1,64,896]{2,1,0:T(8,128)(2,1)S(1)}, bf16[1,64,896]{2,1,0:T(8,128)(2,1)}, u32[]{:S(2)}, u32[]{:S(2)}) collective-permute-start(bf16[1,64,896]{2,1,0:T(8,128)(2,1)S(1)} %maximum_bitcast_fusion.1), channel_id=1, source_target_pairs={{0,6},{1,7},{2,4},{3,5},{4,2},{5,3},{6,0},{7,1},{8,14},{9,15},{10,... | collective-permute-start | bytes 344072 | tf_op jit(solution)/shard_map/ppermute | solution.py:40
  326.1 35.6 %all-to-all-start.11 = ((bf16[8,256,256]{2,1,0:T(8,128)(2,1)}), bf16[8,256,256]{2,1,0:T(8,128)(2,1)S(1)}, u32[]{:S(2)}, u32[]{:S(2)}) async-start(bf16[8,256,256]{2,1,0:T(8,128)(2,1)} %bitcast.41), calls=%async_computation.11 | async-start | bytes 2097152 | tf_op jit(solution)/shard_map/all_to_all | solution.py:107
  336.6 22.1 %collective-permute-start.25 = (bf16[4,64,896]{2,1,0:T(8,128)(2,1)S(1)}, bf16[4,64,896]{2,1,0:T(8,128)(2,1)S(1)}, u32[]{:S(2)}, u32[]{:S(2)}) collective-permute-start(bf16[4,64,896]{2,1,0:T(8,128)(2,1)S(1)} %pad_maximum_fusion.12), channel_id=1, source_target_pairs={{0,1},{1,0},{2,3},{3,2},{4,5},{5,4},{6,7},{7,6},{8,9},{9,8},{10,11... | collective-permute-start | bytes 1376264 | tf_op jit(solution)/shard_map/ppermute | solution.py:40
  342.6 19.0 %collective-permute-start.20 = (bf16[8,56,640]{2,1,0:T(8,128)(2,1)S(1)}, bf16[8,56,640]{2,1,0:T(8,128)(2,1)S(1)}, u32[]{:S(2)}, u32[]{:S(2)}) collective-permute-start(bf16[8,56,640]{2,1,0:T(8,128)(2,1)S(1)} %fusion.6), channel_id=1, source_target_pairs={{0,16},{8,24},{16,0},{24,8},{1,17},{9,25},{17,1},{25,9},{2,18},{10... | collective-permute-start | bytes 1720328 | tf_op jit(solution)/shard_map/ppermute | solution.py:40
  343.1 18.5 %collective-permute-start.21 = (bf16[152,896]{1,0:T(8,128)(2,1)S(1)}, bf16[152,896]{1,0:T(8,128)(2,1)S(1)}, u32[]{:S(2)}, u32[]{:S(2)}) collective-permute-start(bf16[152,896]{1,0:T(8,128)(2,1)S(1)} %get-tuple-element.272), channel_id=1, source_target_pairs={{0,16},{8,24},{16,0},{24,8},{1,17},{9,25},{17,1},{25,9},{2,18},{10... | collective-permute-start | bytes 817160 | tf_op jit(solution)/shard_map/ppermute | solution.py:40
  369.1 26.0 %collective-permute-start.28 = (bf16[8,56,128]{2,1,0:T(8,128)(2,1)}, bf16[8,56,128]{2,1,0:T(8,128)(2,1)}, u32[]{:S(2)}, u32[]{:S(2)}) collective-permute-start(bf16[8,56,128]{2,1,0:T(8,128)(2,1)} %get-tuple-element.389), channel_id=1, source_target_pairs={{0,8},{8,0},{16,24},{24,16},{1,9},{9,1},{17,25},{25,17},{2,10},{10... | collective-permute-start | bytes 344072 | tf_op jit(solution)/shard_map/ppermute | solution.py:40
  369.1 26.0 %collective-permute-start.29 = (bf16[8,56,128]{2,1,0:T(8,128)(2,1)}, bf16[8,56,128]{2,1,0:T(8,128)(2,1)}, u32[]{:S(2)}, u32[]{:S(2)}) collective-permute-start(bf16[8,56,128]{2,1,0:T(8,128)(2,1)} %get-tuple-element.391), channel_id=1, source_target_pairs={{0,16},{8,24},{16,0},{24,8},{1,17},{9,25},{17,1},{25,9},{2,18},{10... | collective-permute-start | bytes 344072 | tf_op jit(solution)/shard_map/ppermute | solution.py:40
  369.7 25.5 %collective-permute-start.30 = (bf16[8,56,128]{2,1,0:T(8,128)(2,1)}, bf16[8,56,128]{2,1,0:T(8,128)(2,1)}, u32[]{:S(2)}, u32[]{:S(2)}) collective-permute-start(bf16[8,56,128]{2,1,0:T(8,128)(2,1)} %get-tuple-element.390), channel_id=1, source_target_pairs={{0,24},{8,16},{16,8},{24,0},{1,25},{9,17},{17,9},{25,1},{2,26},{10... | collective-permute-start | bytes 344072 | tf_op jit(solution)/shard_map/ppermute | solution.py:40
  372.3 34.9 %collective-permute-start.26 = (bf16[112,896]{1,0:T(8,128)(2,1)}, bf16[112,896]{1,0:T(8,128)(2,1)S(1)}, u32[]{:S(2)}, u32[]{:S(2)}) collective-permute-start(bf16[112,896]{1,0:T(8,128)(2,1)} %get-tuple-element.414), channel_id=1, source_target_pairs={{0,8},{8,0},{16,24},{24,16},{1,9},{9,1},{17,25},{25,17},{2,10},{10... | collective-permute-start | bytes 602120 | tf_op jit(solution)/shard_map/ppermute | solution.py:40
  372.6 42.7 %all-to-all-start.12 = ((bf16[32,16,896]{2,1,0:T(8,128)(2,1)}), bf16[32,16,896]{2,1,0:T(8,128)(2,1)S(1)}, u32[]{:S(2)}, u32[]{:S(2)}) async-start(bf16[32,16,896]{2,1,0:T(8,128)(2,1)} %bitcast.50), calls=%async_computation.12 | async-start | bytes 1835008 | tf_op jit(solution)/shard_map/all_to_all | solution.py:107
  396.3 4.2 collective-permute-start.31
  400.6 7.8 %collective-permute-start.32 = (bf16[1,56,128]{2,1,0:T(8,128)(2,1)S(1)}, bf16[1,56,128]{2,1,0:T(8,128)(2,1)S(1)}, u32[]{:S(2)}, u32[]{:S(2)}) collective-permute-start(bf16[1,56,128]{2,1,0:T(8,128)(2,1)S(1)} %get-tuple-element.398), channel_id=1, source_target_pairs={{0,2},{1,3},{2,0},{3,1},{4,6},{5,7},{6,4},{7,5},{8,10},{9,11},{10,... | collective-permute-start | bytes 43016 | tf_op jit(solution)/shard_map/ppermute | solution.py:40
  402.6 5.9 %collective-permute-start.33 = (bf16[1,56,128]{2,1,0:T(8,128)(2,1)S(1)}, bf16[1,56,128]{2,1,0:T(8,128)(2,1)S(1)}, u32[]{:S(2)}, u32[]{:S(2)}) collective-permute-start(bf16[1,56,128]{2,1,0:T(8,128)(2,1)S(1)} %get-tuple-element.400), channel_id=1, source_target_pairs={{0,4},{1,5},{2,6},{3,7},{4,0},{5,1},{6,2},{7,3},{8,12},{9,13},{10,... | collective-permute-start | bytes 43016 | tf_op jit(solution)/shard_map/ppermute | solution.py:40
  405.9 5.5 %collective-permute-start.34 = (bf16[1,56,128]{2,1,0:T(8,128)(2,1)S(1)}, bf16[1,56,128]{2,1,0:T(8,128)(2,1)S(1)}, u32[]{:S(2)}, u32[]{:S(2)}) collective-permute-start(bf16[1,56,128]{2,1,0:T(8,128)(2,1)S(1)} %get-tuple-element.399), channel_id=1, source_target_pairs={{0,6},{1,7},{2,4},{3,5},{4,2},{5,3},{6,0},{7,1},{8,14},{9,15},{10,... | collective-permute-start | bytes 43016 | tf_op jit(solution)/shard_map/ppermute | solution.py:40
  407.3 4.7 collective-permute-start.27
  416.7 28.8 %copy-start.74 = (f32[3,896]{1,0:T(4,128)S(1)}, f32[3,896]{1,0:T(4,128)}, u32[]{:S(2)}) copy-start(f32[3,896]{1,0:T(4,128)} %param.52) | copy-start | bytes 32260
  416.7 29.4 %copy-start.70 = (f32[1152]{0:T(1024)S(1)}, f32[1152]{0:T(1024)}, u32[]{:S(2)}) copy-start(f32[1152]{0:T(1024)} %param.53) | copy-start | bytes 13828
  416.7 29.4 %copy-start.75 = (f32[1152]{0:T(1024)S(1)}, f32[1152]{0:T(1024)}, u32[]{:S(2)}) copy-start(f32[1152]{0:T(1024)} %param.54) | copy-start | bytes 13828
  416.7 29.4 %copy-start.76 = (f32[1152]{0:T(1024)S(1)}, f32[1152]{0:T(1024)}, u32[]{:S(2)}) copy-start(f32[1152]{0:T(1024)} %param.55) | copy-start | bytes 13828
  438.9 30.1 %collective-permute-start.36 = (bf16[56,1024]{1,0:T(8,128)(2,1)S(1)}, bf16[56,1024]{1,0:T(8,128)(2,1)S(1)}, u32[]{:S(2)}, u32[]{:S(2)}) collective-permute-start(bf16[56,1024]{1,0:T(8,128)(2,1)S(1)} %constant_dynamic-update-slice_fusion.2), channel_id=1, source_target_pairs={{0,16},{8,24},{16,0},{24,8},{1,17},{9,25},{17,1},{25,9},{2,18},{10... | collective-permute-start | bytes 344072 | tf_op jit(solution)/shard_map/ppermute | solution.py:40
  439.5 29.5 %collective-permute-start.35 = (bf16[152,896]{1,0:T(8,128)(2,1)S(1)}, bf16[152,896]{1,0:T(8,128)(2,1)S(1)}, u32[]{:S(2)}, u32[]{:S(2)}) collective-permute-start(bf16[152,896]{1,0:T(8,128)(2,1)S(1)} %get-tuple-element.315), channel_id=1, source_target_pairs={{0,16},{8,24},{16,0},{24,8},{1,17},{9,25},{17,1},{25,9},{2,18},{10... | collective-permute-start | bytes 817160 | tf_op jit(solution)/shard_map/ppermute | solution.py:40
  441.0 28.2 %all-to-all-start.14 = ((bf16[8,56,640]{2,1,0:T(8,128)(2,1)}), bf16[8,56,640]{2,1,0:T(8,128)(2,1)S(1)}, u32[]{:S(2)}, u32[]{:S(2)}) async-start(bf16[8,56,640]{2,1,0:T(8,128)(2,1)} %get-tuple-element.309), calls=%async_computation.14 | async-start | bytes 1146880 | tf_op jit(solution)/shard_map/all_to_all | solution.py:107
  469.2 22.8 %collective-permute-start.39 = (bf16[112,1024]{1,0:T(8,128)(2,1)S(1)}, bf16[112,1024]{1,0:T(8,128)(2,1)S(1)}, u32[]{:S(2)}, u32[]{:S(2)}) collective-permute-start(bf16[112,1024]{1,0:T(8,128)(2,1)S(1)} %pad_maximum_fusion.14), channel_id=1, source_target_pairs={{0,8},{8,0},{16,24},{24,16},{1,9},{9,1},{17,25},{25,17},{2,10},{10... | collective-permute-start | bytes 688136 | tf_op jit(solution)/shard_map/ppermute | solution.py:40
  469.9 22.5 %collective-permute-start.37 = (bf16[56,4864]{1,0:T(8,128)(2,1)S(1)}, bf16[56,4864]{1,0:T(8,128)(2,1)S(1)}, u32[]{:S(2)}, u32[]{:S(2)}) collective-permute-start(bf16[56,4864]{1,0:T(8,128)(2,1)S(1)} %reshape.297), channel_id=1, source_target_pairs={{0,16},{8,24},{16,0},{24,8},{1,17},{9,25},{17,1},{25,9},{2,18},{10... | collective-permute-start | bytes 1634312 | tf_op jit(solution)/shard_map/ppermute | solution.py:40
  470.5 21.6 %collective-permute-start.38 = (bf16[2,152,896]{2,1,0:T(8,128)(2,1)S(1)}, bf16[2,152,896]{2,1,0:T(8,128)(2,1)S(1)}, u32[]{:S(2)}, u32[]{:S(2)}) collective-permute-start(bf16[2,152,896]{2,1,0:T(8,128)(2,1)S(1)} %pad_maximum_fusion.9), channel_id=1, source_target_pairs={{0,8},{8,0},{16,24},{24,16},{1,9},{9,1},{17,25},{25,17},{2,10},{10... | collective-permute-start | bytes 1634312 | tf_op jit(solution)/shard_map/ppermute | solution.py:40
  492.7 11.7 %collective-permute-start.40 = (bf16[112,4864]{1,0:T(8,128)(2,1)S(1)}, bf16[112,4864]{1,0:T(8,128)(2,1)S(1)}, u32[]{:S(2)}, u32[]{:S(2)}) collective-permute-start(bf16[112,4864]{1,0:T(8,128)(2,1)S(1)} %pad_maximum_fusion.5), channel_id=1, source_target_pairs={{0,8},{8,0},{16,24},{24,16},{1,9},{9,1},{17,25},{25,17},{2,10},{10... | collective-permute-start | bytes 3268616 | tf_op jit(solution)/shard_map/ppermute | solution.py:40
  (74 other events, 634.3 us)
